TPU v7x, 32 devices: a whole 2x2x4 slice. The times are simulated.
32 devices in a mesh: dp: 8 (over z, x), mp: 4 (over y, core).
Axes of the slice: x: 2, y: 2, z: 4, core: 2. Of those that a mesh axis runs over, the one named last changes fastest.
Arguments:
- frames: bfloat16 [2048, 2, 16, 256], P('dp', None, None, 'mp')
- cache: bfloat16 [2048, 2, 16, 256], P('dp', None, None, 'mp'), may hold values from -6 to 6
- group_offset: int32 [128], replicated, may hold values from 0 to 7, as said below
- cache_offset: int32 [128], replicated, may hold values from 0 to 7, as said below
- cache_group: int32 [128], replicated, may hold values from 0 to 127, each once
- group_rows: int32 [8, 128], P('dp'), may hold values from 1 to 2, 192 in all within a row
- cache_live: int32 [1024], P('dp'), may hold values 0 or 1
- temporal_weight: bfloat16 [3, 256, 512], P(None, None, 'mp')
- spatial_weight: bfloat16 [3, 512, 512], P(None, None, 'mp'), may hold values from -0.15625 to 0.15625
- norm_gain: bfloat16 [512], P('mp'), may hold values from 0.25 to 1.75
Outputs:
- latents: bfloat16 [2048, 2, 16, 512], P('dp', None, None, 'mp')
Inputs may be any that keep to these rules, and one draw needn't show every extreme that they name: group_offset[g] equals group_offset[g2] exactly when g - g2 is a multiple of 8. cache_offset[h] equals cache_offset[h2] exactly when h - h2 is a multiple of 8.
All inputs are finite; a program needn't handle non-finite values. No bound on the sum of `cache_live` on one device may be relied on, other than what follows from the above.
Results may differ from a plain program's by a relative error of at most 0.0026.
Values may be sent and summed in bfloat16 or wider, within the bound.
No kernel may reach another device: no remote copies, remote signals or barrier semaphores. Data moves between devices by JAX's collectives and lax.ppermute only.
A program may use at most 128 MiB of HBM per device.

v0:
```python
import jax
import jax.numpy as jnp
from jax import lax
from jax.sharding import PartitionSpec as P


def temporal_conv(sequence, weight_part, span_steps):
    taps = weight_part.shape[0]
    windows = [
        sequence[:, taps - 1 - tap_index : taps - 1 - tap_index + span_steps]
        for tap_index in range(taps)
    ]
    joined = jnp.concatenate(windows, axis=3)
    flat_weight = weight_part.reshape((taps * weight_part.shape[1], weight_part.shape[2]))
    return jnp.einsum("rtwc,cd->rtwd", joined, flat_weight, preferred_element_type=jnp.float32)


def spatial_conv(activated, weight_part):
    width = activated.shape[2]
    padded = jnp.pad(activated, ((0, 0), (0, 0), (1, 1), (0, 0)))
    joined = jnp.concatenate(
        [padded[:, :, tap_index : tap_index + width] for tap_index in range(3)], axis=3
    )
    flat_weight = weight_part.reshape((3 * weight_part.shape[1], weight_part.shape[2]))
    return jnp.einsum("rtwc,cd->rtwd", joined, flat_weight, preferred_element_type=jnp.float32)


def to_slots(values, slot_index, owner_count, per_pair):
    buffer = (
        jnp.zeros((owner_count * per_pair,) + values.shape[1:], values.dtype)
        .at[slot_index]
        .set(values)
    )
    return buffer.reshape((owner_count, per_pair) + values.shape[1:])


def local(
    frames,
    cache,
    group_offset,
    cache_offset,
    cache_group,
    group_rows,
    cache_live,
    temporal_weight,
    spatial_weight,
    norm_gain,
):
    owner_count = lax.axis_size("dp")
    my_rank = lax.axis_index("dp")
    groups = group_offset.shape[0]
    pair_rows = frames.shape[0] // groups
    span_steps = frames.shape[1]
    per_pair = (groups + owner_count - 1) // owner_count
    group_index = jnp.arange(groups, dtype=jnp.int32)
    slot_level = group_index // owner_count
    grouped = frames.reshape((groups, pair_rows) + frames.shape[1:])
    counts = group_rows.reshape(groups)
    send_slot = (my_rank + group_offset) % owner_count * per_pair + slot_level
    got_rows, got_counts = (
        lax.all_to_all(
            to_slots(grouped, send_slot, owner_count, per_pair),
            "dp",
            split_axis=0,
            concat_axis=0,
            tiled=True,
        ),
        lax.all_to_all(
            to_slots(counts, send_slot, owner_count, per_pair),
            "dp",
            split_axis=0,
            concat_axis=0,
            tiled=True,
        ),
    )
    take_slot = (my_rank - group_offset) % owner_count * per_pair + slot_level
    own_rows = got_rows.reshape((owner_count * per_pair,) + grouped.shape[1:])[take_slot]
    own_counts = got_counts.reshape(owner_count * per_pair)[take_slot]
    cache_grouped = cache.reshape((groups, pair_rows) + cache.shape[1:])
    cache_send = (my_rank + cache_offset) % owner_count * per_pair + slot_level
    got_cache, got_flags = (
        lax.all_to_all(
            to_slots(cache_grouped, cache_send, owner_count, per_pair),
            "dp",
            split_axis=0,
            concat_axis=0,
            tiled=True,
        ),
        lax.all_to_all(
            to_slots(cache_live, cache_send, owner_count, per_pair),
            "dp",
            split_axis=0,
            concat_axis=0,
            tiled=True,
        ),
    )
    inverse = jnp.sum(
        group_index[:, None] * (cache_group[:, None] == group_index[None, :]).astype(jnp.int32),
        axis=0,
    )
    cache_slot = (my_rank - cache_offset[inverse]) % owner_count * per_pair + inverse // owner_count
    own_cache = got_cache.reshape((owner_count * per_pair,) + cache_grouped.shape[1:])[cache_slot]
    own_flags = got_flags.reshape(owner_count * per_pair)[cache_slot]
    own_cache = jnp.where(
        own_flags[:, None, None, None, None] > 0, own_cache, jnp.zeros_like(own_cache)
    )
    sequence = jnp.concatenate([own_cache, own_rows], axis=2)
    sequence = sequence.reshape((groups * pair_rows,) + sequence.shape[2:])
    live_rows = (jnp.arange(pair_rows, dtype=jnp.int32)[None, :] < own_counts[:, None]).reshape(
        groups * pair_rows
    )
    channels = spatial_weight.shape[1]
    weight_cut = temporal_weight
    conv_time = temporal_conv(
        lax.all_gather(sequence, "mp", axis=3, tiled=True), weight_cut, span_steps
    )
    square_sum = lax.psum(jnp.sum(conv_time * conv_time, axis=3), "mp")
    scaled = (
        conv_time
        * lax.rsqrt(square_sum / channels + 1e-06)[..., None]
        * norm_gain.astype(jnp.float32)
    )
    activated = jax.nn.silu(scaled).astype(jnp.bfloat16)
    weight_cut = spatial_weight
    conv_space = spatial_conv(lax.all_gather(activated, "mp", axis=3, tiled=True), weight_cut)
    latents = jnp.where(live_rows[:, None, None, None], conv_time + conv_space, 0.0).astype(
        jnp.bfloat16
    )
    return latents


def solution(mesh):
    in_specs = (
        P("dp", None, None, "mp"),
        P("dp", None, None, "mp"),
        P(),
        P(),
        P(),
        P("dp", None),
        P("dp"),
        P(None, None, "mp"),
        P(None, None, "mp"),
        P("mp"),
    )
    out_specs = P("dp", None, None, "mp")
    return jax.shard_map(local, mesh=mesh, in_specs=in_specs, out_specs=out_specs, check_vma=False)
```

profile of v0, /device:TPU:11, one launch (start us, length us, event | category | flops | bytes accessed | tf_op | source)
XLA Modules:
  0.0 307.6 jit_solution(13049172443261831299)
XLA Ops:
  9.1 5.7 %all-to-all-start.1 = ((s32[8,1,16]{2,1,0:T(1,128)}), s32[8,1,16]{2,1,0:T(1,128)S(1)}, u32[]{:S(2)}, u32[]{:S(2)}) async-start(s32[8,1,16]{2,1,0:T(1,128)} %bitcast.2), calls=%async_computation.1 | async-start | bytes 8192 | tf_op jit(solution)/shard_map/all_to_all | solution.py:89
  14.7 4.6 %copy.40 = bf16[256,2,16,64]{3,2,1,0:T(8,128)(2,1)} copy(bf16[256,2,16,64]{0,3,2,1:T(8,128)(2,1)} %param.10) | data formatting | bytes 2097152 | tf_op args[0]
  19.9 11.9 %scatter_fusion.1 = bf16[128,2,2,16,64]{4,3,2,1,0:T(8,128)(2,1)S(1)} fusion(bf16[128,2,2,16,64]{4,3,2,1,0:T(8,128)(2,1)S(1)} %broadcast.194.clone, s32[128]{0:T(128)S(1)} %get-tuple-element.11, bf16[128,2,2,16,64]{4,3,2,1,0:T(8,128)(2,1)} %bitcast.50), kind=kCustom, calls=%fused_computation.8 | custom fusion | bytes 3146240 | tf_op jit(solution)/shard_map/scatter | solution.py:32
  34.5 5.4 %all-to-all-start.3 = ((bf16[8,2,32768]{2,1,0:T(2,128)(2,1)}), bf16[8,2,32768]{2,1,0:T(2,128)(2,1)S(1)}, u32[]{:S(2)}, u32[]{:S(2)}) async-start(bf16[8,2,32768]{2,1,0:T(2,128)(2,1)} %reshape.297), calls=%async_computation.3 | async-start | bytes 2097152 | tf_op jit(solution)/shard_map/all_to_all | solution.py:61
  39.9 4.6 %copy.38 = bf16[256,2,16,64]{3,2,1,0:T(8,128)(2,1)} copy(bf16[256,2,16,64]{0,3,2,1:T(8,128)(2,1)} %param.11) | data formatting | bytes 2097152 | tf_op args[1]
  45.1 11.9 %scatter_fusion = bf16[128,2,2,16,64]{4,3,2,1,0:T(8,128)(2,1)S(1)} fusion(bf16[128,2,2,16,64]{4,3,2,1,0:T(8,128)(2,1)S(1)} %broadcast.194.clone.1, s32[128]{0:T(128)S(1)} %get-tuple-element.14, bf16[128,2,2,16,64]{4,3,2,1,0:T(8,128)(2,1)} %bitcast.49), kind=kCustom, calls=%fused_computation.7 | custom fusion | bytes 3146240 | tf_op jit(solution)/shard_map/scatter | solution.py:32
  59.7 3.4 %all-to-all-done.3 = bf16[8,2,32768]{2,1,0:T(2,128)(2,1)S(1)} async-done(((bf16[8,2,32768]{2,1,0:T(2,128)(2,1)}), bf16[8,2,32768]{2,1,0:T(2,128)(2,1)S(1)}, u32[]{:S(2)}, u32[]{:S(2)}) %all-to-all-start.3) | async-done | bytes 1048608 | tf_op jit(solution)/shard_map/all_to_all | solution.py:61
  63.1 6.3 %all-to-all-start.2 = ((bf16[8,2,32768]{2,1,0:T(2,128)(2,1)}), bf16[8,2,32768]{2,1,0:T(2,128)(2,1)}, u32[]{:S(2)}, u32[]{:S(2)}) async-start(bf16[8,2,32768]{2,1,0:T(2,128)(2,1)} %reshape.299), calls=%async_computation.2 | async-start | bytes 2097152 | tf_op jit(solution)/shard_map/all_to_all | solution.py:82
  77.2 4.1 %copy.41 = bf16[256,2,16,64]{0,2,1,3:T(8,128)(2,1)S(1)} copy(bf16[256,2,16,64]{3,2,1,0:T(8,128)(2,1)} %bitcast.54) | data formatting | bytes 2097152 | tf_op jit(solution)/shard_map/concatenate | solution.py:107
  81.3 11.3 %all-to-all-done.2 = bf16[8,2,32768]{2,1,0:T(2,128)(2,1)} async-done(((bf16[8,2,32768]{2,1,0:T(2,128)(2,1)}), bf16[8,2,32768]{2,1,0:T(2,128)(2,1)}, u32[]{:S(2)}, u32[]{:S(2)}) %all-to-all-start.2) | async-done | bytes 1048608 | tf_op jit(solution)/shard_map/all_to_all | solution.py:82
  92.7 3.1 %reshape.300 = bf16[8,16,2,2,16,64]{5,4,3,2,1,0:T(8,128)(2,1)S(1)} reshape(bf16[8,2,32768]{2,1,0:T(2,128)(2,1)} %all-to-all-done.2) | data formatting | bytes 2097152
  97.9 4.1 %copy.39 = bf16[256,2,16,64]{0,2,1,3:T(8,128)(2,1)S(1)} copy(bf16[256,2,16,64]{3,2,1,0:T(8,128)(2,1)} %bitcast.52) | data formatting | bytes 2097152 | tf_op jit(solution)/shard_map/gather | solution.py:102
  103.9 60.4 %all-gather.3.cloned.1.call-done = bf16[256,4,16,256]{0,2,1,3:T(8,128)(2,1)} async-done(((bf16[256,4,16,64]{0,2,1,3:T(8,128)(2,1)}), bf16[256,4,16,256]{0,2,1,3:T(8,128)(2,1)}) %all-gather.3.cloned.1.call-update) | async-done | bytes 8388624 | tf_op jit(solution)/shard_map/all_gather | solution.py:115
  164.2 9.1 %fusion.34 = (bf16[256,2,16,256]{0,2,1,3:T(8,128)(2,1)}, bf16[256,2,16,256]{0,2,1,3:T(8,128)(2,1)}, bf16[256,2,16,256]{0,2,1,3:T(8,128)(2,1)}) fusion(bf16[256,4,16,256]{0,2,1,3:T(8,128)(2,1)} %all-gather.3.cloned.1.call-done), kind=kLoop, calls=%fused_computation.82 | loop fusion | bytes 25165824 | tf_op jit(solution)/shard_map/slice | solution.py:10
  173.3 7.5 %copy.54 = bf16[256,2,16,256]{3,0,2,1:T(8,128)(2,1)} copy(bf16[256,2,16,256]{0,2,1,3:T(8,128)(2,1)} %get-tuple-element.7) | data formatting | bytes 8388608
  180.9 7.5 %copy.55 = bf16[256,2,16,256]{3,0,2,1:T(8,128)(2,1)} copy(bf16[256,2,16,256]{0,2,1,3:T(8,128)(2,1)} %get-tuple-element.8) | data formatting | bytes 8388608
  188.4 7.6 %copy.56 = bf16[256,2,16,256]{3,0,2,1:T(8,128)(2,1)} copy(bf16[256,2,16,256]{0,2,1,3:T(8,128)(2,1)} %get-tuple-element.9) | data formatting | bytes 8388608
  196.0 8.5 %multiply_reduce_fusion = (f32[256,2,16]{0,2,1:T(8,128)S(1)}, f32[256,2,16,128]{0,3,2,1:T(8,128)}) fusion(bf16[768,128,1,1]{1,0,3,2:T(8,128)(2,1)S(1)} %bitcast.56, bf16[256,2,16,256]{3,0,2,1:T(8,128)(2,1)} %copy.56, bf16[256,2,16,256]{3,0,2,1:T(8,128)(2,1)} %copy.55, bf16[256,2,16,256]{3,0,2,1:T(8,128)(2,1)} %copy.54), kind=kOutput, calls=%fused_computation.25 | convolution fusion | flops 1650450432 | bytes 17006592 | tf_op jit(solution)/shard_map/rtwc,cd->rtwd/dot_general | solution.py:15
  204.6 10.4 %psum.7 = f32[256,2,16]{0,2,1:T(8,128)S(1)} all-reduce(f32[256,2,16]{0,2,1:T(8,128)S(1)} %get-tuple-element.12), channel_id=1, replica_groups=mesh['dp'=8,'mp'=4] {'mp'}, use_global_device_ids=true, to_apply=%region_6.7 | all-reduce | flops 8192 | bytes 65536 | tf_op jit(solution)/shard_map/psum | solution.py:117
  215.0 5.0 %multiply_convert_fusion = bf16[256,2,16,128]{0,3,2,1:T(8,128)(2,1)} fusion(f32[256,2,16,128]{0,3,2,1:T(8,128)} %get-tuple-element.13, f32[128]{0:T(128)S(1)} %convert_element_type.12, f32[256,2,16]{0,2,1:T(8,128)S(1)} %add_rsqrt_fusion), kind=kLoop, calls=%fused_computation.24 | loop fusion | flops 7340032 | bytes 6324736 | tf_op jit(solution)/shard_map/convert_element_type | solution.py:123
  221.2 8.5 %all_to_all.28 = s32[8,1,16]{2,1,0:T(1,128)S(1)} all-to-all(s32[8,1,16]{2,1,0:T(1,128)S(1)} %bitcast.55), channel_id=1, replica_groups=mesh['dp'=8,'mp'=4] {'dp'}, dimensions={0} | all-to-all | bytes 1024 | tf_op jit(solution)/shard_map/all_to_all | solution.py:68
  232.0 47.6 %all-gather.5.cloned.1.call-done = bf16[256,2,16,512]{0,3,2,1:T(8,128)(2,1)} async-done(((bf16[256,2,16,128]{0,3,2,1:T(8,128)(2,1)}), bf16[256,2,16,512]{0,3,2,1:T(8,128)(2,1)}) %all-gather.5.cloned.1.call-update) | async-done | bytes 8388624 | tf_op jit(solution)/shard_map/all_gather | solution.py:125
  279.6 9.2 %pad_slice_fusion.1 = (bf16[256,2,16,512]{0,3,2,1:T(8,128)(2,1)S(1)}, bf16[256,2,16,512]{0,3,2,1:T(8,128)(2,1)}) fusion(bf16[256,2,16,512]{0,3,2,1:T(8,128)(2,1)} %all-gather.5.cloned.1.call-done), kind=kLoop, calls=%fused_computation.22 | loop fusion | bytes 25165824 | tf_op jit(solution)/shard_map/slice | solution.py:22
  290.6 7.1 %select_convert_fusion = bf16[256,2,16,128]{0,3,2,1:T(8,128)(2,1)S(1)} fusion(f32[256,2,16,128]{0,3,2,1:T(8,128)} %get-tuple-element.13, bf16[1536,128,1,1]{1,0,3,2:T(8,128)(2,1)S(1)} %bitcast.46, bf16[256,2,16,512]{0,3,2,1:T(8,128)(2,1)} %get-tuple-element.6, bf16[256,2,16,512]{0,3,2,1:T(8,128)(2,1)S(1)} %copy-done.2, ...), kind=kOutput, calls=%fused_computation.23 | convolution fusion | flops 3299868672 | bytes 31850752 | tf_op jit(solution)/shard_map/rtwc,cd->rtwd/dot_general | solution.py:25
  (55 shorter events, 28.8 us)
Async XLA Ops:
  6.5 282.2 %copy-start = (bf16[3,512,128]{2,1,0:T(8,128)(2,1)S(1)}, bf16[3,512,128]{2,1,0:T(8,128)(2,1)}, u32[]{:S(2)}) copy-start(bf16[3,512,128]{2,1,0:T(8,128)(2,1)} %param.18) | copy-start | bytes 1179652
  7.3 24.5 %copy-start.3 = (s32[128]{0:T(128)}, s32[128]{0:T(128)S(1)}, u32[]{:S(2)}) copy-start(s32[128]{0:T(128)S(1)} %get-tuple-element.11) | copy-start | bytes 1540
  9.1 25.4 %all-to-all-start.1 = ((s32[8,1,16]{2,1,0:T(1,128)}), s32[8,1,16]{2,1,0:T(1,128)S(1)}, u32[]{:S(2)}, u32[]{:S(2)}) async-start(s32[8,1,16]{2,1,0:T(1,128)} %bitcast.2), calls=%async_computation.1 | async-start | bytes 8192 | tf_op jit(solution)/shard_map/all_to_all | solution.py:89
  34.5 28.6 %all-to-all-start.3 = ((bf16[8,2,32768]{2,1,0:T(2,128)(2,1)}), bf16[8,2,32768]{2,1,0:T(2,128)(2,1)S(1)}, u32[]{:S(2)}, u32[]{:S(2)}) async-start(bf16[8,2,32768]{2,1,0:T(2,128)(2,1)} %reshape.297), calls=%async_computation.3 | async-start | bytes 2097152 | tf_op jit(solution)/shard_map/all_to_all | solution.py:61
  57.0 12.5 %copy-start.5 = (s32[128]{0:T(128)S(1)}, s32[128]{0:T(128)}, u32[]{:S(2)}) copy-start(s32[128]{0:T(128)} %param.14) | copy-start | bytes 1540
  57.0 12.6 %copy-start.1 = (s32[128]{0:T(128)S(1)}, s32[128]{0:T(128)}, u32[]{:S(2)}) copy-start(s32[128]{0:T(128)} %param.13) | copy-start | bytes 1540
  63.1 29.5 %all-to-all-start.2 = ((bf16[8,2,32768]{2,1,0:T(2,128)(2,1)}), bf16[8,2,32768]{2,1,0:T(2,128)(2,1)}, u32[]{:S(2)}, u32[]{:S(2)}) async-start(bf16[8,2,32768]{2,1,0:T(2,128)(2,1)} %reshape.299), calls=%async_computation.2 | async-start | bytes 2097152 | tf_op jit(solution)/shard_map/all_to_all | solution.py:82
  69.5 94.8 %all-gather.3.cloned.1.call-start = ((), (), s32[]{:S(2)}) async-start(), calls=%async_computation.4 | async-start | bytes 10485760 | tf_op jit(solution)/shard_map/all_gather | solution.py:115
  102.0 1.9 copy-start.6
  103.6 175.9 %all-gather.5.cloned.1.call-start = ((), (), s32[]{:S(2)}) async-start(), calls=%async_computation.5 | async-start | bytes 10485760 | tf_op jit(solution)/shard_map/all_gather | solution.py:125
  188.4 7.6 %copy-start.4 = (bf16[3,256,128]{2,1,0:T(8,128)(2,1)S(1)}, bf16[3,256,128]{2,1,0:T(8,128)(2,1)}, u32[]{:S(2)}) copy-start(bf16[3,256,128]{2,1,0:T(8,128)(2,1)} %param.17) | copy-start | bytes 589828
  279.6 11.0 %copy-start.2 = (bf16[256,2,16,512]{0,3,2,1:T(8,128)(2,1)S(1)}, bf16[256,2,16,512]{0,3,2,1:T(8,128)(2,1)}, u32[]{:S(2)}) copy-start(bf16[256,2,16,512]{0,3,2,1:T(8,128)(2,1)} %all-gather.5.cloned.1.call-done) | copy-start | bytes 25165828
Sparse Core Ops, SparseCore 0:
  103.7 60.4 all-gather.2
  220.2 59.3 all-gather.4
where the time goes:
time: 310 us; the launch traced here: 308 us
  waiting for transfers between devices  123 us (40%)
  local copies, waits for them, and re-layouts  110 us (35%)
  blocking collectives  18.9 us (6%)
  starting transfers between devices  17.7 us (6%)
  matrix products  15.7 us (5%)
  between operations  13.7 us (4%)
  other arithmetic  8.86 us (3%)
    all_gather x1, waiting for transfers between devices, local(): lax.all_gather(sequence, 'mp', axis=3, tiled=True)  60.4 us
    all_gather x1, waiting for transfers between devices, local(): lax.all_gather(activated, 'mp', axis=3, tiled=True)  47.6 us
    unnamed x23, local copies, waits for them, and re-layouts  43.7 us
    scatter x4, local copies, waits for them, and re-layouts, to_slots(): buffer = jnp.zeros((owner_count * per_pair,) + values.shape[1:], values.d...  26 us
    all_to_all x1, waiting for transfers between devices, local(): lax.all_to_all(to_slots(cache_grouped, cache_send, owner_count, per_pair)...  11.3 us
    psum x1, blocking collectives, local(): square_sum = lax.psum(jnp.sum(conv_time * conv_time, axis=3), 'mp')  10.4 us
    slice x1, local copies, waits for them, and re-layouts, spatial_conv(): padded[:, :, tap_index:tap_index + width]  9.19 us
    slice x1, local copies, waits for them, and re-layouts, temporal_conv(): sequence[:, taps - 1 - tap_index:taps - 1 - tap_index + span_steps]  9.11 us
  transfers between devices with their start and end apart: 5, of which 4 were waited for; matrix products, arithmetic and copies ran while one was open for 18% of the time, Pallas kernels for 0%

commit v1 on v0

--- a/solution.py
+++ b/solution.py
@@ -1,6 +1,10 @@
+import functools
+
 import jax
 import jax.numpy as jnp
 from jax import lax
+from jax.experimental import pallas as pl
+from jax.experimental.pallas import tpu as pltpu
 from jax.sharding import PartitionSpec as P
 
 
@@ -34,7 +38,7 @@
     return buffer.reshape((owner_count, per_pair) + values.shape[1:])
 
 
-def local(
+def plain_local(
     frames,
     cache,
     group_offset,
@@ -129,6 +133,434 @@
     return latents
 
 
+CORES = 2
+VMEM_LIMIT = 56 * 1024 * 1024
+
+
+def shift_order(size):
+    far = sorted(range(1, size), key=lambda k: (abs(k - size // 2), k))
+    return [0] + far
+
+
+def lane_iota(shape):
+    return lax.broadcasted_iota(jnp.int32, shape, len(shape) - 1)
+
+
+def pick(index, table):
+    out = jnp.zeros_like(index)
+    for at, value in enumerate(table):
+        out = jnp.where(index == at, value, out)
+    return out
+
+
+def position_of(shift, order):
+    out = jnp.int32(0)
+    for at, k in enumerate(order):
+        out = jnp.where(shift == k, jnp.int32(at), out)
+    return out
+
+
+def pack_kernel(order, pair_rows, mark_dead, offset_ref, flag_ref, own_ref, other_ref, *rest):
+    outs, joined = rest[:-1], rest[-1]
+    core = lax.axis_index("mp") % CORES
+    tokens, _, part, rows = joined.shape
+    joined[:, core] = own_ref[...].reshape(tokens, part, rows)
+    joined[:, 1 - core] = other_ref[...].reshape(tokens, part, rows)
+    shifts = len(order)
+    groups = rows // pair_rows
+    half_levels = groups // shifts // CORES
+    slots = half_levels * pair_rows
+    total = shifts * slots
+    row = lane_iota((1, rows))
+    place = pick(row // pair_rows % shifts, [position_of(offset_ref[j], order) for j in range(shifts)])
+    level = row // (pair_rows * shifts) - core * half_levels
+    target = place * slots + level * pair_rows + row % pair_rows
+    target = jnp.where((level >= 0) & (level < half_levels), target, -1)
+    hit = lax.broadcasted_iota(jnp.int32, (total, rows), 0) == target
+    spread = (
+        lax.broadcasted_iota(jnp.int32, (groups, rows), 0) == lane_iota((groups, rows)) // pair_rows
+    ).astype(jnp.float32)
+    flag = jnp.dot(flag_ref[...].astype(jnp.float32), spread, preferred_element_type=jnp.float32)
+    if mark_dead:
+        live = (row % pair_rows).astype(jnp.float32) < flag
+        dead = jnp.sum(jnp.where(hit & jnp.logical_not(live), 1.0, 0.0), axis=1, keepdims=True) > 0.5
+    else:
+        hit = hit & (flag > 0.5)
+    onehot = jnp.where(hit, 1.0, 0.0).astype(jnp.bfloat16)
+    flat = joined.reshape(tokens * CORES * part, rows)
+    step = 512
+    for start in range(0, tokens * CORES * part, step):
+        tile = lax.dot_general(
+            onehot,
+            flat[start : start + step],
+            (((1,), (1,)), ((), ())),
+            preferred_element_type=jnp.float32,
+        )
+        if mark_dead:
+            tile = jnp.where(dead, jnp.inf, tile)
+        tile = tile.astype(jnp.bfloat16)
+        for at, out in enumerate(outs):
+            out[:, start : start + step] = tile[at * slots : (at + 1) * slots]
+
+
+def pack(order, pair_rows, mark_dead, offset, flag, own, other):
+    rows = own.shape[1]
+    shifts = len(order)
+    slots = rows // shifts // CORES
+    part = 64
+    tokens = own.shape[0] // part
+    width = own.shape[0] * CORES
+    vmem = pl.BlockSpec(memory_space=pltpu.VMEM)
+    return pl.pallas_call(
+        functools.partial(pack_kernel, order, pair_rows, mark_dead),
+        out_shape=[jax.ShapeDtypeStruct((slots, width), jnp.bfloat16)] * shifts,
+        in_specs=[pl.BlockSpec(memory_space=pltpu.SMEM), vmem, vmem, vmem],
+        out_specs=[vmem] * shifts,
+        scratch_shapes=[pltpu.VMEM((tokens, CORES, part, rows), jnp.bfloat16)],
+        compiler_params=pltpu.CompilerParams(vmem_limit_bytes=VMEM_LIMIT),
+        cost_estimate=pl.CostEstimate(
+            flops=2 * shifts * slots * width * rows, bytes_accessed=3 * width * rows, transcendentals=0
+        ),
+        name="pack_dead" if mark_dead else "pack_carried",
+    )(offset, flag, own, other)
+
+
+def choose_kernel(
+    order, pair_rows, group_offset_ref, cache_offset_ref, group_ref, own0, own1, other0, other1, out
+):
+    core = lax.axis_index("mp") % CORES
+    shifts = len(order)
+    half, width = own0.shape
+    groups = group_ref.shape[1]
+    rows = groups * pair_rows
+    half_levels = groups // shifts // CORES
+    slots = half_levels * pair_rows
+    column = lane_iota((1, rows))
+    home = jnp.where(column < half, core, 1 - core)
+    within = column % half
+    shift_at = within // slots
+    residue = jnp.zeros_like(column)
+    for j in range(shifts):
+        residue = jnp.where(shift_at == position_of(cache_offset_ref[j], order), j, residue)
+    level = within % slots // pair_rows + home * half_levels
+    cached = level * shifts + residue
+    pickers = (lax.broadcasted_iota(jnp.int32, (groups, rows), 0) == cached).astype(jnp.float32)
+    group = jnp.dot(
+        group_ref[...].astype(jnp.float32), pickers, preferred_element_type=jnp.float32
+    )
+    group = (group + 0.5).astype(jnp.int32)
+    place = pick(group % shifts, [position_of(group_offset_ref[j], order) for j in range(shifts)])
+    goal = group // shifts - core * half_levels
+    target = place * slots + goal * pair_rows + column % pair_rows
+    target = jnp.where((goal >= 0) & (goal < half_levels), target, -1)
+    onehot = jnp.where(
+        lax.broadcasted_iota(jnp.int32, (half, rows), 0) == target, 1.0, 0.0
+    ).astype(jnp.bfloat16)
+    step = 512
+    for side, (own, other) in enumerate(((own0, other0), (own1, other1))):
+        for start in range(0, width, step):
+            both = jnp.concatenate(
+                [own[:, start : start + step], other[:, start : start + step]], axis=0
+            )
+            out[:, side * width + start : side * width + start + step] = jnp.dot(
+                onehot, both, preferred_element_type=jnp.float32
+            ).astype(jnp.bfloat16)
+
+
+def choose(order, pair_rows, group_offset, cache_offset, group, own, other):
+    half, width = own[0].shape
+    vmem = pl.BlockSpec(memory_space=pltpu.VMEM)
+    smem = pl.BlockSpec(memory_space=pltpu.SMEM)
+    return pl.pallas_call(
+        functools.partial(choose_kernel, order, pair_rows),
+        out_shape=jax.ShapeDtypeStruct((half, 2 * width), jnp.bfloat16),
+        in_specs=[smem, smem] + [vmem] * 5,
+        out_specs=vmem,
+        compiler_params=pltpu.CompilerParams(vmem_limit_bytes=VMEM_LIMIT),
+        cost_estimate=pl.CostEstimate(
+            flops=8 * half * half * width, bytes_accessed=12 * half * width, transcendentals=0
+        ),
+        name="choose_carried",
+    )(group_offset, cache_offset, group, *own, *other)
+
+
+def weights_kernel(taps, near, near_core, far_core, space, space_core, time_out, space_out, gain_out):
+    index = lax.axis_index("mp")
+    part = near.shape[1]
+    inner = (near.shape[0] - 16) // taps
+    side = inner // 2
+    chip = index // CORES
+    for tap in range(taps):
+        for at in range(2):
+            source = pl.ds(pl.multiple_of(tap * inner + (chip ^ at) * side, side), side)
+            rows = slice(tap * inner + at * side, tap * inner + (at + 1) * side)
+            for block, ref in enumerate((near, near_core)):
+                time_out[rows, block * part : (block + 1) * part] = ref[source, :]
+            for block in range(2):
+                base = block * near.shape[0]
+                source = pl.ds(
+                    pl.multiple_of(base + tap * inner + (chip ^ at) * side, 16), side
+                )
+                time_out[rows, (2 + block) * part : (3 + block) * part] = far_core[source, :]
+    gain_row = taps * inner
+    gains = [near, near_core]
+    for block, ref in enumerate(gains):
+        gain_out[:, block * part : (block + 1) * part] = ref[gain_row : gain_row + 16, :]
+    for block in range(2):
+        base = block * near.shape[0] + gain_row
+        gain_out[:, (2 + block) * part : (3 + block) * part] = far_core[base : base + 16, :]
+    channels = 4 * part
+    for tap in range(space.shape[0] // channels):
+        for block in range(4):
+            source = pl.ds(
+                pl.multiple_of(tap * channels + (index ^ block) * part, part), part
+            )
+            rows = slice(tap * channels + block * part, tap * channels + (block + 1) * part)
+            space_out[rows, :part] = space[source, :]
+            space_out[rows, part:] = space_core[source, :]
+
+
+def arrange_weights(taps, near, near_core, far_core, space, space_core):
+    part = near.shape[1]
+    vmem = pl.BlockSpec(memory_space=pltpu.VMEM)
+    return pl.pallas_call(
+        functools.partial(weights_kernel, taps),
+        out_shape=[
+            jax.ShapeDtypeStruct((near.shape[0] - 16, 4 * part), jnp.bfloat16),
+            jax.ShapeDtypeStruct((space.shape[0], 2 * part), jnp.bfloat16),
+            jax.ShapeDtypeStruct((16, 4 * part), jnp.bfloat16),
+        ],
+        in_specs=[vmem] * 5,
+        out_specs=[vmem] * 3,
+        compiler_params=pltpu.CompilerParams(vmem_limit_bytes=VMEM_LIMIT),
+        cost_estimate=pl.CostEstimate(
+            flops=0, bytes_accessed=4 * (near.size * 4 + space.size * 2), transcendentals=0
+        ),
+        name="arrange_weights",
+    )(near, near_core, far_core, space, space_core)
+
+
+def encode_kernel(count, width, *refs):
+    near, far = refs[:count], refs[count : 2 * count]
+    carried, time_w, space_w, gain_ref, kept, sent, seq, act = refs[2 * count :]
+    slots = near[0].shape[0]
+    rows = count * slots
+    side = seq.shape[2] // 2
+    channels = time_w.shape[1]
+    half_width = carried.shape[1] // 2
+    past = half_width // (side * width)
+    span = near[0].shape[1] // (side * width)
+    taps = time_w.shape[0] // (2 * side)
+    tokens = width * rows
+    for step in range(past):
+        for w in range(width):
+            lane = (step * width + w) * side
+            at = slice(w * rows, (w + 1) * rows)
+            seq[step, at, :side] = carried[:, lane : lane + side]
+            seq[step, at, side:] = carried[:, half_width + lane : half_width + lane + side]
+    for step in range(span):
+        for w in range(width):
+            lane = (step * width + w) * side
+            for u in range(count):
+                at = slice(w * rows + u * slots, w * rows + (u + 1) * slots)
+                seq[past + step, at, :side] = near[u][:, lane : lane + side]
+                seq[past + step, at, side:] = far[u][:, lane : lane + side]
+    first = jnp.concatenate([ref[:, :side].astype(jnp.float32)[:, :1] for ref in near], axis=0)
+    live = (first < jnp.inf)[None]
+    gain = gain_ref[0:1, :].astype(jnp.float32)
+    act[0:rows] = jnp.zeros((rows, channels), jnp.bfloat16)
+    act[(width + 1) * rows :] = jnp.zeros((rows, channels), jnp.bfloat16)
+    block = slots * width
+    row_index = lax.broadcasted_iota(jnp.int32, (block, block), 0)
+    column_index = lax.broadcasted_iota(jnp.int32, (block, block), 1)
+    turn = jnp.where(
+        (row_index // width == column_index % slots) & (row_index % width == column_index // slots),
+        1.0,
+        0.0,
+    ).astype(jnp.bfloat16)
+    for t in range(span):
+        conv = jnp.dot(
+            jnp.concatenate([seq[past + t - tap] for tap in range(taps)], axis=1),
+            time_w[...],
+            preferred_element_type=jnp.float32,
+        )
+        square = jnp.sum(conv * conv, axis=1, keepdims=True)
+        scaled = conv * lax.rsqrt(square / channels + 1e-06) * gain
+        act[rows : (width + 1) * rows] = jax.nn.silu(scaled).astype(jnp.bfloat16)
+        kept_columns = space_w.shape[1]
+        total = conv[:, :kept_columns] + jnp.dot(
+            jnp.concatenate([act[tap * rows : tap * rows + tokens] for tap in range(3)], axis=1),
+            space_w[...],
+            preferred_element_type=jnp.float32,
+        )
+        total = jnp.where(live, total.reshape(width, rows, kept_columns), 0.0).astype(jnp.bfloat16)
+        for u in range(count):
+            part = total[:, u * slots : (u + 1) * slots].reshape(block, kept_columns)
+            part = jnp.dot(turn, part, preferred_element_type=jnp.float32).astype(jnp.bfloat16)
+            part = part.reshape(slots, width, kept_columns)
+            at = slice(u * slots, (u + 1) * slots)
+            kept[at, t] = part[:, :, : kept_columns // 2]
+            sent[at, t] = part[:, :, kept_columns // 2 :]
+
+
+def encode(width, span, index, near, far, carried, time_w, space_w, gain):
+    count = len(near)
+    slots, lanes = near[0].shape
+    rows = count * slots
+    side = lanes // (span * width)
+    past = carried.shape[1] // 2 // (side * width)
+    channels = time_w.shape[1]
+    vmem = pl.BlockSpec(memory_space=pltpu.VMEM)
+    part = space_w.shape[1] // 2
+    out = jax.ShapeDtypeStruct((rows, span, width, part), jnp.bfloat16)
+    tokens = rows * span * width
+    return pl.pallas_call(
+        functools.partial(encode_kernel, count, width),
+        out_shape=[out, out],
+        grid=(1,),
+        in_specs=[vmem] * (2 * count)
+        + [pl.BlockSpec((rows, carried.shape[1]), lambda i: (index, 0))]
+        + [vmem] * 3,
+        out_specs=[vmem] * 2,
+        scratch_shapes=[
+            pltpu.VMEM((past + span, width * rows, 2 * side), jnp.bfloat16),
+            pltpu.VMEM(((width + 2) * rows, channels), jnp.bfloat16),
+        ],
+        compiler_params=pltpu.CompilerParams(vmem_limit_bytes=VMEM_LIMIT),
+        cost_estimate=pl.CostEstimate(
+            flops=2 * tokens * (time_w.size + space_w.size),
+            bytes_accessed=2 * (time_w.size + space_w.size) + 16 * rows * lanes,
+            transcendentals=tokens * channels,
+        ),
+        name="encode_rows",
+    )(*near, *far, carried, time_w, space_w, gain)
+
+
+def place_kernel(order, chunks, offset_ref, *refs):
+    blocks, out = refs[:-1], refs[-1]
+    core = lax.axis_index("mp") % CORES
+    shifts = len(order)
+    for chunk in range(len(chunks)):
+        for u, shift in enumerate(chunks[chunk]):
+            residue = jnp.int32(0)
+            for j in range(shifts):
+                residue = jnp.where(offset_ref[j] == shift, jnp.int32(j), residue)
+            for kind in range(2):
+                out[core ^ kind, :, residue] = blocks[kind * len(chunks) + chunk][u]
+
+
+def place(order, chunks, pair_rows, offset, kept, got):
+    count = len(chunks[0])
+    rows, span, width, part = kept[0].shape
+    half_levels = rows // count // pair_rows
+    tail = (pair_rows, span, width, part)
+    blocks = [a.reshape((count, half_levels) + tail) for a in kept + got]
+    vmem = pl.BlockSpec(memory_space=pltpu.VMEM)
+    out = pl.pallas_call(
+        functools.partial(place_kernel, order, chunks),
+        out_shape=jax.ShapeDtypeStruct((CORES, half_levels, len(order)) + tail, jnp.bfloat16),
+        in_specs=[pl.BlockSpec(memory_space=pltpu.SMEM)] + [vmem] * len(blocks),
+        out_specs=vmem,
+        compiler_params=pltpu.CompilerParams(vmem_limit_bytes=VMEM_LIMIT),
+        cost_estimate=pl.CostEstimate(
+            flops=0, bytes_accessed=4 * sum(a.size for a in blocks), transcendentals=0
+        ),
+        name="place_rows",
+    )(offset, *blocks)
+    return out.reshape((-1, span, width, part))
+
+
+def routed_local(
+    frames,
+    cache,
+    group_offset,
+    cache_offset,
+    cache_group,
+    group_rows,
+    cache_live,
+    temporal_weight,
+    spatial_weight,
+    norm_gain,
+):
+    shifts = lax.axis_size("dp")
+    parts = lax.axis_size("mp")
+    groups = group_offset.shape[0]
+    rows, span, width, part_in = frames.shape
+    pair_rows = rows // groups
+    taps = temporal_weight.shape[0]
+    order = shift_order(shifts)
+    per_chunk = 2
+    chunks = [order[i : i + per_chunk] for i in range(0, shifts, per_chunk)]
+
+    def flip(x, mask):
+        return lax.ppermute(x, "mp", [(i, i ^ mask) for i in range(parts)])
+
+    def send(x, shift):
+        if shift == 0:
+            return x
+        return lax.ppermute(x, "dp", [(i, (i + shift) % shifts) for i in range(shifts)])
+
+    cache_rows = cache.transpose((1, 2, 3, 0)).reshape((-1, rows))
+    frame_rows = frames.transpose((1, 2, 3, 0)).reshape((-1, rows))
+    cache_packed = pack(
+        order,
+        pair_rows,
+        False,
+        cache_offset,
+        cache_live.reshape((1, groups)),
+        cache_rows,
+        flip(cache_rows, 1),
+    )
+    frame_packed = pack(
+        order,
+        pair_rows,
+        True,
+        group_offset,
+        group_rows.reshape((1, groups)),
+        frame_rows,
+        flip(frame_rows, 1),
+    )
+    flat_time = temporal_weight.reshape((-1, temporal_weight.shape[2]))
+    near = jnp.concatenate([flat_time, jnp.broadcast_to(norm_gain[None], (16, norm_gain.shape[0]))], axis=0)
+    space = spatial_weight.reshape((-1, spatial_weight.shape[2]))
+    far = flip(near, 2)
+    near_core, far_core, space_core = flip(near, 1), flip(far, 1), flip(space, 1)
+    time_w, space_w, gain = arrange_weights(
+        taps, near, near_core, jnp.concatenate([far, far_core], axis=0), space, space_core
+    )
+    cache_near = [send(x, k) for x, k in zip(cache_packed, order)]
+    cache_far = [flip(x, 2) for x in cache_near]
+    own = jnp.concatenate(cache_near, axis=0), jnp.concatenate(cache_far, axis=0)
+    other = flip(own[0], 1), flip(own[1], 1)
+    carried = choose(
+        order, pair_rows, group_offset, cache_offset, cache_group.reshape((1, groups)), own, other
+    )
+    frame_near = [send(x, k) for x, k in zip(frame_packed, order)]
+    frame_far = [flip(x, 2) for x in frame_near]
+    kept, got = [], []
+    for index in range(len(chunks)):
+        at = slice(index * per_chunk, (index + 1) * per_chunk)
+        keep, give = encode(
+            width, span, index, frame_near[at], frame_far[at], carried, time_w, space_w, gain
+        )
+        kept.append(keep)
+        got.append(flip(give, 1))
+    return place(order, chunks, pair_rows, group_offset, kept, got)
+
+
+def fits(mesh, frames, group_offset, temporal_weight):
+    shifts, parts = mesh.shape["dp"], mesh.shape["mp"]
+    groups = group_offset.shape[0]
+    rows = frames.shape[0] // shifts
+    if parts != 4 or frames.shape[3] != 64 * parts or groups > 256:
+        return False
+    if temporal_weight.shape[2] != 128 * parts or shifts % 2:
+        return False
+    if groups % (shifts * CORES):
+        return False
+    return rows // shifts // CORES % 16 == 0 and rows % 128 == 0
+
+
 def solution(mesh):
     in_specs = (
         P("dp", None, None, "mp"),
@@ -143,4 +575,11 @@
         P("mp"),
     )
     out_specs = P("dp", None, None, "mp")
-    return jax.shard_map(local, mesh=mesh, in_specs=in_specs, out_specs=out_specs, check_vma=False)
+
+    def call(*args):
+        body = routed_local if fits(mesh, args[0], args[2], args[7]) else plain_local
+        return jax.shard_map(
+            body, mesh=mesh, in_specs=in_specs, out_specs=out_specs, check_vma=False
+        )(*args)
+
+    return call

time: 310 us -> 144 us (0.46)
  local copies, waits for them, and re-layouts: 110 us -> 5.68 us
  waiting for transfers between devices: 123 us -> 52.9 us
  Pallas kernels: 0 us -> 43.5 us
  starting transfers between devices: 17.7 us -> 39.7 us
  blocking collectives: 18.9 us -> 0 us
  matrix products: 15.7 us -> 0 us
  between operations: 13.7 us -> 0.36 us
  other arithmetic: 8.86 us -> 0.79 us
    all_gather x2 -> x0, waiting for transfers between devices: 108 us -> none  [the longest x1 60.4 us: local(): lax.all_gather(sequence, 'mp', axis=3, tiled=True)]
    ppermute x0 -> x42, waiting for transfers between devices: none -> 52.9 us  [the longest x28 29.5 us: flip(): return lax.ppermute(x, 'mp', [(i, i ^ mask) for i in range(parts)])]
    pallas_call x0 -> x9, Pallas kernels: none -> 43.5 us  [the longest x4 26.2 us: encode(): pl.pallas_call(functools.partial(encode_kernel, count, width), out_shape=...]
    ppermute x0 -> x42, starting transfers between devices: none -> 39.7 us  [the longest x28 20.2 us: flip(): return lax.ppermute(x, 'mp', [(i, i ^ mask) for i in range(parts)])]
    unnamed x23 -> x84, local copies, waits for them, and re-layouts: 43.7 us -> 5.65 us
    scatter x4 -> x0, local copies, waits for them, and re-layouts: 26 us -> none  [to_slots(): buffer = jnp.zeros((owner_count * per_pair,) + values.shape[1:], values.d...]
    slice x2 -> x0, local copies, waits for them, and re-layouts: 18.3 us -> none  [the longest x1 9.19 us: spatial_conv(): padded[:, :, tap_index:tap_index + width]]
    all_to_all x3 -> x0, starting transfers between devices: 17.4 us -> none  [the longest x1 6.35 us: local(): lax.all_to_all(to_slots(cache_grouped, cache_send, owner_count, per_pair)...]
  transfers between devices with their start and end apart: 5 -> 42, of which waited for: 4 -> 17; matrix products, arithmetic and copies ran while one was open for 18% -> 1% of each run, Pallas kernels for 0% -> 28%
where the time goes in v1:
time: 144 us; the launch traced here: 143 us
  waiting for transfers between devices  52.9 us (37%)
  Pallas kernels  43.5 us (30%)
  starting transfers between devices  39.7 us (28%)
  local copies, waits for them, and re-layouts  5.68 us (4%)
    ppermute x28, waiting for transfers between devices, flip(): return lax.ppermute(x, 'mp', [(i, i ^ mask) for i in range(parts)])  29.5 us
    pallas_call x4, Pallas kernels, encode(): pl.pallas_call(functools.partial(encode_kernel, count, width), out_shape=...  26.2 us
    ppermute x14, waiting for transfers between devices, send(): lax.ppermute(x, 'dp', [(i, (i + shift) % shifts) for i in range(shifts)])  23.4 us
    ppermute x28, starting transfers between devices, flip(): return lax.ppermute(x, 'mp', [(i, i ^ mask) for i in range(parts)])  20.2 us
    ppermute x14, starting transfers between devices, send(): lax.ppermute(x, 'dp', [(i, (i + shift) % shifts) for i in range(shifts)])  19.5 us
    pallas_call x2, Pallas kernels, pack(): pl.pallas_call(functools.partial(pack_kernel, order, pair_rows, mark_dead...  7.02 us
    unnamed x84, local copies, waits for them, and re-layouts  5.65 us
    pallas_call x1, Pallas kernels, choose(): pl.pallas_call(functools.partial(choose_kernel, order, pair_rows), out_sh...  4.45 us
  transfers between devices with their start and end apart: 42, of which 17 were waited for; matrix products, arithmetic and copies ran while one was open for 1% of the time, Pallas kernels for 28%

profile of v1, /device:TPU:11, one launch (start us, length us, event | category | flops | bytes accessed | tf_op | source)
XLA Modules:
  0.0 142.9 jit_solution(2947237820258170445)
XLA Ops:
  4.1 3.5 %pack_carried.1 = (bf16[16,4096]{1,0:T(8,128)(2,1)}, bf16[16,4096]{1,0:T(8,128)(2,1)}, bf16[16,4096]{1,0:T(8,128)(2,1)}, bf16[16,4096]{1,0:T(8,128)(2,1)}, bf16[...) custom-call(s32[128]{0:T(128)} %cache_offset_ref.1, ...), custom_call_target="tpu_custom_call" | custom-call | flops 268435456 | bytes 3145728 | tf_op jit(solution)/shard_map/pack_carried/pallas_call | solution.py:214
  14.5 8.5 %collective-permute-done.5 = bf16[16,4096]{1,0:T(8,128)(2,1)S(1)} collective-permute-done((bf16[16,4096]{1,0:T(8,128)(2,1)}, bf16[16,4096]{1,0:T(8,128)(2,1)S(1)}, u32[]{:S(2)}, u32[]{:S(2)}) %collective-permute-start.5) | collective-permute-done | bytes 131104 | tf_op jit(solution)/shard_map/ppermute | solution.py:501
  23.1 2.8 %collective-permute-done.6 = bf16[16,4096]{1,0:T(8,128)(2,1)S(1)} collective-permute-done((bf16[16,4096]{1,0:T(8,128)(2,1)}, bf16[16,4096]{1,0:T(8,128)(2,1)S(1)}, u32[]{:S(2)}, u32[]{:S(2)}) %collective-permute-start.6) | collective-permute-done | bytes 131104 | tf_op jit(solution)/shard_map/ppermute | solution.py:501
  26.0 4.8 %collective-permute-done.8 = bf16[16,4096]{1,0:T(8,128)(2,1)S(1)} collective-permute-done((bf16[16,4096]{1,0:T(8,128)(2,1)}, bf16[16,4096]{1,0:T(8,128)(2,1)S(1)}, u32[]{:S(2)}, u32[]{:S(2)}) %collective-permute-start.8) | collective-permute-done | bytes 131104 | tf_op jit(solution)/shard_map/ppermute | solution.py:501
  39.6 3.3 %collective-permute-done.13 = bf16[16,4096]{1,0:T(8,128)(2,1)S(1)} collective-permute-done((bf16[16,4096]{1,0:T(8,128)(2,1)S(1)}, bf16[16,4096]{1,0:T(8,128)(2,1)S(1)}, u32[]{:S(2)}, u32[]{:S(2)}) %collective-permute-start.13) | collective-permute-done | bytes 131104 | tf_op jit(solution)/shard_map/ppermute | solution.py:496
  43.2 2.6 %collective-permute-done.14 = bf16[16,4096]{1,0:T(8,128)(2,1)S(1)} collective-permute-done((bf16[16,4096]{1,0:T(8,128)(2,1)S(1)}, bf16[16,4096]{1,0:T(8,128)(2,1)S(1)}, u32[]{:S(2)}, u32[]{:S(2)}) %collective-permute-start.14) | collective-permute-done | bytes 131104 | tf_op jit(solution)/shard_map/ppermute | solution.py:496
  46.0 2.6 %collective-permute-done.15 = bf16[16,4096]{1,0:T(8,128)(2,1)S(1)} collective-permute-done((bf16[16,4096]{1,0:T(8,128)(2,1)S(1)}, bf16[16,4096]{1,0:T(8,128)(2,1)S(1)}, u32[]{:S(2)}, u32[]{:S(2)}) %collective-permute-start.15) | collective-permute-done | bytes 131104 | tf_op jit(solution)/shard_map/ppermute | solution.py:496
  48.8 2.6 %collective-permute-done.16 = bf16[16,4096]{1,0:T(8,128)(2,1)S(1)} collective-permute-done((bf16[16,4096]{1,0:T(8,128)(2,1)S(1)}, bf16[16,4096]{1,0:T(8,128)(2,1)S(1)}, u32[]{:S(2)}, u32[]{:S(2)}) %collective-permute-start.16) | collective-permute-done | bytes 131104 | tf_op jit(solution)/shard_map/ppermute | solution.py:496
  51.6 2.6 %collective-permute-done.17 = bf16[16,4096]{1,0:T(8,128)(2,1)S(1)} collective-permute-done((bf16[16,4096]{1,0:T(8,128)(2,1)S(1)}, bf16[16,4096]{1,0:T(8,128)(2,1)S(1)}, u32[]{:S(2)}, u32[]{:S(2)}) %collective-permute-start.17) | collective-permute-done | bytes 131104 | tf_op jit(solution)/shard_map/ppermute | solution.py:496
  54.2 2.8 %collective-permute-done.18 = bf16[16,4096]{1,0:T(8,128)(2,1)S(1)} collective-permute-done((bf16[16,4096]{1,0:T(8,128)(2,1)S(1)}, bf16[16,4096]{1,0:T(8,128)(2,1)S(1)}, u32[]{:S(2)}, u32[]{:S(2)}) %collective-permute-start.18) | collective-permute-done | bytes 131104 | tf_op jit(solution)/shard_map/ppermute | solution.py:496
  57.0 2.8 %collective-permute-done.19 = bf16[16,4096]{1,0:T(8,128)(2,1)S(1)} collective-permute-done((bf16[16,4096]{1,0:T(8,128)(2,1)S(1)}, bf16[16,4096]{1,0:T(8,128)(2,1)S(1)}, u32[]{:S(2)}, u32[]{:S(2)}) %collective-permute-start.19) | collective-permute-done | bytes 131104 | tf_op jit(solution)/shard_map/ppermute | solution.py:496
  61.4 6.0 %collective-permute-done.23 = bf16[784,128]{1,0:T(8,128)(2,1)S(1)} collective-permute-done((bf16[784,128]{1,0:T(8,128)(2,1)S(1)}, bf16[784,128]{1,0:T(8,128)(2,1)S(1)}, u32[]{:S(2)}, u32[]{:S(2)}) %collective-permute-start.23) | collective-permute-done | bytes 200736 | tf_op jit(solution)/shard_map/ppermute | solution.py:496
  69.2 3.5 %pack_dead.1 = (bf16[16,4096]{1,0:T(8,128)(2,1)}, bf16[16,4096]{1,0:T(8,128)(2,1)}, bf16[16,4096]{1,0:T(8,128)(2,1)}, bf16[16,4096]{1,0:T(8,128)(2,1)}, bf16[16,...) custom-call(s32[128]{0:T(128)} %offset_ref.5, ...), custom_call_target="tpu_custom_call" | custom-call | flops 268435456 | bytes 3145728 | tf_op jit(solution)/shard_map/pack_dead/pallas_call | solution.py:214
  72.8 2.9 %collective-permute-start.34 = (bf16[16,4096]{1,0:T(8,128)(2,1)}, bf16[16,4096]{1,0:T(8,128)(2,1)S(1)}, u32[]{:S(2)}, u32[]{:S(2)}) collective-permute-start(bf16[16,4096]{1,0:T(8,128)(2,1)} %get-tuple-element.52), channel_id=1, source_target_pairs={{0,4},{4,8},{8,12},{12,16},{16,20},{20,24},{24,28},{28,0},{1,5},{5... | collective-permute-start | bytes 393224 | tf_op jit(solution)/shard_map/ppermute | solution.py:501
  78.9 4.5 %collective-permute-start.31 = (bf16[16,4096]{1,0:T(8,128)(2,1)}, bf16[16,4096]{1,0:T(8,128)(2,1)S(1)}, u32[]{:S(2)}, u32[]{:S(2)}) collective-permute-start(bf16[16,4096]{1,0:T(8,128)(2,1)} %get-tuple-element.50), channel_id=1, source_target_pairs={{0,24},{4,28},{8,0},{12,4},{16,8},{20,12},{24,16},{28,20},{1,25},{... | collective-permute-start | bytes 393224 | tf_op jit(solution)/shard_map/ppermute | solution.py:501
  85.7 2.9 %arrange_weights.1 = (bf16[768,512]{1,0:T(8,128)(2,1)}, bf16[1536,256]{1,0:T(8,128)(2,1)}, bf16[16,512]{1,0:T(8,128)(2,1)}) custom-call(bf16[784,128]{1,0:T(8,128)(2,1)} %copy-done.6, bf16[784,128]{1,0:T(8,128)(2,1)} %copy-done.13, bf16[1568,128]{1,0:T(8,128)(2,1)} %pad_maximum_fusion.far_core, bf16[1536,128]{1,0:T(8,128)(2,1)} %bitcast.23, ...), custom_call_target="tpu_custom_call" | custom-call | bytes 3178496 | tf_op jit(solution)/shard_map/arrange_weights/pallas_call | solution.py:326
  90.5 4.5 %choose_carried.1.refs_4_ = bf16[128,8192]{1,0:T(8,128)(2,1)} custom-call(s32[128]{0:T(128)} %offset_ref.5, s32[128]{0:T(128)} %cache_offset_ref.1, s32[1,128]{1,0:T(1,128)} %bitcast.34, bf16[128,4096]{1,0:T(8,128)(2,1)} %copy-done, bf16[128,4096]{1,0:T(8,128)(2,1)} %copy-done.1, bf16[128,4096]{1,0:T(8,128)(2,1)} %copy-done.4, bf16[128,4096]{1,0:T(8,128)(2,1)} %copy-done.5), custom_call_target="tpu_custom_call" | custom-call | flops 536870912 | bytes 6291456 | tf_op jit(solution)/shard_map/choose_carried/pallas_call | solution.py:274
  95.8 3.4 %collective-permute-start.1 = (bf16[16,4096]{1,0:T(8,128)(2,1)S(1)}, bf16[16,4096]{1,0:T(8,128)(2,1)S(1)}, u32[]{:S(2)}, u32[]{:S(2)}) collective-permute-start(bf16[16,4096]{1,0:T(8,128)(2,1)S(1)} %copy-done.18), channel_id=1, source_target_pairs={{0,16},{4,20},{8,24},{12,28},{16,0},{20,4},{24,8},{28,12},{1,17},{... | collective-permute-start | bytes 393224 | tf_op jit(solution)/shard_map/ppermute | solution.py:501
  100.7 6.6 %encode_rows.7 = (bf16[32,2,16,128]{3,2,1,0:T(8,128)(2,1)}, bf16[32,2,16,128]{3,2,1,0:T(8,128)(2,1)}) custom-call(bf16[16,4096]{1,0:T(8,128)(2,1)} %copy-done.24, bf16[16,4096]{1,0:T(8,128)(2,1)} %copy-done.26, bf16[16,4096]{1,0:T(8,128)(2,1)} %copy-done.28, bf16[16,4096]{1,0:T(8,128)(2,1)} %copy-done.29, bf16[128,8192]{1,0:T(8,128)(2,1)} %choose_carried.1.refs_4_, ...), custom_call_target="tpu_custom_call" | custom-call | flops 1610612736 | bytes 3670016 | tf_op jit(solution)/shard_map/encode_rows/pallas_call | solution.py:417
  110.3 4.3 %collective-permute-start.41 = (bf16[32,2,16,128]{3,2,1,0:T(8,128)(2,1)}, bf16[32,2,16,128]{3,2,1,0:T(8,128)(2,1)S(1)}, u32[]{:S(2)}, u32[]{:S(2)}) collective-permute-start(bf16[32,2,16,128]{3,2,1,0:T(8,128)(2,1)} %get-tuple-element.58), channel_id=1, source_target_pairs={{0,1},{1,0},{2,3},{3,2},{4,5},{5,4},{6,7},{7,6},{8,9},{9,8},{10,11... | collective-permute-start | bytes 786440 | tf_op jit(solution)/shard_map/ppermute | solution.py:496
  114.6 6.6 %encode_rows.6 = (bf16[32,2,16,128]{3,2,1,0:T(8,128)(2,1)}, bf16[32,2,16,128]{3,2,1,0:T(8,128)(2,1)}) custom-call(bf16[16,4096]{1,0:T(8,128)(2,1)} %copy-done.17, bf16[16,4096]{1,0:T(8,128)(2,1)} %copy-done.19, bf16[16,4096]{1,0:T(8,128)(2,1)} %copy-done.30, bf16[16,4096]{1,0:T(8,128)(2,1)} %copy-done.31, bf16[128,8192]{1,0:T(8,128)(2,1)} %choose_carried.1.refs_4_, ...), custom_call_target="tpu_custom_call" | custom-call | flops 1610612736 | bytes 3670016 | tf_op jit(solution)/shard_map/encode_rows/pallas_call | solution.py:417
  122.6 6.5 %encode_rows.5 = (bf16[32,2,16,128]{3,2,1,0:T(8,128)(2,1)}, bf16[32,2,16,128]{3,2,1,0:T(8,128)(2,1)}) custom-call(bf16[16,4096]{1,0:T(8,128)(2,1)} %copy-done.23, bf16[16,4096]{1,0:T(8,128)(2,1)} %copy-done.25, bf16[16,4096]{1,0:T(8,128)(2,1)} %copy-done.33, bf16[16,4096]{1,0:T(8,128)(2,1)} %copy-done.34, bf16[128,8192]{1,0:T(8,128)(2,1)} %choose_carried.1.refs_4_, ...), custom_call_target="tpu_custom_call" | custom-call | flops 1610612736 | bytes 3670016 | tf_op jit(solution)/shard_map/encode_rows/pallas_call | solution.py:417
  131.0 6.5 %encode_rows.4 = (bf16[32,2,16,128]{3,2,1,0:T(8,128)(2,1)}, bf16[32,2,16,128]{3,2,1,0:T(8,128)(2,1)}) custom-call(bf16[16,4096]{1,0:T(8,128)(2,1)} %get-tuple-element.32.refs_0_, bf16[16,4096]{1,0:T(8,128)(2,1)} %copy-done.22, bf16[16,4096]{1,0:T(8,128)(2,1)} %copy-done.27, bf16[16,4096]{1,0:T(8,128)(2,1)} %copy-done.32, ...), custom_call_target="tpu_custom_call" | custom-call | flops 1610612736 | bytes 3670016 | tf_op jit(solution)/shard_map/encode_rows/pallas_call | solution.py:417
  139.9 3.0 %place_rows.1 = bf16[2,8,8,2,2,16,128]{6,5,4,3,2,1,0:T(8,128)(2,1)} custom-call(s32[128]{0:T(128)} %offset_ref.5, bf16[2,8,2,2,16,128]{5,4,3,2,1,0:T(8,128)(2,1)} %bitcast.31, bf16[2,8,2,2,16,128]{5,4,3,2,1,0:T(8,128)(2,1)} %bitcast.29, bf16[2,8,2,2,16,128]{5,4,3,2,1,0:T(8,128)(2,1)} %bitcast.27, bf16[2,8,2,2,16,128]{5,4,3,2,1,0:T(8,128)(2,1)} %bitcast.25, ...), custom_call_target="tpu_custom_call" | custom-call | bytes 4194304 | tf_op jit(solution)/shard_map/place_rows/pallas_call | solution.py:459
  (158 shorter events, 42.7 us)
Async XLA Ops:
  0.7 67.6 %collective-permute-start = (bf16[2048,256]{1,0:T(8,128)(2,1)}, bf16[2048,256]{1,0:T(8,128)(2,1)S(1)}, u32[]{:S(2)}, u32[]{:S(2)}) collective-permute-start(bf16[2048,256]{1,0:T(8,128)(2,1)} %bitcast.21), channel_id=1, source_target_pairs={{0,1},{1,0},{2,3},{3,2},{4,5},{5,4},{6,7},{7,6},{8,9},{9,8},{10,11... | collective-permute-start | bytes 3145736 | tf_op jit(solution)/shard_map/ppermute | solution.py:496
  7.6 31.7 %collective-permute-start.12 = (bf16[16,4096]{1,0:T(8,128)(2,1)}, bf16[16,4096]{1,0:T(8,128)(2,1)S(1)}, u32[]{:S(2)}, u32[]{:S(2)}) collective-permute-start(bf16[16,4096]{1,0:T(8,128)(2,1)} %get-tuple-element.34), channel_id=1, source_target_pairs={{0,2},{1,3},{2,0},{3,1},{4,6},{5,7},{6,4},{7,5},{8,10},{9,11},{10,... | collective-permute-start | bytes 393224 | tf_op jit(solution)/shard_map/ppermute | solution.py:496
  8.9 14.2 %collective-permute-start.5 = (bf16[16,4096]{1,0:T(8,128)(2,1)}, bf16[16,4096]{1,0:T(8,128)(2,1)S(1)}, u32[]{:S(2)}, u32[]{:S(2)}) collective-permute-start(bf16[16,4096]{1,0:T(8,128)(2,1)} %get-tuple-element.35), channel_id=1, source_target_pairs={{0,16},{4,20},{8,24},{12,28},{16,0},{20,4},{24,8},{28,12},{1,17},{... | collective-permute-start | bytes 393224 | tf_op jit(solution)/shard_map/ppermute | solution.py:501
  12.1 13.7 %collective-permute-start.6 = (bf16[16,4096]{1,0:T(8,128)(2,1)}, bf16[16,4096]{1,0:T(8,128)(2,1)S(1)}, u32[]{:S(2)}, u32[]{:S(2)}) collective-permute-start(bf16[16,4096]{1,0:T(8,128)(2,1)} %get-tuple-element.36), channel_id=1, source_target_pairs={{0,12},{4,16},{8,20},{12,24},{16,28},{20,0},{24,4},{28,8},{1,13},{... | collective-permute-start | bytes 393224 | tf_op jit(solution)/shard_map/ppermute | solution.py:501
  12.2 13.6 %collective-permute-start.7 = (bf16[16,4096]{1,0:T(8,128)(2,1)}, bf16[16,4096]{1,0:T(8,128)(2,1)S(1)}, u32[]{:S(2)}, u32[]{:S(2)}) collective-permute-start(bf16[16,4096]{1,0:T(8,128)(2,1)} %get-tuple-element.37), channel_id=1, source_target_pairs={{0,20},{4,24},{8,28},{12,0},{16,4},{20,8},{24,12},{28,16},{1,21},{... | collective-permute-start | bytes 393224 | tf_op jit(solution)/shard_map/ppermute | solution.py:501
  36.1 47.6 %collective-permute-start.20 = (bf16[128,4096]{1,0:T(8,128)(2,1)S(1)}, bf16[128,4096]{1,0:T(8,128)(2,1)S(1)}, u32[]{:S(2)}, u32[]{:S(2)}) collective-permute-start(bf16[128,4096]{1,0:T(8,128)(2,1)S(1)} %constant_dynamic-update-slice_fusion.own0), channel_id=1, source_target_pairs={{0,1},{1,0},{2,3},{3,2},{4,5},{5,4},{6,7},{7,6},{8,9},{9,8},{10,11... | collective-permute-start | bytes 3145736 | tf_op jit(solution)/shard_map/ppermute | solution.py:496
  39.3 9.2 %collective-permute-start.15 = (bf16[16,4096]{1,0:T(8,128)(2,1)S(1)}, bf16[16,4096]{1,0:T(8,128)(2,1)S(1)}, u32[]{:S(2)}, u32[]{:S(2)}) collective-permute-start(bf16[16,4096]{1,0:T(8,128)(2,1)S(1)} %collective-permute-done.7), channel_id=1, source_target_pairs={{0,2},{1,3},{2,0},{3,1},{4,6},{5,7},{6,4},{7,5},{8,10},{9,11},{10,... | collective-permute-start | bytes 393224 | tf_op jit(solution)/shard_map/ppermute | solution.py:496
  59.8 28.8 %collective-permute-start.21 = (bf16[128,4096]{1,0:T(8,128)(2,1)S(1)}, bf16[128,4096]{1,0:T(8,128)(2,1)S(1)}, u32[]{:S(2)}, u32[]{:S(2)}) collective-permute-start(bf16[128,4096]{1,0:T(8,128)(2,1)S(1)} %constant_dynamic-update-slice_fusion.8.own1), channel_id=1, source_target_pairs={{0,1},{1,0},{2,3},{3,2},{4,5},{5,4},{6,7},{7,6},{8,9},{9,8},{10,11... | collective-permute-start | bytes 3145736 | tf_op jit(solution)/shard_map/ppermute | solution.py:496
  61.1 14.6 %collective-permute-start.25 = (bf16[1536,128]{1,0:T(8,128)(2,1)S(1)}, bf16[1536,128]{1,0:T(8,128)(2,1)S(1)}, u32[]{:S(2)}, u32[]{:S(2)}) collective-permute-start(bf16[1536,128]{1,0:T(8,128)(2,1)S(1)} %bitcast.24), channel_id=1, source_target_pairs={{0,1},{1,0},{2,3},{3,2},{4,5},{5,4},{6,7},{7,6},{8,9},{9,8},{10,11... | collective-permute-start | bytes 1179656 | tf_op jit(solution)/shard_map/ppermute | solution.py:496
  75.6 19.3 %collective-permute-start.30 = (bf16[16,4096]{1,0:T(8,128)(2,1)}, bf16[16,4096]{1,0:T(8,128)(2,1)S(1)}, u32[]{:S(2)}, u32[]{:S(2)}) collective-permute-start(bf16[16,4096]{1,0:T(8,128)(2,1)} %get-tuple-element.49), channel_id=1, source_target_pairs={{0,8},{4,12},{8,16},{12,20},{16,24},{20,28},{24,0},{28,4},{1,9},{5... | collective-permute-start | bytes 393224 | tf_op jit(solution)/shard_map/ppermute | solution.py:501
  78.9 16.8 %collective-permute-start.31 = (bf16[16,4096]{1,0:T(8,128)(2,1)}, bf16[16,4096]{1,0:T(8,128)(2,1)S(1)}, u32[]{:S(2)}, u32[]{:S(2)}) collective-permute-start(bf16[16,4096]{1,0:T(8,128)(2,1)} %get-tuple-element.50), channel_id=1, source_target_pairs={{0,24},{4,28},{8,0},{12,4},{16,8},{20,12},{24,16},{28,20},{1,25},{... | collective-permute-start | bytes 393224 | tf_op jit(solution)/shard_map/ppermute | solution.py:501
  83.5 15.8 %collective-permute-start.36 = (bf16[16,4096]{1,0:T(8,128)(2,1)S(1)}, bf16[16,4096]{1,0:T(8,128)(2,1)S(1)}, u32[]{:S(2)}, u32[]{:S(2)}) collective-permute-start(bf16[16,4096]{1,0:T(8,128)(2,1)S(1)} %collective-permute-done.34.refs_0_), channel_id=1, source_target_pairs={{0,2},{1,3},{2,0},{3,1},{4,6},{5,7},{6,4},{7,5},{8,10},{9,11},{10,... | collective-permute-start | bytes 393224 | tf_op jit(solution)/shard_map/ppermute | solution.py:496
  83.7 15.8 %collective-permute-start.37 = (bf16[16,4096]{1,0:T(8,128)(2,1)S(1)}, bf16[16,4096]{1,0:T(8,128)(2,1)S(1)}, u32[]{:S(2)}, u32[]{:S(2)}) collective-permute-start(bf16[16,4096]{1,0:T(8,128)(2,1)S(1)} %collective-permute-done.35.refs_1_), channel_id=1, source_target_pairs={{0,2},{1,3},{2,0},{3,1},{4,6},{5,7},{6,4},{7,5},{8,10},{9,11},{10,... | collective-permute-start | bytes 393224 | tf_op jit(solution)/shard_map/ppermute | solution.py:496
  88.6 18.7 %collective-permute-start.26 = (bf16[16,4096]{1,0:T(8,128)(2,1)S(1)}, bf16[16,4096]{1,0:T(8,128)(2,1)S(1)}, u32[]{:S(2)}, u32[]{:S(2)}) collective-permute-start(bf16[16,4096]{1,0:T(8,128)(2,1)S(1)} %copy-done.21), channel_id=1, source_target_pairs={{0,12},{4,16},{8,20},{12,24},{16,28},{20,0},{24,4},{28,8},{1,13},{... | collective-permute-start | bytes 393224 | tf_op jit(solution)/shard_map/ppermute | solution.py:501
  95.0 13.0 %collective-permute-start.27 = (bf16[16,4096]{1,0:T(8,128)(2,1)S(1)}, bf16[16,4096]{1,0:T(8,128)(2,1)S(1)}, u32[]{:S(2)}, u32[]{:S(2)}) collective-permute-start(bf16[16,4096]{1,0:T(8,128)(2,1)S(1)} %copy-done.20), channel_id=1, source_target_pairs={{0,20},{4,24},{8,28},{12,0},{16,4},{20,8},{24,12},{28,16},{1,21},{... | collective-permute-start | bytes 393224 | tf_op jit(solution)/shard_map/ppermute | solution.py:501
  95.8 13.1 %collective-permute-start.1 = (bf16[16,4096]{1,0:T(8,128)(2,1)S(1)}, bf16[16,4096]{1,0:T(8,128)(2,1)S(1)}, u32[]{:S(2)}, u32[]{:S(2)}) collective-permute-start(bf16[16,4096]{1,0:T(8,128)(2,1)S(1)} %copy-done.18), channel_id=1, source_target_pairs={{0,16},{4,20},{8,24},{12,28},{16,0},{20,4},{24,8},{28,12},{1,17},{... | collective-permute-start | bytes 393224 | tf_op jit(solution)/shard_map/ppermute | solution.py:501
  99.2 10.3 %collective-permute-start.32 = (bf16[16,4096]{1,0:T(8,128)(2,1)S(1)}, bf16[16,4096]{1,0:T(8,128)(2,1)S(1)}, u32[]{:S(2)}, u32[]{:S(2)}) collective-permute-start(bf16[16,4096]{1,0:T(8,128)(2,1)S(1)} %collective-permute-done.30.refs_0_), channel_id=1, source_target_pairs={{0,2},{1,3},{2,0},{3,1},{4,6},{5,7},{6,4},{7,5},{8,10},{9,11},{10,... | collective-permute-start | bytes 393224 | tf_op jit(solution)/shard_map/ppermute | solution.py:496
  99.5 10.8 %collective-permute-start.33 = (bf16[16,4096]{1,0:T(8,128)(2,1)S(1)}, bf16[16,4096]{1,0:T(8,128)(2,1)S(1)}, u32[]{:S(2)}, u32[]{:S(2)}) collective-permute-start(bf16[16,4096]{1,0:T(8,128)(2,1)S(1)} %collective-permute-done.31.refs_1_), channel_id=1, source_target_pairs={{0,2},{1,3},{2,0},{3,1},{4,6},{5,7},{6,4},{7,5},{8,10},{9,11},{10,... | collective-permute-start | bytes 393224 | tf_op jit(solution)/shard_map/ppermute | solution.py:496
  107.3 22.3 %collective-permute-start.2 = (bf16[16,4096]{1,0:T(8,128)(2,1)S(1)}, bf16[16,4096]{1,0:T(8,128)(2,1)S(1)}, u32[]{:S(2)}, u32[]{:S(2)}) collective-permute-start(bf16[16,4096]{1,0:T(8,128)(2,1)S(1)} %copy-done.16), channel_id=1, source_target_pairs={{0,2},{1,3},{2,0},{3,1},{4,6},{5,7},{6,4},{7,5},{8,10},{9,11},{10,... | collective-permute-start | bytes 393224 | tf_op jit(solution)/shard_map/ppermute | solution.py:496
  108.0 13.1 %collective-permute-start.28 = (bf16[16,4096]{1,0:T(8,128)(2,1)S(1)}, bf16[16,4096]{1,0:T(8,128)(2,1)S(1)}, u32[]{:S(2)}, u32[]{:S(2)}) collective-permute-start(bf16[16,4096]{1,0:T(8,128)(2,1)S(1)} %collective-permute-done.26.refs_0_), channel_id=1, source_target_pairs={{0,2},{1,3},{2,0},{3,1},{4,6},{5,7},{6,4},{7,5},{8,10},{9,11},{10,... | collective-permute-start | bytes 393224 | tf_op jit(solution)/shard_map/ppermute | solution.py:496
  108.9 13.0 %collective-permute-start.29 = (bf16[16,4096]{1,0:T(8,128)(2,1)S(1)}, bf16[16,4096]{1,0:T(8,128)(2,1)S(1)}, u32[]{:S(2)}, u32[]{:S(2)}) collective-permute-start(bf16[16,4096]{1,0:T(8,128)(2,1)S(1)} %collective-permute-done.27.refs_1_), channel_id=1, source_target_pairs={{0,2},{1,3},{2,0},{3,1},{4,6},{5,7},{6,4},{7,5},{8,10},{9,11},{10,... | collective-permute-start | bytes 393224 | tf_op jit(solution)/shard_map/ppermute | solution.py:496
  109.5 20.2 %collective-permute-start.3 = (bf16[16,4096]{1,0:T(8,128)(2,1)S(1)}, bf16[16,4096]{1,0:T(8,128)(2,1)S(1)}, u32[]{:S(2)}, u32[]{:S(2)}) collective-permute-start(bf16[16,4096]{1,0:T(8,128)(2,1)S(1)} %collective-permute-done.1.refs_1_), channel_id=1, source_target_pairs={{0,2},{1,3},{2,0},{3,1},{4,6},{5,7},{6,4},{7,5},{8,10},{9,11},{10,... | collective-permute-start | bytes 393224 | tf_op jit(solution)/shard_map/ppermute | solution.py:496
  110.3 27.2 %collective-permute-start.41 = (bf16[32,2,16,128]{3,2,1,0:T(8,128)(2,1)}, bf16[32,2,16,128]{3,2,1,0:T(8,128)(2,1)S(1)}, u32[]{:S(2)}, u32[]{:S(2)}) collective-permute-start(bf16[32,2,16,128]{3,2,1,0:T(8,128)(2,1)} %get-tuple-element.58), channel_id=1, source_target_pairs={{0,1},{1,0},{2,3},{3,2},{4,5},{5,4},{6,7},{7,6},{8,9},{9,8},{10,11... | collective-permute-start | bytes 786440 | tf_op jit(solution)/shard_map/ppermute | solution.py:496
  121.2 16.3 %collective-permute-start.40 = (bf16[32,2,16,128]{3,2,1,0:T(8,128)(2,1)}, bf16[32,2,16,128]{3,2,1,0:T(8,128)(2,1)S(1)}, u32[]{:S(2)}, u32[]{:S(2)}) collective-permute-start(bf16[32,2,16,128]{3,2,1,0:T(8,128)(2,1)} %get-tuple-element.57), channel_id=1, source_target_pairs={{0,1},{1,0},{2,3},{3,2},{4,5},{5,4},{6,7},{7,6},{8,9},{9,8},{10,11... | collective-permute-start | bytes 786440 | tf_op jit(solution)/shard_map/ppermute | solution.py:496
  (53 other events, 530.9 us)

commit v2 on v1

v2 whole, which is shorter than its diff:
```python
import functools

import jax
import jax.numpy as jnp
from jax import lax
from jax.experimental import pallas as pl
from jax.experimental.pallas import tpu as pltpu
from jax.sharding import PartitionSpec as P


def temporal_conv(sequence, weight_part, span_steps):
    taps = weight_part.shape[0]
    windows = [
        sequence[:, taps - 1 - tap_index : taps - 1 - tap_index + span_steps]
        for tap_index in range(taps)
    ]
    joined = jnp.concatenate(windows, axis=3)
    flat_weight = weight_part.reshape((taps * weight_part.shape[1], weight_part.shape[2]))
    return jnp.einsum("rtwc,cd->rtwd", joined, flat_weight, preferred_element_type=jnp.float32)


def spatial_conv(activated, weight_part):
    width = activated.shape[2]
    padded = jnp.pad(activated, ((0, 0), (0, 0), (1, 1), (0, 0)))
    joined = jnp.concatenate(
        [padded[:, :, tap_index : tap_index + width] for tap_index in range(3)], axis=3
    )
    flat_weight = weight_part.reshape((3 * weight_part.shape[1], weight_part.shape[2]))
    return jnp.einsum("rtwc,cd->rtwd", joined, flat_weight, preferred_element_type=jnp.float32)


def to_slots(values, slot_index, owner_count, per_pair):
    buffer = (
        jnp.zeros((owner_count * per_pair,) + values.shape[1:], values.dtype)
        .at[slot_index]
        .set(values)
    )
    return buffer.reshape((owner_count, per_pair) + values.shape[1:])


def plain_local(
    frames,
    cache,
    group_offset,
    cache_offset,
    cache_group,
    group_rows,
    cache_live,
    temporal_weight,
    spatial_weight,
    norm_gain,
):
    owner_count = lax.axis_size("dp")
    my_rank = lax.axis_index("dp")
    groups = group_offset.shape[0]
    pair_rows = frames.shape[0] // groups
    span_steps = frames.shape[1]
    per_pair = (groups + owner_count - 1) // owner_count
    group_index = jnp.arange(groups, dtype=jnp.int32)
    slot_level = group_index // owner_count
    grouped = frames.reshape((groups, pair_rows) + frames.shape[1:])
    counts = group_rows.reshape(groups)
    send_slot = (my_rank + group_offset) % owner_count * per_pair + slot_level
    got_rows, got_counts = (
        lax.all_to_all(
            to_slots(grouped, send_slot, owner_count, per_pair),
            "dp",
            split_axis=0,
            concat_axis=0,
            tiled=True,
        ),
        lax.all_to_all(
            to_slots(counts, send_slot, owner_count, per_pair),
            "dp",
            split_axis=0,
            concat_axis=0,
            tiled=True,
        ),
    )
    take_slot = (my_rank - group_offset) % owner_count * per_pair + slot_level
    own_rows = got_rows.reshape((owner_count * per_pair,) + grouped.shape[1:])[take_slot]
    own_counts = got_counts.reshape(owner_count * per_pair)[take_slot]
    cache_grouped = cache.reshape((groups, pair_rows) + cache.shape[1:])
    cache_send = (my_rank + cache_offset) % owner_count * per_pair + slot_level
    got_cache, got_flags = (
        lax.all_to_all(
            to_slots(cache_grouped, cache_send, owner_count, per_pair),
            "dp",
            split_axis=0,
            concat_axis=0,
            tiled=True,
        ),
        lax.all_to_all(
            to_slots(cache_live, cache_send, owner_count, per_pair),
            "dp",
            split_axis=0,
            concat_axis=0,
            tiled=True,
        ),
    )
    inverse = jnp.sum(
        group_index[:, None] * (cache_group[:, None] == group_index[None, :]).astype(jnp.int32),
        axis=0,
    )
    cache_slot = (my_rank - cache_offset[inverse]) % owner_count * per_pair + inverse // owner_count
    own_cache = got_cache.reshape((owner_count * per_pair,) + cache_grouped.shape[1:])[cache_slot]
    own_flags = got_flags.reshape(owner_count * per_pair)[cache_slot]
    own_cache = jnp.where(
        own_flags[:, None, None, None, None] > 0, own_cache, jnp.zeros_like(own_cache)
    )
    sequence = jnp.concatenate([own_cache, own_rows], axis=2)
    sequence = sequence.reshape((groups * pair_rows,) + sequence.shape[2:])
    live_rows = (jnp.arange(pair_rows, dtype=jnp.int32)[None, :] < own_counts[:, None]).reshape(
        groups * pair_rows
    )
    channels = spatial_weight.shape[1]
    weight_cut = temporal_weight
    conv_time = temporal_conv(
        lax.all_gather(sequence, "mp", axis=3, tiled=True), weight_cut, span_steps
    )
    square_sum = lax.psum(jnp.sum(conv_time * conv_time, axis=3), "mp")
    scaled = (
        conv_time
        * lax.rsqrt(square_sum / channels + 1e-06)[..., None]
        * norm_gain.astype(jnp.float32)
    )
    activated = jax.nn.silu(scaled).astype(jnp.bfloat16)
    weight_cut = spatial_weight
    conv_space = spatial_conv(lax.all_gather(activated, "mp", axis=3, tiled=True), weight_cut)
    latents = jnp.where(live_rows[:, None, None, None], conv_time + conv_space, 0.0).astype(
        jnp.bfloat16
    )
    return latents


CORES = 2
MIB = 1024 * 1024
Z_DEPTH = 4
Y_DEPTH = 2
C_CUTS = ((0, 4), (4, 8))
F_CUTS = ((0, 4), (4, 6), (6, 8))
CHOSEN = 6


def shift_order(size):
    far = sorted(range(1, size), key=lambda k: (abs(k - size // 2), k))
    return [0] + far


def lane_iota(shape):
    return lax.broadcasted_iota(jnp.int32, shape, len(shape) - 1)


def pick(index, table):
    out = jnp.zeros_like(index)
    for at, value in enumerate(table):
        out = jnp.where(index == at, value, out)
    return out


def position_of(shift, order):
    out = jnp.int32(0)
    for at, k in enumerate(order):
        out = jnp.where(shift == k, jnp.int32(at), out)
    return out


def pack_kernel(order, pair_rows, mark_dead, offset_ref, flag_ref, *refs):
    shifts = len(order)
    outs = refs[-shifts - (1 if mark_dead else 0) :][:shifts]
    groups = flag_ref.shape[1]
    rows = groups * pair_rows
    levels = groups // shifts
    first = 0
    if mark_dead:
        own_ref, other_ref, joined = refs[0], refs[1], refs[-1]
        tokens, _, part, _ = joined.shape
        joined[:, 0] = own_ref[...].reshape(tokens, part, rows)
        joined[:, 1] = other_ref[...].reshape(tokens, part, rows)
        flat = joined.reshape(tokens * CORES * part, rows)
        levels = levels // CORES
        first = lax.axis_index("mp") % CORES * levels
    else:
        flat = refs[0]
    slots = levels * pair_rows
    total = shifts * slots
    row = lane_iota((1, rows))
    place = pick(row // pair_rows % shifts, [position_of(offset_ref[j], order) for j in range(shifts)])
    level = row // (pair_rows * shifts) - first
    target = place * slots + level * pair_rows + row % pair_rows
    target = jnp.where((level >= 0) & (level < levels), target, -1)
    hit = lax.broadcasted_iota(jnp.int32, (total, rows), 0) == target
    spread = (
        lax.broadcasted_iota(jnp.int32, (groups, rows), 0) == lane_iota((groups, rows)) // pair_rows
    ).astype(jnp.float32)
    flag = jnp.dot(flag_ref[...].astype(jnp.float32), spread, preferred_element_type=jnp.float32)
    if mark_dead:
        live = (row % pair_rows).astype(jnp.float32) < flag
        dead = jnp.sum(jnp.where(hit & jnp.logical_not(live), 1.0, 0.0), axis=1, keepdims=True) > 0.5
    else:
        hit = hit & (flag > 0.5)
    onehot = jnp.where(hit, 1.0, 0.0).astype(jnp.bfloat16)
    step = 512
    for start in range(0, flat.shape[0], step):
        tile = lax.dot_general(
            onehot,
            flat[start : start + step],
            (((1,), (1,)), ((), ())),
            preferred_element_type=jnp.float32,
        )
        if mark_dead:
            tile = jnp.where(dead, jnp.inf, tile)
        tile = tile.astype(jnp.bfloat16)
        for at, out in enumerate(outs):
            out[:, start : start + step] = tile[at * slots : (at + 1) * slots]


def pack(order, pair_rows, mark_dead, offset, flag, *sources):
    height, rows = sources[0].shape
    shifts = len(order)
    slots = rows // shifts // len(sources)
    width = height * len(sources)
    vmem = pl.BlockSpec(memory_space=pltpu.VMEM)
    scratch = []
    if mark_dead:
        part = 64
        scratch = [pltpu.VMEM((height // part, CORES, part, rows), jnp.bfloat16)]
    return pl.pallas_call(
        functools.partial(pack_kernel, order, pair_rows, mark_dead),
        out_shape=[jax.ShapeDtypeStruct((slots, width), jnp.bfloat16)] * shifts,
        in_specs=[pl.BlockSpec(memory_space=pltpu.SMEM)] + [vmem] * (1 + len(sources)),
        out_specs=[vmem] * shifts,
        scratch_shapes=scratch,
        compiler_params=pltpu.CompilerParams(vmem_limit_bytes=16 * MIB),
        cost_estimate=pl.CostEstimate(
            flops=2 * shifts * slots * width * rows, bytes_accessed=2 * width * rows, transcendentals=0
        ),
        name="pack_dead" if mark_dead else "pack_carried",
    )(offset, flag, *sources)


def choose_kernel(order, pair_rows, count, group_offset_ref, cache_offset_ref, group_ref, *refs):
    shifts = len(order)
    near, far, near_other, far_other = (refs[i * count : (i + 1) * count] for i in range(4))
    outs = refs[4 * count :]
    core = lax.axis_index("mp") % CORES
    groups = group_ref.shape[1]
    rows = groups * pair_rows
    width = near[0].shape[1]
    slots = rows // shifts
    half_levels = groups // shifts // CORES
    column = lane_iota((1, rows))
    shift_at = column // slots
    residue = jnp.zeros_like(column)
    for j in range(shifts):
        residue = jnp.where(shift_at == position_of(cache_offset_ref[j], order), j, residue)
    cached = column % slots // pair_rows * shifts + residue
    pickers = (lax.broadcasted_iota(jnp.int32, (groups, rows), 0) == cached).astype(jnp.float32)
    group = jnp.dot(
        group_ref[...].astype(jnp.float32), pickers, preferred_element_type=jnp.float32
    )
    group = (group + 0.5).astype(jnp.int32)
    place = pick(group % shifts, [position_of(group_offset_ref[j], order) for j in range(shifts)])
    goal = group // shifts - core * half_levels
    half = rows // CORES
    target = (place * half_levels + goal) * pair_rows + column % pair_rows
    target = jnp.where((goal >= 0) & (goal < half_levels), target, -1)
    onehot = jnp.where(
        lax.broadcasted_iota(jnp.int32, (half, rows), 0) == target, 1.0, 0.0
    ).astype(jnp.bfloat16)
    step = 512
    part = 64
    piece = half // len(outs)
    for side, pair in enumerate(((near, near_other), (far, far_other))):
        for start in range(0, width, step):
            got = [
                jnp.dot(
                    onehot,
                    jnp.concatenate([ref[:, start : start + step] for ref in one], axis=0),
                    preferred_element_type=jnp.float32,
                )
                for one in pair
            ]
            mixed = jnp.concatenate(
                [one[:, at : at + part] for at in range(0, step, part) for one in got], axis=1
            ).astype(jnp.bfloat16)
            for at, out in enumerate(outs):
                lane = CORES * (side * width + start)
                out[:, lane : lane + CORES * step] = mixed[at * piece : (at + 1) * piece]


def choose(order, pair_rows, pieces, group_offset, cache_offset, group, *sources):
    width = sources[0][0].shape[1]
    rows = group.shape[1] * pair_rows
    vmem = pl.BlockSpec(memory_space=pltpu.VMEM)
    smem = pl.BlockSpec(memory_space=pltpu.SMEM)
    flat = [x for source in sources for x in source]
    out = jax.ShapeDtypeStruct((rows // CORES // pieces, 2 * CORES * width), jnp.bfloat16)
    return pl.pallas_call(
        functools.partial(choose_kernel, order, pair_rows, len(sources[0])),
        out_shape=[out] * pieces,
        in_specs=[smem, smem] + [vmem] * (1 + len(flat)),
        out_specs=[vmem] * pieces,
        compiler_params=pltpu.CompilerParams(vmem_limit_bytes=16 * MIB),
        cost_estimate=pl.CostEstimate(
            flops=4 * rows * rows * width, bytes_accessed=12 * rows * width, transcendentals=0
        ),
        name="choose_carried",
    )(group_offset, cache_offset, group, *flat)


def weights_kernel(taps, own, other, far, time_out, space_out, gain_out):
    index = lax.axis_index("mp")
    part = own.shape[1]
    height = far.shape[0] // 2
    inner = (height - 16) // taps
    side = inner // 4
    sources = ((own, 0), (other, 0), (far, 0), (far, height))
    for block, (ref, base) in enumerate(sources):
        columns = slice(block * part, (block + 1) * part)
        for tap in range(taps):
            for at in range(4):
                begin = pl.multiple_of(base + tap * inner + (index ^ at) * side, 16)
                rows = slice(tap * inner + at * side, tap * inner + (at + 1) * side)
                time_out[rows, columns] = ref[pl.ds(begin, side), :]
        gain_out[:, columns] = ref[base + taps * inner : base + height, :]
    channels = 4 * part
    for tap in range(3):
        for block in range(4):
            begin = pl.multiple_of(height + tap * channels + (index ^ block) * part, 16)
            rows = slice(tap * channels + block * part, tap * channels + (block + 1) * part)
            space_out[rows, :part] = own[pl.ds(begin, part), :]
            space_out[rows, part:] = other[pl.ds(begin, part), :]


def arrange_weights(taps, own, other, far):
    part = own.shape[1]
    height = far.shape[0] // 2
    vmem = pl.BlockSpec(memory_space=pltpu.VMEM)
    return pl.pallas_call(
        functools.partial(weights_kernel, taps),
        out_shape=[
            jax.ShapeDtypeStruct((height - 16, 4 * part), jnp.bfloat16),
            jax.ShapeDtypeStruct((own.shape[0] - height, 2 * part), jnp.bfloat16),
            jax.ShapeDtypeStruct((16, 4 * part), jnp.bfloat16),
        ],
        in_specs=[vmem] * 3,
        out_specs=[vmem] * 3,
        compiler_params=pltpu.CompilerParams(vmem_limit_bytes=12 * MIB),
        cost_estimate=pl.CostEstimate(
            flops=0, bytes_accessed=8 * own.size, transcendentals=0
        ),
        name="arrange_weights",
    )(own, other, far)


def encode_kernel(cuts, width, *refs):
    count = len(cuts[0]) + len(cuts[1])
    near, far = refs[: len(cuts[0])], refs[len(cuts[0]) : count]
    carried, time_w, space_w, gain_ref, kept, sent, seq, act, rest = refs[count:]
    rows = carried.shape[0]
    channels = time_w.shape[1]
    span = seq.shape[0]
    tokens = width * rows
    inner = near[0].shape[1] // (span * width) * 2
    side = inner // 2
    taps = time_w.shape[0] // inner
    half_width = carried.shape[1] // 2
    past = half_width // (side * width)

    def fill(step, rows_at, column, value):
        for t in range(span):
            tap = past + t - step
            if 0 <= tap < taps:
                seq[t, rows_at, tap * inner + column : tap * inner + column + side] = value

    for w in range(width):
        for step in range(past):
            lane = (step * width + w) * side
            for column, base in ((0, 0), (side, half_width)):
                value = carried[:, base + lane : base + lane + side]
                fill(step, slice(w * rows, (w + 1) * rows), column, value)
        for step in range(span):
            lane = (step * width + w) * side
            for column, sources, cut in ((0, near, cuts[0]), (side, far, cuts[1])):
                begin = w * rows
                for ref, (low, high) in zip(sources, cut):
                    value = ref[low:high, lane : lane + side]
                    fill(past + step, slice(begin, begin + high - low), column, value)
                    begin += high - low
    first = jnp.concatenate(
        [ref[a:b, :side].astype(jnp.float32)[:, :1] for ref, (a, b) in zip(near, cuts[0])], axis=0
    )
    live = (first < jnp.inf)[None]
    gain = gain_ref[0:1, :].astype(jnp.float32)
    kept_columns = space_w.shape[1]
    edge = jnp.zeros((rows, channels), jnp.bfloat16)
    for t in range(span):
        act[t, 0:rows, :channels] = edge
        act[t, tokens - rows :, 2 * channels :] = edge
    tile = 256
    for t in range(span):
        for start in range(0, tokens, tile):
            conv = jnp.dot(
                seq[t, start : start + tile], time_w[...], preferred_element_type=jnp.float32
            )
            square = jnp.sum(conv * conv, axis=1, keepdims=True)
            rest[t, start : start + tile] = conv[:, :kept_columns]
            scaled = conv * lax.rsqrt(square / channels + 1e-06) * gain
            value = jax.nn.silu(scaled).astype(jnp.bfloat16)
            act[t, start : start + tile, channels : 2 * channels] = value
            if start + tile < tokens:
                act[t, start + rows : start + rows + tile, :channels] = value
            else:
                act[t, start + rows : tokens, :channels] = value[: tile - rows]
            if start > 0:
                act[t, start - rows : start - rows + tile, 2 * channels :] = value
            else:
                act[t, : tile - rows, 2 * channels :] = value[rows:]
    tile = 256
    for t in range(span):
        for start in range(0, tokens, tile):
            total = rest[t, start : start + tile] + jnp.dot(
                act[t, start : start + tile], space_w[...], preferred_element_type=jnp.float32
            )
            wide = tile // rows
            total = jnp.where(live, total.reshape(wide, rows, kept_columns), 0.0)
            total = jnp.swapaxes(total, 0, 1).astype(jnp.bfloat16)
            place = slice(start // rows, start // rows + wide)
            kept[:, t, place] = total[:, :, : kept_columns // 2]
            sent[:, t, place] = total[:, :, kept_columns // 2 :]


def encode(width, span, near, far, carried, time_w, space_w, gain):
    cuts = [[(a, b) for _, a, b in pieces] for pieces in (near, far)]
    arrays = [x for pieces in (near, far) for x, _, _ in pieces]
    rows, lanes = carried.shape[0], arrays[0].shape[1]
    channels = time_w.shape[1]
    vmem = pl.BlockSpec(memory_space=pltpu.VMEM)
    part = space_w.shape[1] // 2
    out = jax.ShapeDtypeStruct((rows, span, width, part), jnp.bfloat16)
    tokens = rows * span * width
    return pl.pallas_call(
        functools.partial(encode_kernel, cuts, width),
        out_shape=[out, out],
        in_specs=[vmem] * (len(arrays) + 4),
        out_specs=[vmem] * 2,
        scratch_shapes=[
            pltpu.VMEM((span, width * rows, time_w.shape[0]), jnp.bfloat16),
            pltpu.VMEM((span, width * rows, space_w.shape[0]), jnp.bfloat16),
            pltpu.VMEM((span, width * rows, space_w.shape[1]), jnp.float32),
        ],
        compiler_params=pltpu.CompilerParams(vmem_limit_bytes=24 * MIB),
        cost_estimate=pl.CostEstimate(
            flops=2 * tokens * (time_w.size + space_w.size),
            bytes_accessed=2 * (time_w.size + space_w.size) + 16 * rows * lanes,
            transcendentals=tokens * channels,
        ),
        name="encode_rows",
    )(*arrays, carried, time_w, space_w, gain)


def place_kernel(order, chunks, offset_ref, *refs):
    blocks, out = refs[:-1], refs[-1]
    core = lax.axis_index("mp") % CORES
    shifts = len(order)
    for chunk in range(len(chunks)):
        for u, shift in enumerate(chunks[chunk]):
            residue = jnp.int32(0)
            for j in range(shifts):
                residue = jnp.where(offset_ref[j] == shift, jnp.int32(j), residue)
            for kind in range(2):
                out[core ^ kind, :, residue] = blocks[kind * len(chunks) + chunk][u]


def place(order, chunks, pair_rows, offset, kept, got):
    count = len(chunks[0])
    rows, span, width, part = kept[0].shape
    half_levels = rows // count // pair_rows
    tail = (pair_rows, span, width, part)
    blocks = [a.reshape((count, half_levels) + tail) for a in kept + got]
    vmem = pl.BlockSpec(memory_space=pltpu.VMEM)
    out = pl.pallas_call(
        functools.partial(place_kernel, order, chunks),
        out_shape=jax.ShapeDtypeStruct((CORES, half_levels, len(order)) + tail, jnp.bfloat16),
        in_specs=[pl.BlockSpec(memory_space=pltpu.SMEM)] + [vmem] * len(blocks),
        out_specs=vmem,
        compiler_params=pltpu.CompilerParams(vmem_limit_bytes=12 * MIB),
        cost_estimate=pl.CostEstimate(
            flops=0, bytes_accessed=4 * sum(a.size for a in blocks), transcendentals=0
        ),
        name="place_rows",
    )(offset, *blocks)
    return out.reshape((-1, span, width, part))


def routed_local(
    frames,
    cache,
    group_offset,
    cache_offset,
    cache_group,
    group_rows,
    cache_live,
    temporal_weight,
    spatial_weight,
    norm_gain,
):
    shifts = lax.axis_size("dp")
    parts = lax.axis_size("mp")
    groups = group_offset.shape[0]
    rows, span, width, part_in = frames.shape
    pair_rows = rows // groups
    taps = temporal_weight.shape[0]
    order = shift_order(shifts)
    per_chunk = 2
    chunks = [order[i : i + per_chunk] for i in range(0, shifts, per_chunk)]

    def after(x, *cells):
        got = lax.optimization_barrier((x, *[cell[0] for cell in cells]))
        for cell, value in zip(cells, got[1:]):
            cell[0] = value
        return got[0]

    lanes = {}

    def move(x, lane, depth, axis, pairs, cells=()):
        line = lanes.setdefault(lane, [])
        cells = list(cells) + (line[-depth : len(line) - depth + 1] if len(line) >= depth else [])
        if cells:
            x = after(x, *cells)
        line.append([lax.ppermute(x, axis, pairs)])
        return line[-1]

    def flip(x, mask, lane, depth, *cells):
        return move(x, lane, depth, "mp", [(i, i ^ mask) for i in range(parts)], cells)

    def send(x, shift, *cells):
        if shift == 0:
            return [x]
        return move(x, "z", Z_DEPTH, "dp", [(i, (i + shift) % shifts) for i in range(shifts)], cells)

    def join(pieces):
        if len(pieces) == 1:
            return pieces[0][0]
        return jnp.concatenate([x[0] for x in pieces], axis=0)

    cache_rows = cache.transpose((1, 2, 3, 0)).reshape((-1, rows))
    frame_rows = frames.transpose((1, 2, 3, 0)).reshape((-1, rows))
    frame_swapped = flip(frame_rows, 1, "core", 3)
    cache_packed = pack(
        order, pair_rows, False, cache_offset, cache_live.reshape((1, groups)), cache_rows
    )
    frame_packed = [
        [x]
        for x in pack(
            order,
            pair_rows,
            True,
            group_offset,
            group_rows.reshape((1, groups)),
            frame_rows,
            frame_swapped[0],
        )
    ]
    part = norm_gain.shape[0]
    time_rows = taps * temporal_weight.shape[1] + 16
    own_w = jnp.concatenate(
        [
            temporal_weight.reshape((-1, part)),
            jnp.broadcast_to(norm_gain[None], (16, part)),
            spatial_weight.reshape((-1, part)),
        ],
        axis=0,
    )
    other_w = flip(own_w, 1, "core", 3)
    far_w = flip(
        jnp.concatenate([own_w[:time_rows], other_w[0][:time_rows]], axis=0), 2, "y", 2
    )
    arranged = [[x] for x in arrange_weights(taps, own_w, other_w[0], far_w[0])]
    wait = {1: [frame_packed[0]], 2: [other_w], 5: [arranged[0]]}
    cache_near = [send(x, k, *wait.get(i, [])) for i, (x, k) in enumerate(zip(cache_packed, order))]
    near, far = [], []
    for a, b in C_CUTS:
        near.append([join(cache_near[a:b])])
        far.append(flip(near[-1][0], 2, "y", Y_DEPTH))
    near_other = [flip(x[0], 1, "core", 3) for x in near]
    far_other = [flip(x[0], 1, "core", 3) for x in far]
    carried = [
        [x]
        for x in choose(
            order,
            pair_rows,
            len(chunks),
            group_offset,
            cache_offset,
            cache_group.reshape((1, groups)),
            *[[x[0] for x in source] for source in (near, far, near_other, far_other)],
        )
    ]
    wait = {CHOSEN: [carried[0]]}
    frame_near = [
        send(x[0], k, *wait.get(i, [])) for i, (x, k) in enumerate(zip(frame_packed, order))
    ]

    def forward(pieces):
        return flip(join(pieces), 2, "y", Y_DEPTH)

    frame_far = {}
    for a, b in F_CUTS:
        cell = forward(frame_near[a:b])
        frame_far.update({at: (cell, at - a) for at in range(a, b)})
    slots = frame_near[0][0].shape[0]
    kept, got = [], []
    for index in range(len(chunks)):
        picked = range(index * per_chunk, (index + 1) * per_chunk)
        ours = [(frame_near[at][0], 0, slots) for at in picked]
        theirs = [
            (frame_far[at][0][0], frame_far[at][1] * slots, (frame_far[at][1] + 1) * slots)
            for at in picked
        ]
        keep, give = encode(
            width, span, ours, theirs, carried[index][0], *[x[0] for x in arranged]
        )
        kept.append(keep)
        got.append(flip(give, 1, "core", 3)[0])
    return place(order, chunks, pair_rows, group_offset, kept, got)


def fits(mesh, frames, group_offset, temporal_weight):
    shifts, parts = mesh.shape["dp"], mesh.shape["mp"]
    groups = group_offset.shape[0]
    rows = frames.shape[0] // shifts
    if parts != 4 or frames.shape[3] != 64 * parts or groups > 256:
        return False
    if temporal_weight.shape[2] != 128 * parts or shifts % 2:
        return False
    if groups % (shifts * CORES):
        return False
    return rows // shifts // CORES % 16 == 0 and rows % 128 == 0


def solution(mesh):
    in_specs = (
        P("dp", None, None, "mp"),
        P("dp", None, None, "mp"),
        P(),
        P(),
        P(),
        P("dp", None),
        P("dp"),
        P(None, None, "mp"),
        P(None, None, "mp"),
        P("mp"),
    )
    out_specs = P("dp", None, None, "mp")

    def call(*args):
        body = routed_local if fits(mesh, args[0], args[2], args[7]) else plain_local
        return jax.shard_map(
            body, mesh=mesh, in_specs=in_specs, out_specs=out_specs, check_vma=False
        )(*args)

    return call
```

time: 144 us -> 99.3 us (0.69)
  the two profiles are of different devices: /device:TPU:11 before, /device:TPU:0 now
where the time goes in v2:
time: 99.3 us; the launch traced here: 99.1 us
  waiting for transfers between devices  45.6 us (46%)
  starting transfers between devices  36.6 us (37%)
  Pallas kernels  14.5 us (15%)
  other arithmetic  1.22 us (1%)
    ppermute x30, waiting for transfers between devices, move(): line.append([lax.ppermute(x, axis, pairs)])  45.6 us
    ppermute x30, starting transfers between devices, move(): line.append([lax.ppermute(x, axis, pairs)])  36.6 us
    pallas_call x4, Pallas kernels, encode(): pl.pallas_call(functools.partial(encode_kernel, cuts, width), out_shape=[...  8.08 us
    pallas_call x2, Pallas kernels, pack(): pl.pallas_call(functools.partial(pack_kernel, order, pair_rows, mark_dead...  2.35 us
    pallas_call x1, Pallas kernels, place(): pl.pallas_call(functools.partial(place_kernel, order, chunks), out_shape=...  2.01 us
  transfers between devices with their start and end apart: 30, of which 11 were waited for; matrix products, arithmetic and copies ran while one was open for 0% of the time, Pallas kernels for 13%

profile of v2, /device:TPU:0, one launch (start us, length us, event | category | flops | bytes accessed | tf_op | source)
XLA Modules:
  0.0 99.1 jit_solution(15138819033200330132)
XLA Ops:
  3.6 3.1 %collective-permute-start.1 = (bf16[32,2048]{1,0:T(8,128)(2,1)S(1)}, bf16[32,2048]{1,0:T(8,128)(2,1)S(1)}, u32[]{:S(2)}, u32[]{:S(2)}) collective-permute-start(bf16[32,2048]{1,0:T(8,128)(2,1)S(1)} %get-tuple-element.74), channel_id=1, source_target_pairs={{0,8},{4,12},{8,16},{12,20},{16,24},{20,28},{24,0},{28,4},{1,9},{5... | collective-permute-start | bytes 393224 | tf_op jit(solution)/shard_map/ppermute | solution.py:532
  6.7 3.5 %collective-permute-start.7 = (bf16[32,2048]{1,0:T(8,128)(2,1)S(1)}, bf16[32,2048]{1,0:T(8,128)(2,1)S(1)}, u32[]{:S(2)}, u32[]{:S(2)}) collective-permute-start(bf16[32,2048]{1,0:T(8,128)(2,1)S(1)} %get-tuple-element.88), channel_id=1, source_target_pairs={{0,20},{4,24},{8,28},{12,0},{16,4},{20,8},{24,12},{28,16},{1,21},{... | collective-permute-start | bytes 393224 | tf_op jit(solution)/shard_map/ppermute | solution.py:532
  11.9 3.7 %collective-permute-done.7 = bf16[32,2048]{1,0:T(8,128)(2,1)S(1)} collective-permute-done((bf16[32,2048]{1,0:T(8,128)(2,1)S(1)}, bf16[32,2048]{1,0:T(8,128)(2,1)S(1)}, u32[]{:S(2)}, u32[]{:S(2)}) %collective-permute-start.7) | collective-permute-done | bytes 131104 | tf_op jit(solution)/shard_map/ppermute | solution.py:532
  15.6 5.0 %collective-permute-start.10 = (bf16[32,2048]{1,0:T(8,128)(2,1)S(1)}, bf16[32,2048]{1,0:T(8,128)(2,1)S(1)}, u32[]{:S(2)}, u32[]{:S(2)}) collective-permute-start(bf16[32,2048]{1,0:T(8,128)(2,1)S(1)} %get-tuple-element.92), channel_id=1, source_target_pairs={{0,28},{4,0},{8,4},{12,8},{16,12},{20,16},{24,20},{28,24},{1,29},{... | collective-permute-start | bytes 393224 | tf_op jit(solution)/shard_map/ppermute | solution.py:532
  22.5 10.6 %collective-permute-done.6 = bf16[32,2048]{1,0:T(8,128)(2,1)S(1)} collective-permute-done((bf16[32,2048]{1,0:T(8,128)(2,1)S(1)}, bf16[32,2048]{1,0:T(8,128)(2,1)S(1)}, u32[]{:S(2)}, u32[]{:S(2)}) %collective-permute-start.6) | collective-permute-done | bytes 131104 | tf_op jit(solution)/shard_map/ppermute | solution.py:532
  33.5 1.7 %collective-permute-start.8 = (bf16[32,2048]{1,0:T(8,128)(2,1)S(1)}, bf16[32,2048]{1,0:T(8,128)(2,1)S(1)}, u32[]{:S(2)}, u32[]{:S(2)}) collective-permute-start(bf16[32,2048]{1,0:T(8,128)(2,1)S(1)} %get-tuple-element.90), channel_id=1, source_target_pairs={{0,24},{4,28},{8,0},{12,4},{16,8},{20,12},{24,16},{28,20},{1,25},{... | collective-permute-start | bytes 393224 | tf_op jit(solution)/shard_map/ppermute | solution.py:532
  35.3 1.6 %collective-permute-start.11 = (bf16[128,2048]{1,0:T(8,128)(2,1)S(1)}, bf16[128,2048]{1,0:T(8,128)(2,1)S(1)}, u32[]{:S(2)}, u32[]{:S(2)}) collective-permute-start(bf16[128,2048]{1,0:T(8,128)(2,1)S(1)} %constant_dynamic-update-slice_fusion.refs_0_), channel_id=1, source_target_pairs={{0,2},{1,3},{2,0},{3,1},{4,6},{5,7},{6,4},{7,5},{8,10},{9,11},{10,... | collective-permute-start | bytes 1572872 | tf_op jit(solution)/shard_map/ppermute | solution.py:532
  36.9 1.6 %collective-permute-done.8 = bf16[32,2048]{1,0:T(8,128)(2,1)S(1)} collective-permute-done((bf16[32,2048]{1,0:T(8,128)(2,1)S(1)}, bf16[32,2048]{1,0:T(8,128)(2,1)S(1)}, u32[]{:S(2)}, u32[]{:S(2)}) %collective-permute-start.8) | collective-permute-done | bytes 131104 | tf_op jit(solution)/shard_map/ppermute | solution.py:532
  38.5 3.0 %collective-permute-done.9 = bf16[32,2048]{1,0:T(8,128)(2,1)S(1)} collective-permute-done((bf16[32,2048]{1,0:T(8,128)(2,1)S(1)}, bf16[32,2048]{1,0:T(8,128)(2,1)S(1)}, u32[]{:S(2)}, u32[]{:S(2)}) %collective-permute-start.9) | collective-permute-done | bytes 131104 | tf_op jit(solution)/shard_map/ppermute | solution.py:532
  41.5 1.6 %collective-permute-start.12 = (bf16[128,2048]{1,0:T(8,128)(2,1)S(1)}, bf16[128,2048]{1,0:T(8,128)(2,1)S(1)}, u32[]{:S(2)}, u32[]{:S(2)}) collective-permute-start(bf16[128,2048]{1,0:T(8,128)(2,1)S(1)} %constant_dynamic-update-slice_fusion.4.refs_1_), channel_id=1, source_target_pairs={{0,2},{1,3},{2,0},{3,1},{4,6},{5,7},{6,4},{7,5},{8,10},{9,11},{10,... | collective-permute-start | bytes 1572872 | tf_op jit(solution)/shard_map/ppermute | solution.py:532
  43.1 4.3 %collective-permute-start.19 = (bf16[16,4096]{1,0:T(8,128)(2,1)S(1)}, bf16[16,4096]{1,0:T(8,128)(2,1)S(1)}, u32[]{:S(2)}, u32[]{:S(2)}) collective-permute-start(bf16[16,4096]{1,0:T(8,128)(2,1)S(1)} %get-tuple-element.103), channel_id=1, source_target_pairs={{0,20},{4,24},{8,28},{12,0},{16,4},{20,8},{24,12},{28,16},{1,21},{... | collective-permute-start | bytes 393224 | tf_op jit(solution)/shard_map/ppermute | solution.py:532
  47.5 3.7 %collective-permute-done.2.refs_1_ = bf16[16,4096]{1,0:T(8,128)(2,1)S(1)} collective-permute-done((bf16[16,4096]{1,0:T(8,128)(2,1)S(1)}, bf16[16,4096]{1,0:T(8,128)(2,1)S(1)}, u32[]{:S(2)}, u32[]{:S(2)}) %collective-permute-start.2) | collective-permute-done | bytes 131104 | tf_op jit(solution)/shard_map/ppermute | solution.py:532
  51.5 3.5 %collective-permute-start.23 = (bf16[16,4096]{1,0:T(8,128)(2,1)S(1)}, bf16[16,4096]{1,0:T(8,128)(2,1)S(1)}, u32[]{:S(2)}, u32[]{:S(2)}) collective-permute-start(bf16[16,4096]{1,0:T(8,128)(2,1)S(1)} %get-tuple-element.118), channel_id=1, source_target_pairs={{0,24},{4,28},{8,0},{12,4},{16,8},{20,12},{24,16},{28,20},{1,25},{... | collective-permute-start | bytes 393224 | tf_op jit(solution)/shard_map/ppermute | solution.py:532
  55.0 5.9 %collective-permute-done.12.refs_3_ = bf16[128,2048]{1,0:T(8,128)(2,1)S(1)} collective-permute-done((bf16[128,2048]{1,0:T(8,128)(2,1)S(1)}, bf16[128,2048]{1,0:T(8,128)(2,1)S(1)}, u32[]{:S(2)}, u32[]{:S(2)}) %collective-permute-start.12) | collective-permute-done | bytes 524320 | tf_op jit(solution)/shard_map/ppermute | solution.py:532
  61.4 3.1 %collective-permute-start.20 = (bf16[16,4096]{1,0:T(8,128)(2,1)S(1)}, bf16[16,4096]{1,0:T(8,128)(2,1)S(1)}, u32[]{:S(2)}, u32[]{:S(2)}) collective-permute-start(bf16[16,4096]{1,0:T(8,128)(2,1)S(1)} %get-tuple-element.104), channel_id=1, source_target_pairs={{0,28},{4,0},{8,4},{12,8},{16,12},{20,16},{24,20},{28,24},{1,29},{... | collective-permute-start | bytes 393224 | tf_op jit(solution)/shard_map/ppermute | solution.py:532
  66.1 1.8 %choose_carried.1 = (bf16[32,8192]{1,0:T(8,128)(2,1)S(1)}, bf16[32,8192]{1,0:T(8,128)(2,1)S(1)}, bf16[32,8192]{1,0:T(8,128)(2,1)S(1)}, bf16[32,8192]{1,0:T(8,128)(2,1)S(1)}) custom-call(s32[128]{0:T(128)S(1)} %copy-done.2, s32[128]{0:T(128)S(1)} %copy-done.3, s32[1,128]{1,0:T(1,128)S(1)} %bitcast.31, ...), custom_call_target="tpu_custom_call" | custom-call | flops 536870912 | bytes 6291456 | tf_op jit(solution)/shard_map/choose_carried/pallas_call | solution.py:299
  67.9 6.3 %collective-permute-done.17.refs_0_ = bf16[16,4096]{1,0:T(8,128)(2,1)S(1)} collective-permute-done((bf16[16,4096]{1,0:T(8,128)(2,1)S(1)}, bf16[16,4096]{1,0:T(8,128)(2,1)S(1)}, u32[]{:S(2)}, u32[]{:S(2)}) %collective-permute-start.17) | collective-permute-done | bytes 131104 | tf_op jit(solution)/shard_map/ppermute | solution.py:532
  75.9 2.0 %encode_rows.6 = (bf16[32,2,16,128]{3,2,1,0:T(8,128)(2,1)S(1)}, bf16[32,2,16,128]{3,2,1,0:T(8,128)(2,1)S(1)}) custom-call(bf16[16,4096]{1,0:T(8,128)(2,1)S(1)} %collective-permute-done.22.refs_0_, bf16[16,4096]{1,0:T(8,128)(2,1)S(1)} %collective-permute-done.23.refs_1_, bf16[32,4096]{1,0:T(8,128)(2,1)S(1)} %collective-permute-done.24.refs_2_.refs_3_, ...), custom_call_target="tpu_custom_call" | custom-call | flops 1610612736 | bytes 3670016 | tf_op jit(solution)/shard_map/encode_rows/pallas_call | solution.py:443
  78.0 3.9 %collective-permute-done.18.refs_0_ = bf16[16,4096]{1,0:T(8,128)(2,1)S(1)} collective-permute-done((bf16[16,4096]{1,0:T(8,128)(2,1)S(1)}, bf16[16,4096]{1,0:T(8,128)(2,1)S(1)}, u32[]{:S(2)}, u32[]{:S(2)}) %collective-permute-start.18) | collective-permute-done | bytes 131104 | tf_op jit(solution)/shard_map/ppermute | solution.py:532
  82.0 5.1 %collective-permute-done.21.refs_2_.refs_3_ = bf16[64,4096]{1,0:T(8,128)(2,1)S(1)} collective-permute-done((bf16[64,4096]{1,0:T(8,128)(2,1)S(1)}, bf16[64,4096]{1,0:T(8,128)(2,1)S(1)}, u32[]{:S(2)}, u32[]{:S(2)}) %collective-permute-start.21) | collective-permute-done | bytes 524320 | tf_op jit(solution)/shard_map/ppermute | solution.py:532
  88.6 2.0 %encode_rows.4 = (bf16[32,2,16,128]{3,2,1,0:T(8,128)(2,1)S(1)}, bf16[32,2,16,128]{3,2,1,0:T(8,128)(2,1)S(1)}) custom-call(bf16[16,4096]{1,0:T(8,128)(2,1)S(1)} %get-tuple-element.71.refs_0_, bf16[16,4096]{1,0:T(8,128)(2,1)S(1)} %collective-permute-done.2.refs_1_, bf16[64,4096]{1,0:T(8,128)(2,1)S(1)} %collective-permute-done.21.refs_2_.refs_3_, ...), custom_call_target="tpu_custom_call" | custom-call | flops 1610612736 | bytes 3670016 | tf_op jit(solution)/shard_map/encode_rows/pallas_call | solution.py:443
  90.7 2.0 %encode_rows.5 = (bf16[32,2,16,128]{3,2,1,0:T(8,128)(2,1)S(1)}, bf16[32,2,16,128]{3,2,1,0:T(8,128)(2,1)S(1)}) custom-call(bf16[16,4096]{1,0:T(8,128)(2,1)S(1)} %collective-permute-done.17.refs_0_, bf16[16,4096]{1,0:T(8,128)(2,1)S(1)} %collective-permute-done.19.refs_1_, bf16[64,4096]{1,0:T(8,128)(2,1)S(1)} %collective-permute-done.21.refs_2_.refs_3_, ...), custom_call_target="tpu_custom_call" | custom-call | flops 1610612736 | bytes 3670016 | tf_op jit(solution)/shard_map/encode_rows/pallas_call | solution.py:443
  93.5 2.0 %encode_rows.7 = (bf16[32,2,16,128]{3,2,1,0:T(8,128)(2,1)S(1)}, bf16[32,2,16,128]{3,2,1,0:T(8,128)(2,1)S(1)}) custom-call(bf16[16,4096]{1,0:T(8,128)(2,1)S(1)} %collective-permute-done.18.refs_0_, bf16[16,4096]{1,0:T(8,128)(2,1)S(1)} %collective-permute-done.20.refs_1_, bf16[32,4096]{1,0:T(8,128)(2,1)S(1)} %collective-permute-done.25.refs_2_.refs_3_, ...), custom_call_target="tpu_custom_call" | custom-call | flops 1610612736 | bytes 3670016 | tf_op jit(solution)/shard_map/encode_rows/pallas_call | solution.py:443
  97.1 2.0 %place_rows.1 = bf16[2,8,8,2,2,16,128]{6,5,4,3,2,1,0:T(8,128)(2,1)} custom-call(s32[128]{0:T(128)S(1)} %copy-done.2, bf16[2,8,2,2,16,128]{5,4,3,2,1,0:T(8,128)(2,1)S(1)} %bitcast.24, bf16[2,8,2,2,16,128]{5,4,3,2,1,0:T(8,128)(2,1)S(1)} %bitcast.26, bf16[2,8,2,2,16,128]{5,4,3,2,1,0:T(8,128)(2,1)S(1)} %bitcast.22, bf16[2,8,2,2,16,128]{5,4,3,2,1,0:T(8,128)(2,1)S(1)} %bitcast.28, ...), custom_call_target="tpu_custom_call" | custom-call | bytes 4194304 | tf_op jit(solution)/shard_map/place_rows/pallas_call | solution.py:483
  (76 shorter events, 15.6 us)
Async XLA Ops:
  1.9 8.3 %collective-permute-start.3 = (bf16[2320,128]{1,0:T(8,128)(2,1)S(1)}, bf16[2320,128]{1,0:T(8,128)(2,1)S(1)}, u32[]{:S(2)}, u32[]{:S(2)}) collective-permute-start(bf16[2320,128]{1,0:T(8,128)(2,1)S(1)} %pad_maximum_fusion.own), channel_id=1, source_target_pairs={{0,1},{1,0},{2,3},{3,2},{4,5},{5,4},{6,7},{7,6},{8,9},{9,8},{10,11... | collective-permute-start | bytes 1781768 | tf_op jit(solution)/shard_map/ppermute | solution.py:532
  2.4 18.2 %collective-permute-start = (bf16[2048,256]{1,0:T(8,128)(2,1)}, bf16[2048,256]{1,0:T(8,128)(2,1)S(1)}, u32[]{:S(2)}, u32[]{:S(2)}) collective-permute-start(bf16[2048,256]{1,0:T(8,128)(2,1)} %bitcast.20), channel_id=1, source_target_pairs={{0,1},{1,0},{2,3},{3,2},{4,5},{5,4},{6,7},{7,6},{8,9},{9,8},{10,11... | collective-permute-start | bytes 3145736 | tf_op jit(solution)/shard_map/ppermute | solution.py:532
  3.6 18.9 %collective-permute-start.1 = (bf16[32,2048]{1,0:T(8,128)(2,1)S(1)}, bf16[32,2048]{1,0:T(8,128)(2,1)S(1)}, u32[]{:S(2)}, u32[]{:S(2)}) collective-permute-start(bf16[32,2048]{1,0:T(8,128)(2,1)S(1)} %get-tuple-element.74), channel_id=1, source_target_pairs={{0,8},{4,12},{8,16},{12,20},{16,24},{20,28},{24,0},{28,4},{1,9},{5... | collective-permute-start | bytes 393224 | tf_op jit(solution)/shard_map/ppermute | solution.py:532
  6.7 8.9 %collective-permute-start.7 = (bf16[32,2048]{1,0:T(8,128)(2,1)S(1)}, bf16[32,2048]{1,0:T(8,128)(2,1)S(1)}, u32[]{:S(2)}, u32[]{:S(2)}) collective-permute-start(bf16[32,2048]{1,0:T(8,128)(2,1)S(1)} %get-tuple-element.88), channel_id=1, source_target_pairs={{0,20},{4,24},{8,28},{12,0},{16,4},{20,8},{24,12},{28,16},{1,21},{... | collective-permute-start | bytes 393224 | tf_op jit(solution)/shard_map/ppermute | solution.py:532
  10.3 22.9 %collective-permute-start.4 = (bf16[1568,128]{1,0:T(8,128)(2,1)S(1)}, bf16[1568,128]{1,0:T(8,128)(2,1)S(1)}, u32[]{:S(2)}, u32[]{:S(2)}) collective-permute-start(bf16[1568,128]{1,0:T(8,128)(2,1)S(1)} %pad_maximum_fusion.2), channel_id=1, source_target_pairs={{0,2},{1,3},{2,0},{3,1},{4,6},{5,7},{6,4},{7,5},{8,10},{9,11},{10,... | collective-permute-start | bytes 1204232 | tf_op jit(solution)/shard_map/ppermute | solution.py:532
  15.6 25.9 %collective-permute-start.10 = (bf16[32,2048]{1,0:T(8,128)(2,1)S(1)}, bf16[32,2048]{1,0:T(8,128)(2,1)S(1)}, u32[]{:S(2)}, u32[]{:S(2)}) collective-permute-start(bf16[32,2048]{1,0:T(8,128)(2,1)S(1)} %get-tuple-element.92), channel_id=1, source_target_pairs={{0,28},{4,0},{8,4},{12,8},{16,12},{20,16},{24,20},{28,24},{1,29},{... | collective-permute-start | bytes 393224 | tf_op jit(solution)/shard_map/ppermute | solution.py:532
  20.6 12.5 %collective-permute-start.6 = (bf16[32,2048]{1,0:T(8,128)(2,1)S(1)}, bf16[32,2048]{1,0:T(8,128)(2,1)S(1)}, u32[]{:S(2)}, u32[]{:S(2)}) collective-permute-start(bf16[32,2048]{1,0:T(8,128)(2,1)S(1)} %get-tuple-element.85), channel_id=1, source_target_pairs={{0,12},{4,16},{8,20},{12,24},{16,28},{20,0},{24,4},{28,8},{1,13},{... | collective-permute-start | bytes 393224 | tf_op jit(solution)/shard_map/ppermute | solution.py:532
  21.9 11.6 %collective-permute-start.5 = (bf16[32,2048]{1,0:T(8,128)(2,1)S(1)}, bf16[32,2048]{1,0:T(8,128)(2,1)S(1)}, u32[]{:S(2)}, u32[]{:S(2)}) collective-permute-start(bf16[32,2048]{1,0:T(8,128)(2,1)S(1)} %get-tuple-element.81), channel_id=1, source_target_pairs={{0,16},{4,20},{8,24},{12,28},{16,0},{20,4},{24,8},{28,12},{1,17},{... | collective-permute-start | bytes 393224 | tf_op jit(solution)/shard_map/ppermute | solution.py:532
  33.1 8.4 %collective-permute-start.9 = (bf16[32,2048]{1,0:T(8,128)(2,1)S(1)}, bf16[32,2048]{1,0:T(8,128)(2,1)S(1)}, u32[]{:S(2)}, u32[]{:S(2)}) collective-permute-start(bf16[32,2048]{1,0:T(8,128)(2,1)S(1)} %get-tuple-element.91), channel_id=1, source_target_pairs={{0,4},{4,8},{8,12},{12,16},{16,20},{20,24},{24,28},{28,0},{1,5},{5... | collective-permute-start | bytes 393224 | tf_op jit(solution)/shard_map/ppermute | solution.py:532
  35.2 19.8 %collective-permute-start.13 = (bf16[128,2048]{1,0:T(8,128)(2,1)S(1)}, bf16[128,2048]{1,0:T(8,128)(2,1)S(1)}, u32[]{:S(2)}, u32[]{:S(2)}) collective-permute-start(bf16[128,2048]{1,0:T(8,128)(2,1)S(1)} %constant_dynamic-update-slice_fusion.refs_0_), channel_id=1, source_target_pairs={{0,1},{1,0},{2,3},{3,2},{4,5},{5,4},{6,7},{7,6},{8,9},{9,8},{10,11... | collective-permute-start | bytes 1572872 | tf_op jit(solution)/shard_map/ppermute | solution.py:532
  35.3 16.2 %collective-permute-start.11 = (bf16[128,2048]{1,0:T(8,128)(2,1)S(1)}, bf16[128,2048]{1,0:T(8,128)(2,1)S(1)}, u32[]{:S(2)}, u32[]{:S(2)}) collective-permute-start(bf16[128,2048]{1,0:T(8,128)(2,1)S(1)} %constant_dynamic-update-slice_fusion.refs_0_), channel_id=1, source_target_pairs={{0,2},{1,3},{2,0},{3,1},{4,6},{5,7},{6,4},{7,5},{8,10},{9,11},{10,... | collective-permute-start | bytes 1572872 | tf_op jit(solution)/shard_map/ppermute | solution.py:532
  41.5 19.3 %collective-permute-start.12 = (bf16[128,2048]{1,0:T(8,128)(2,1)S(1)}, bf16[128,2048]{1,0:T(8,128)(2,1)S(1)}, u32[]{:S(2)}, u32[]{:S(2)}) collective-permute-start(bf16[128,2048]{1,0:T(8,128)(2,1)S(1)} %constant_dynamic-update-slice_fusion.4.refs_1_), channel_id=1, source_target_pairs={{0,2},{1,3},{2,0},{3,1},{4,6},{5,7},{6,4},{7,5},{8,10},{9,11},{10,... | collective-permute-start | bytes 1572872 | tf_op jit(solution)/shard_map/ppermute | solution.py:532
  43.1 8.0 %collective-permute-start.2 = (bf16[16,4096]{1,0:T(8,128)(2,1)S(1)}, bf16[16,4096]{1,0:T(8,128)(2,1)S(1)}, u32[]{:S(2)}, u32[]{:S(2)}) collective-permute-start(bf16[16,4096]{1,0:T(8,128)(2,1)S(1)} %get-tuple-element.75), channel_id=1, source_target_pairs={{0,16},{4,20},{8,24},{12,28},{16,0},{20,4},{24,8},{28,12},{1,17},{... | collective-permute-start | bytes 393224 | tf_op jit(solution)/shard_map/ppermute | solution.py:532
  43.1 17.7 %collective-permute-start.19 = (bf16[16,4096]{1,0:T(8,128)(2,1)S(1)}, bf16[16,4096]{1,0:T(8,128)(2,1)S(1)}, u32[]{:S(2)}, u32[]{:S(2)}) collective-permute-start(bf16[16,4096]{1,0:T(8,128)(2,1)S(1)} %get-tuple-element.103), channel_id=1, source_target_pairs={{0,20},{4,24},{8,28},{12,0},{16,4},{20,8},{24,12},{28,16},{1,21},{... | collective-permute-start | bytes 393224 | tf_op jit(solution)/shard_map/ppermute | solution.py:532
  51.2 10.2 %collective-permute-start.22 = (bf16[16,4096]{1,0:T(8,128)(2,1)S(1)}, bf16[16,4096]{1,0:T(8,128)(2,1)S(1)}, u32[]{:S(2)}, u32[]{:S(2)}) collective-permute-start(bf16[16,4096]{1,0:T(8,128)(2,1)S(1)} %get-tuple-element.117), channel_id=1, source_target_pairs={{0,8},{4,12},{8,16},{12,20},{16,24},{20,28},{24,0},{28,4},{1,9},{5... | collective-permute-start | bytes 393224 | tf_op jit(solution)/shard_map/ppermute | solution.py:532
  51.5 13.0 %collective-permute-start.23 = (bf16[16,4096]{1,0:T(8,128)(2,1)S(1)}, bf16[16,4096]{1,0:T(8,128)(2,1)S(1)}, u32[]{:S(2)}, u32[]{:S(2)}) collective-permute-start(bf16[16,4096]{1,0:T(8,128)(2,1)S(1)} %get-tuple-element.118), channel_id=1, source_target_pairs={{0,24},{4,28},{8,0},{12,4},{16,8},{20,12},{24,16},{28,20},{1,25},{... | collective-permute-start | bytes 393224 | tf_op jit(solution)/shard_map/ppermute | solution.py:532
  55.0 9.5 %collective-permute-start.14 = (bf16[128,2048]{1,0:T(8,128)(2,1)S(1)}, bf16[128,2048]{1,0:T(8,128)(2,1)S(1)}, u32[]{:S(2)}, u32[]{:S(2)}) collective-permute-start(bf16[128,2048]{1,0:T(8,128)(2,1)S(1)} %constant_dynamic-update-slice_fusion.4.refs_1_), channel_id=1, source_target_pairs={{0,1},{1,0},{2,3},{3,2},{4,5},{5,4},{6,7},{7,6},{8,9},{9,8},{10,11... | collective-permute-start | bytes 1572872 | tf_op jit(solution)/shard_map/ppermute | solution.py:532
  61.4 16.6 %collective-permute-start.20 = (bf16[16,4096]{1,0:T(8,128)(2,1)S(1)}, bf16[16,4096]{1,0:T(8,128)(2,1)S(1)}, u32[]{:S(2)}, u32[]{:S(2)}) collective-permute-start(bf16[16,4096]{1,0:T(8,128)(2,1)S(1)} %get-tuple-element.104), channel_id=1, source_target_pairs={{0,28},{4,0},{8,4},{12,8},{16,12},{20,16},{24,20},{28,24},{1,29},{... | collective-permute-start | bytes 393224 | tf_op jit(solution)/shard_map/ppermute | solution.py:532
  64.5 9.8 %collective-permute-start.17 = (bf16[16,4096]{1,0:T(8,128)(2,1)S(1)}, bf16[16,4096]{1,0:T(8,128)(2,1)S(1)}, u32[]{:S(2)}, u32[]{:S(2)}) collective-permute-start(bf16[16,4096]{1,0:T(8,128)(2,1)S(1)} %get-tuple-element.99), channel_id=1, source_target_pairs={{0,12},{4,16},{8,20},{12,24},{16,28},{20,0},{24,4},{28,8},{1,13},{... | collective-permute-start | bytes 393224 | tf_op jit(solution)/shard_map/ppermute | solution.py:532
  64.5 11.4 %collective-permute-start.24 = (bf16[32,4096]{1,0:T(8,128)(2,1)S(1)}, bf16[32,4096]{1,0:T(8,128)(2,1)S(1)}, u32[]{:S(2)}, u32[]{:S(2)}) collective-permute-start(bf16[32,4096]{1,0:T(8,128)(2,1)S(1)} %pad_maximum_fusion.4), channel_id=1, source_target_pairs={{0,2},{1,3},{2,0},{3,1},{4,6},{5,7},{6,4},{7,5},{8,10},{9,11},{10,... | collective-permute-start | bytes 786440 | tf_op jit(solution)/shard_map/ppermute | solution.py:532
  74.3 7.7 %collective-permute-start.18 = (bf16[16,4096]{1,0:T(8,128)(2,1)S(1)}, bf16[16,4096]{1,0:T(8,128)(2,1)S(1)}, u32[]{:S(2)}, u32[]{:S(2)}) collective-permute-start(bf16[16,4096]{1,0:T(8,128)(2,1)S(1)} %get-tuple-element.100), channel_id=1, source_target_pairs={{0,4},{4,8},{8,12},{12,16},{16,20},{20,24},{24,28},{28,0},{1,5},{5... | collective-permute-start | bytes 393224 | tf_op jit(solution)/shard_map/ppermute | solution.py:532
  74.3 12.8 %collective-permute-start.21 = (bf16[64,4096]{1,0:T(8,128)(2,1)S(1)}, bf16[64,4096]{1,0:T(8,128)(2,1)S(1)}, u32[]{:S(2)}, u32[]{:S(2)}) collective-permute-start(bf16[64,4096]{1,0:T(8,128)(2,1)S(1)} %pad_maximum_fusion.1), channel_id=1, source_target_pairs={{0,2},{1,3},{2,0},{3,1},{4,6},{5,7},{6,4},{7,5},{8,10},{9,11},{10,... | collective-permute-start | bytes 1572872 | tf_op jit(solution)/shard_map/ppermute | solution.py:532
  77.9 17.6 %collective-permute-start.28 = (bf16[32,2,16,128]{3,2,1,0:T(8,128)(2,1)S(1)}, bf16[32,2,16,128]{3,2,1,0:T(8,128)(2,1)S(1)}, u32[]{:S(2)}, u32[]{:S(2)}) collective-permute-start(bf16[32,2,16,128]{3,2,1,0:T(8,128)(2,1)S(1)} %get-tuple-element.130), channel_id=1, source_target_pairs={{0,1},{1,0},{2,3},{3,2},{4,5},{5,4},{6,7},{7,6},{8,9},{9,8},{10,11... | collective-permute-start | bytes 786440 | tf_op jit(solution)/shard_map/ppermute | solution.py:532
  87.1 6.4 %collective-permute-start.25 = (bf16[32,4096]{1,0:T(8,128)(2,1)S(1)}, bf16[32,4096]{1,0:T(8,128)(2,1)S(1)}, u32[]{:S(2)}, u32[]{:S(2)}) collective-permute-start(bf16[32,4096]{1,0:T(8,128)(2,1)S(1)} %pad_maximum_fusion.3), channel_id=1, source_target_pairs={{0,2},{1,3},{2,0},{3,1},{4,6},{5,7},{6,4},{7,5},{8,10},{9,11},{10,... | collective-permute-start | bytes 786440 | tf_op jit(solution)/shard_map/ppermute | solution.py:532
  (14 other events, 128.7 us)

commit v3 on v2

--- a/solution.py
+++ b/solution.py
@@ -135,16 +135,10 @@
 
 CORES = 2
 MIB = 1024 * 1024
-Z_DEPTH = 4
-Y_DEPTH = 2
-C_CUTS = ((0, 4), (4, 8))
-F_CUTS = ((0, 4), (4, 6), (6, 8))
-CHOSEN = 6
-
-
-def shift_order(size):
-    far = sorted(range(1, size), key=lambda k: (abs(k - size // 2), k))
-    return [0] + far
+
+
+def hop_order(hops):
+    return [0] + sorted(range(1, hops), key=lambda k: (abs(k - hops // 2), k))
 
 
 def lane_iota(shape):
@@ -158,20 +152,27 @@
     return out
 
 
-def position_of(shift, order):
-    out = jnp.int32(0)
-    for at, k in enumerate(order):
-        out = jnp.where(shift == k, jnp.int32(at), out)
-    return out
-
-
-def pack_kernel(order, pair_rows, mark_dead, offset_ref, flag_ref, *refs):
-    shifts = len(order)
-    outs = refs[-shifts - (1 if mark_dead else 0) :][:shifts]
+def partners(offset_ref, size, sign):
+    rank = lax.axis_index("dp")
+    return [lax.rem(rank + sign * offset_ref[j] + size, size) for j in range(size)]
+
+
+def lane_of(rank, size, sign):
+    me = lax.axis_index("dp")
+    hops = size // 2
+    hop = lax.rem(sign * (rank // 2 - me // 2) + hops, hops)
+    at = jnp.int32(0)
+    for index, value in enumerate(hop_order(hops)):
+        at = jnp.where(hop == value, jnp.int32(index), at)
+    return 2 * at + (rank + me) % 2
+
+
+def pack_kernel(shifts, pair_rows, mark_dead, offset_ref, flag_ref, *refs):
     groups = flag_ref.shape[1]
     rows = groups * pair_rows
     levels = groups // shifts
     first = 0
+    lanes = partners(offset_ref, shifts, 1)
     if mark_dead:
         own_ref, other_ref, joined = refs[0], refs[1], refs[-1]
         tokens, _, part, _ = joined.shape
@@ -180,12 +181,16 @@
         flat = joined.reshape(tokens * CORES * part, rows)
         levels = levels // CORES
         first = lax.axis_index("mp") % CORES * levels
+        outs = refs[2:-1]
+        lanes = [lane_of(rank, shifts, 1) for rank in lanes]
+        lanes = [lane // 2 + lane % 2 * (shifts // 2) for lane in lanes]
     else:
         flat = refs[0]
+        outs = refs[1:]
     slots = levels * pair_rows
     total = shifts * slots
     row = lane_iota((1, rows))
-    place = pick(row // pair_rows % shifts, [position_of(offset_ref[j], order) for j in range(shifts)])
+    place = pick(row // pair_rows % shifts, lanes)
     level = row // (pair_rows * shifts) - first
     target = place * slots + level * pair_rows + row % pair_rows
     target = jnp.where((level >= 0) & (level < levels), target, -1)
@@ -211,56 +216,58 @@
         if mark_dead:
             tile = jnp.where(dead, jnp.inf, tile)
         tile = tile.astype(jnp.bfloat16)
-        for at, out in enumerate(outs):
-            out[:, start : start + step] = tile[at * slots : (at + 1) * slots]
-
-
-def pack(order, pair_rows, mark_dead, offset, flag, *sources):
+        begin = 0
+        for out in outs:
+            out[:, start : start + step] = tile[begin : begin + out.shape[0]]
+            begin += out.shape[0]
+
+
+def pack(shifts, pair_rows, mark_dead, offset, flag, *sources):
     height, rows = sources[0].shape
-    shifts = len(order)
-    slots = rows // shifts // len(sources)
+    total = rows // len(sources)
     width = height * len(sources)
     vmem = pl.BlockSpec(memory_space=pltpu.VMEM)
     scratch = []
+    pieces = [total]
     if mark_dead:
         part = 64
         scratch = [pltpu.VMEM((height // part, CORES, part, rows), jnp.bfloat16)]
+        pieces = [total // shifts] * (shifts // 2) + [total // 2]
     return pl.pallas_call(
-        functools.partial(pack_kernel, order, pair_rows, mark_dead),
-        out_shape=[jax.ShapeDtypeStruct((slots, width), jnp.bfloat16)] * shifts,
+        functools.partial(pack_kernel, shifts, pair_rows, mark_dead),
+        out_shape=[jax.ShapeDtypeStruct((piece, width), jnp.bfloat16) for piece in pieces],
         in_specs=[pl.BlockSpec(memory_space=pltpu.SMEM)] + [vmem] * (1 + len(sources)),
-        out_specs=[vmem] * shifts,
+        out_specs=[vmem] * len(pieces),
         scratch_shapes=scratch,
         compiler_params=pltpu.CompilerParams(vmem_limit_bytes=16 * MIB),
         cost_estimate=pl.CostEstimate(
-            flops=2 * shifts * slots * width * rows, bytes_accessed=2 * width * rows, transcendentals=0
+            flops=2 * total * width * rows, bytes_accessed=2 * width * rows, transcendentals=0
         ),
         name="pack_dead" if mark_dead else "pack_carried",
     )(offset, flag, *sources)
 
 
-def choose_kernel(order, pair_rows, count, group_offset_ref, cache_offset_ref, group_ref, *refs):
-    shifts = len(order)
-    near, far, near_other, far_other = (refs[i * count : (i + 1) * count] for i in range(4))
-    outs = refs[4 * count :]
+def choose_kernel(shifts, pair_rows, group_offset_ref, cache_offset_ref, group_ref, *refs):
+    near, far, near_other, far_other = refs[:4]
+    outs = refs[4:]
     core = lax.axis_index("mp") % CORES
     groups = group_ref.shape[1]
-    rows = groups * pair_rows
-    width = near[0].shape[1]
+    rows, width = near.shape
     slots = rows // shifts
     half_levels = groups // shifts // CORES
     column = lane_iota((1, rows))
-    shift_at = column // slots
+    source = column // slots
     residue = jnp.zeros_like(column)
-    for j in range(shifts):
-        residue = jnp.where(shift_at == position_of(cache_offset_ref[j], order), j, residue)
+    for j, rank in enumerate(partners(cache_offset_ref, shifts, -1)):
+        residue = jnp.where(source == rank, j, residue)
     cached = column % slots // pair_rows * shifts + residue
     pickers = (lax.broadcasted_iota(jnp.int32, (groups, rows), 0) == cached).astype(jnp.float32)
     group = jnp.dot(
         group_ref[...].astype(jnp.float32), pickers, preferred_element_type=jnp.float32
     )
     group = (group + 0.5).astype(jnp.int32)
-    place = pick(group % shifts, [position_of(group_offset_ref[j], order) for j in range(shifts)])
+    lanes = [lane_of(rank, shifts, -1) for rank in partners(group_offset_ref, shifts, -1)]
+    place = pick(group % shifts, lanes)
     goal = group // shifts - core * half_levels
     half = rows // CORES
     target = (place * half_levels + goal) * pair_rows + column % pair_rows
@@ -274,39 +281,34 @@
     for side, pair in enumerate(((near, near_other), (far, far_other))):
         for start in range(0, width, step):
             got = [
-                jnp.dot(
-                    onehot,
-                    jnp.concatenate([ref[:, start : start + step] for ref in one], axis=0),
-                    preferred_element_type=jnp.float32,
-                )
+                jnp.dot(onehot, one[:, start : start + step], preferred_element_type=jnp.float32)
                 for one in pair
             ]
             mixed = jnp.concatenate(
                 [one[:, at : at + part] for at in range(0, step, part) for one in got], axis=1
             ).astype(jnp.bfloat16)
+            lane = CORES * (side * width + start)
             for at, out in enumerate(outs):
-                lane = CORES * (side * width + start)
                 out[:, lane : lane + CORES * step] = mixed[at * piece : (at + 1) * piece]
 
 
-def choose(order, pair_rows, pieces, group_offset, cache_offset, group, *sources):
-    width = sources[0][0].shape[1]
-    rows = group.shape[1] * pair_rows
+def choose(shifts, pair_rows, pieces, group_offset, cache_offset, group, *sources):
+    rows, width = sources[0].shape
     vmem = pl.BlockSpec(memory_space=pltpu.VMEM)
     smem = pl.BlockSpec(memory_space=pltpu.SMEM)
-    flat = [x for source in sources for x in source]
-    out = jax.ShapeDtypeStruct((rows // CORES // pieces, 2 * CORES * width), jnp.bfloat16)
+    total = len(sources) * width
+    out = jax.ShapeDtypeStruct((rows // CORES // pieces, total), jnp.bfloat16)
     return pl.pallas_call(
-        functools.partial(choose_kernel, order, pair_rows, len(sources[0])),
+        functools.partial(choose_kernel, shifts, pair_rows),
         out_shape=[out] * pieces,
-        in_specs=[smem, smem] + [vmem] * (1 + len(flat)),
+        in_specs=[smem, smem] + [vmem] * (1 + len(sources)),
         out_specs=[vmem] * pieces,
         compiler_params=pltpu.CompilerParams(vmem_limit_bytes=16 * MIB),
         cost_estimate=pl.CostEstimate(
-            flops=4 * rows * rows * width, bytes_accessed=12 * rows * width, transcendentals=0
+            flops=rows * rows * total, bytes_accessed=3 * rows * total, transcendentals=0
         ),
         name="choose_carried",
-    )(group_offset, cache_offset, group, *flat)
+    )(group_offset, cache_offset, group, *sources)
 
 
 def weights_kernel(taps, own, other, far, time_out, space_out, gain_out):
@@ -460,29 +462,28 @@
     )(*arrays, carried, time_w, space_w, gain)
 
 
-def place_kernel(order, chunks, offset_ref, *refs):
+def place_kernel(shifts, offset_ref, *refs):
     blocks, out = refs[:-1], refs[-1]
     core = lax.axis_index("mp") % CORES
-    shifts = len(order)
-    for chunk in range(len(chunks)):
-        for u, shift in enumerate(chunks[chunk]):
-            residue = jnp.int32(0)
-            for j in range(shifts):
-                residue = jnp.where(offset_ref[j] == shift, jnp.int32(j), residue)
-            for kind in range(2):
-                out[core ^ kind, :, residue] = blocks[kind * len(chunks) + chunk][u]
-
-
-def place(order, chunks, pair_rows, offset, kept, got):
-    count = len(chunks[0])
+    lanes = [lane_of(rank, shifts, -1) for rank in partners(offset_ref, shifts, -1)]
+    chunks = len(blocks) // 2
+    for lane in range(shifts):
+        residue = jnp.int32(0)
+        for j in range(shifts):
+            residue = jnp.where(lanes[j] == lane, jnp.int32(j), residue)
+        for kind in range(2):
+            out[core ^ kind, :, residue] = blocks[kind * chunks + lane // 2][lane % 2]
+
+
+def place(shifts, pair_rows, offset, kept, got):
     rows, span, width, part = kept[0].shape
-    half_levels = rows // count // pair_rows
+    half_levels = rows // 2 // pair_rows
     tail = (pair_rows, span, width, part)
-    blocks = [a.reshape((count, half_levels) + tail) for a in kept + got]
+    blocks = [a.reshape((2, half_levels) + tail) for a in kept + got]
     vmem = pl.BlockSpec(memory_space=pltpu.VMEM)
     out = pl.pallas_call(
-        functools.partial(place_kernel, order, chunks),
-        out_shape=jax.ShapeDtypeStruct((CORES, half_levels, len(order)) + tail, jnp.bfloat16),
+        functools.partial(place_kernel, shifts),
+        out_shape=jax.ShapeDtypeStruct((CORES, half_levels, shifts) + tail, jnp.bfloat16),
         in_specs=[pl.BlockSpec(memory_space=pltpu.SMEM)] + [vmem] * len(blocks),
         out_specs=vmem,
         compiler_params=pltpu.CompilerParams(vmem_limit_bytes=12 * MIB),
@@ -512,9 +513,7 @@
     rows, span, width, part_in = frames.shape
     pair_rows = rows // groups
     taps = temporal_weight.shape[0]
-    order = shift_order(shifts)
-    per_chunk = 2
-    chunks = [order[i : i + per_chunk] for i in range(0, shifts, per_chunk)]
+    hops = shifts // 2
 
     def after(x, *cells):
         got = lax.optimization_barrier((x, *[cell[0] for cell in cells]))
@@ -522,47 +521,37 @@
             cell[0] = value
         return got[0]
 
-    lanes = {}
-
-    def move(x, lane, depth, axis, pairs, cells=()):
-        line = lanes.setdefault(lane, [])
-        cells = list(cells) + (line[-depth : len(line) - depth + 1] if len(line) >= depth else [])
-        if cells:
-            x = after(x, *cells)
-        line.append([lax.ppermute(x, axis, pairs)])
-        return line[-1]
-
-    def flip(x, mask, lane, depth, *cells):
-        return move(x, lane, depth, "mp", [(i, i ^ mask) for i in range(parts)], cells)
-
-    def send(x, shift, *cells):
-        if shift == 0:
-            return [x]
-        return move(x, "z", Z_DEPTH, "dp", [(i, (i + shift) % shifts) for i in range(shifts)], cells)
-
-    def join(pieces):
-        if len(pieces) == 1:
-            return pieces[0][0]
-        return jnp.concatenate([x[0] for x in pieces], axis=0)
+    def flip(x, mask, *cells):
+        x = after(x, *cells) if cells else x
+        return [lax.ppermute(x, "mp", [(i, i ^ mask) for i in range(parts)])]
+
+    def hop(x, distance, *cells):
+        x = after(x, *cells) if cells else x
+        return [lax.ppermute(x, "dp", [(i, (i + 2 * distance) % shifts) for i in range(shifts)])]
 
     cache_rows = cache.transpose((1, 2, 3, 0)).reshape((-1, rows))
     frame_rows = frames.transpose((1, 2, 3, 0)).reshape((-1, rows))
-    frame_swapped = flip(frame_rows, 1, "core", 3)
-    cache_packed = pack(
-        order, pair_rows, False, cache_offset, cache_live.reshape((1, groups)), cache_rows
-    )
-    frame_packed = [
-        [x]
-        for x in pack(
-            order,
-            pair_rows,
-            True,
-            group_offset,
-            group_rows.reshape((1, groups)),
-            frame_rows,
-            frame_swapped[0],
-        )
+    (cache_packed,) = pack(
+        shifts, pair_rows, False, cache_offset, cache_live.reshape((1, groups)), cache_rows
+    )
+    near = [lax.all_to_all(cache_packed, "dp", split_axis=0, concat_axis=0, tiled=True)]
+    frame_swapped = flip(frame_rows, 1)
+    *straight, crossing = pack(
+        shifts,
+        pair_rows,
+        True,
+        group_offset,
+        group_rows.reshape((1, groups)),
+        frame_rows,
+        frame_swapped[0],
+    )
+    crossed = lax.ppermute(crossing, "dp", [(i, i ^ 1) for i in range(shifts)])
+    slots = straight[0].shape[0]
+    ready = [
+        [jnp.concatenate([x, crossed[at * slots : (at + 1) * slots]], axis=0)]
+        for at, x in enumerate(straight)
     ]
+    first_far = flip(ready[0][0], 2)
     part = norm_gain.shape[0]
     time_rows = taps * temporal_weight.shape[1] + 16
     own_w = jnp.concatenate(
@@ -573,58 +562,40 @@
         ],
         axis=0,
     )
-    other_w = flip(own_w, 1, "core", 3)
+    other_w = flip(own_w, 1)
     far_w = flip(
-        jnp.concatenate([own_w[:time_rows], other_w[0][:time_rows]], axis=0), 2, "y", 2
+        jnp.concatenate([own_w[:time_rows], other_w[0][:time_rows]], axis=0), 2
     )
     arranged = [[x] for x in arrange_weights(taps, own_w, other_w[0], far_w[0])]
-    wait = {1: [frame_packed[0]], 2: [other_w], 5: [arranged[0]]}
-    cache_near = [send(x, k, *wait.get(i, [])) for i, (x, k) in enumerate(zip(cache_packed, order))]
-    near, far = [], []
-    for a, b in C_CUTS:
-        near.append([join(cache_near[a:b])])
-        far.append(flip(near[-1][0], 2, "y", Y_DEPTH))
-    near_other = [flip(x[0], 1, "core", 3) for x in near]
-    far_other = [flip(x[0], 1, "core", 3) for x in far]
-    carried = [
-        [x]
-        for x in choose(
-            order,
-            pair_rows,
-            len(chunks),
-            group_offset,
-            cache_offset,
-            cache_group.reshape((1, groups)),
-            *[[x[0] for x in source] for source in (near, far, near_other, far_other)],
-        )
-    ]
-    wait = {CHOSEN: [carried[0]]}
-    frame_near = [
-        send(x[0], k, *wait.get(i, [])) for i, (x, k) in enumerate(zip(frame_packed, order))
-    ]
-
-    def forward(pieces):
-        return flip(join(pieces), 2, "y", Y_DEPTH)
-
-    frame_far = {}
-    for a, b in F_CUTS:
-        cell = forward(frame_near[a:b])
-        frame_far.update({at: (cell, at - a) for at in range(a, b)})
-    slots = frame_near[0][0].shape[0]
+    far = flip(near[0], 2, arranged[0], first_far)
+    near_other = flip(near[0], 1, first_far)
+    frame_near, frame_far = [ready[0]], [first_far]
+    for at, distance in enumerate(hop_order(hops)[1:], 1):
+        frame_near.append(hop(ready[at][0], distance, near))
+    far_other = flip(far[0], 1, *frame_near[1:])
+    carried = choose(
+        shifts,
+        pair_rows,
+        hops,
+        group_offset,
+        cache_offset,
+        cache_group.reshape((1, groups)),
+        near[0],
+        far[0],
+        near_other[0],
+        far_other[0],
+    )
+    frame_far += [flip(x[0], 2) for x in frame_near[1:]]
     kept, got = [], []
-    for index in range(len(chunks)):
-        picked = range(index * per_chunk, (index + 1) * per_chunk)
-        ours = [(frame_near[at][0], 0, slots) for at in picked]
-        theirs = [
-            (frame_far[at][0][0], frame_far[at][1] * slots, (frame_far[at][1] + 1) * slots)
-            for at in picked
-        ]
+    for index in range(hops):
+        ours = [(frame_near[index][0], 0, 2 * slots)]
+        theirs = [(frame_far[index][0], 0, 2 * slots)]
         keep, give = encode(
-            width, span, ours, theirs, carried[index][0], *[x[0] for x in arranged]
+            width, span, ours, theirs, carried[index], *[x[0] for x in arranged]
         )
         kept.append(keep)
-        got.append(flip(give, 1, "core", 3)[0])
-    return place(order, chunks, pair_rows, group_offset, kept, got)
+        got.append(flip(give, 1)[0])
+    return place(shifts, pair_rows, group_offset, kept, got)
 
 
 def fits(mesh, frames, group_offset, temporal_weight):

time: 99.3 us -> 91 us (0.916)
  the two profiles are of different devices: /device:TPU:0 before, /device:TPU:11 now
where the time goes in v3:
time: 91 us; the launch traced here: 90.7 us
  waiting for transfers between devices  44.7 us (49%)
  starting transfers between devices  22.9 us (25%)
  Pallas kernels  15.5 us (17%)
  local copies, waits for them, and re-layouts  4.32 us (5%)
  other arithmetic  3.08 us (3%)
    ppermute x3, waiting for transfers between devices, hop(): lax.ppermute(x, 'dp', [(i, (i + 2 * distance) % shifts) for i in range(sh...  20.6 us
    ppermute x14, starting transfers between devices, flip(): return [lax.ppermute(x, 'mp', [(i, i ^ mask) for i in range(parts)])]  12.4 us
    ppermute x14, waiting for transfers between devices, flip(): return [lax.ppermute(x, 'mp', [(i, i ^ mask) for i in range(parts)])]  11 us
    ppermute x1, waiting for transfers between devices, routed_local(): crossed = lax.ppermute(crossing, 'dp', [(i, i ^ 1) for i in range(shifts)])  8.55 us
    pallas_call x4, Pallas kernels, encode(): pl.pallas_call(functools.partial(encode_kernel, cuts, width), out_shape=[...  7.8 us
    all_to_all x1, starting transfers between devices, routed_local(): lax.all_to_all(cache_packed, 'dp', split_axis=0, concat_axis=0, tiled=True)  5.69 us
    all_to_all x1, waiting for transfers between devices, routed_local(): lax.all_to_all(cache_packed, 'dp', split_axis=0, concat_axis=0, tiled=True)  4.65 us
    ppermute x3, starting transfers between devices, hop(): lax.ppermute(x, 'dp', [(i, (i + 2 * distance) % shifts) for i in range(sh...  4.53 us
  transfers between devices with their start and end apart: 19, of which 12 were waited for; matrix products, arithmetic and copies ran while one was open for 6% of the time, Pallas kernels for 15%

profile of v3, /device:TPU:11, one launch (start us, length us, event | category | flops | bytes accessed | tf_op | source)
XLA Modules:
  0.0 90.7 jit_solution(11950645010243247405)
XLA Ops:
  3.3 1.5 %pack_dead.1 = (bf16[16,4096]{1,0:T(8,128)(2,1)S(1)}, bf16[16,4096]{1,0:T(8,128)(2,1)S(1)}, bf16[16,4096]{1,0:T(8,128)(2,1)S(1)}, bf16[16,4096]{1,0:T(8,128)(2,1)S(1)}, bf16[64,4096]{1,0:T(8,128)(2,1)S(1)}) custom-call(s32[128]{0:T(128)S(1)} %copy-done.2, s32[1,128]{1,0:T(1,128)S(1)} %copy-done.5, bf16[2048,256]{1,0:T(8,128)(2,1)S(1)} %bitcast.25, ...), custom_call_target="tpu_custom_call" | custom-call | flops 268435456 | bytes 2097152 | tf_op jit(solution)/shard_map/pack_dead/pallas_call | solution.py:236
  5.1 2.1 %pack_carried.1 = bf16[256,2048]{1,0:T(8,128)(2,1)} custom-call(s32[128]{0:T(128)S(1)} %copy-done.3, s32[1,128]{1,0:T(1,128)S(1)} %bitcast.36, bf16[2048,256]{1,0:T(8,128)(2,1)S(1)} %bitcast.26), custom_call_target="tpu_custom_call" | custom-call | flops 268435456 | bytes 1048576 | tf_op jit(solution)/shard_map/pack_carried/pallas_call | solution.py:236
  7.1 5.7 %all-to-all-start = ((bf16[8,32,2048]{2,1,0:T(8,128)(2,1)}), bf16[8,32,2048]{2,1,0:T(8,128)(2,1)S(1)}, u32[]{:S(2)}, u32[]{:S(2)}) async-start(bf16[8,32,2048]{2,1,0:T(8,128)(2,1)} %bitcast.6), calls=%async_computation | async-start | bytes 2097152 | tf_op jit(solution)/shard_map/all_to_all | solution.py:537
  13.8 1.3 %collective-permute-start.3 = (bf16[1568,128]{1,0:T(8,128)(2,1)S(1)}, bf16[1568,128]{1,0:T(8,128)(2,1)S(1)}, u32[]{:S(2)}, u32[]{:S(2)}) collective-permute-start(bf16[1568,128]{1,0:T(8,128)(2,1)S(1)} %pad_maximum_fusion.1), channel_id=1, source_target_pairs={{0,2},{1,3},{2,0},{3,1},{4,6},{5,7},{6,4},{7,5},{8,10},{9,11},{10,... | collective-permute-start | bytes 1204232 | tf_op jit(solution)/shard_map/ppermute | solution.py:526
  15.1 8.5 %collective-permute-done.1 = bf16[64,4096]{1,0:T(8,128)(2,1)} collective-permute-done((bf16[64,4096]{1,0:T(8,128)(2,1)S(1)}, bf16[64,4096]{1,0:T(8,128)(2,1)}, u32[]{:S(2)}, u32[]{:S(2)}) %collective-permute-start.1) | collective-permute-done | bytes 524320 | tf_op jit(solution)/shard_map/ppermute | solution.py:548
  23.7 1.8 %fusion = (bf16[16,4096]{1,0:T(8,128)(2,1)S(1)}, bf16[16,4096]{1,0:T(8,128)(2,1)}, bf16[16,4096]{1,0:T(8,128)(2,1)}, bf16[16,4096]{1,0:T(8,128)(2,1)S(1)}) fusion(bf16[64,4096]{1,0:T(8,128)(2,1)} %collective-permute-done.1), kind=kLoop, calls=%fused_computation.6 | loop fusion | bytes 1048576 | tf_op jit(solution)/shard_map/slice | solution.py:551
  25.5 1.3 %collective-permute-start.4 = (bf16[32,4096]{1,0:T(8,128)(2,1)S(1)}, bf16[32,4096]{1,0:T(8,128)(2,1)S(1)}, u32[]{:S(2)}, u32[]{:S(2)}) collective-permute-start(bf16[32,4096]{1,0:T(8,128)(2,1)S(1)} %pad_maximum_fusion.2.refs_0_), channel_id=1, source_target_pairs={{0,2},{1,3},{2,0},{3,1},{4,6},{5,7},{6,4},{7,5},{8,10},{9,11},{10,... | collective-permute-start | bytes 786440 | tf_op jit(solution)/shard_map/ppermute | solution.py:526
  28.9 2.5 %collective-permute-done.4.refs_1_ = bf16[32,4096]{1,0:T(8,128)(2,1)S(1)} collective-permute-done((bf16[32,4096]{1,0:T(8,128)(2,1)S(1)}, bf16[32,4096]{1,0:T(8,128)(2,1)S(1)}, u32[]{:S(2)}, u32[]{:S(2)}) %collective-permute-start.4) | collective-permute-done | bytes 262176 | tf_op jit(solution)/shard_map/ppermute | solution.py:526
  31.3 4.7 %all-to-all-done = bf16[8,32,2048]{2,1,0:T(8,128)(2,1)S(1)} async-done(((bf16[8,32,2048]{2,1,0:T(8,128)(2,1)}), bf16[8,32,2048]{2,1,0:T(8,128)(2,1)S(1)}, u32[]{:S(2)}, u32[]{:S(2)}) %all-to-all-start) | async-done | bytes 1048608 | tf_op jit(solution)/shard_map/all_to_all | solution.py:537
  38.3 3.1 %collective-permute-start.7 = (bf16[32,4096]{1,0:T(8,128)(2,1)S(1)}, bf16[32,4096]{1,0:T(8,128)(2,1)S(1)}, u32[]{:S(2)}, u32[]{:S(2)}) collective-permute-start(bf16[32,4096]{1,0:T(8,128)(2,1)S(1)} %pad_maximum_fusion.5), channel_id=1, source_target_pairs={{0,16},{4,20},{8,24},{12,28},{16,0},{20,4},{24,8},{28,12},{1,17},{... | collective-permute-start | bytes 786440 | tf_op jit(solution)/shard_map/ppermute | solution.py:530
  42.8 1.6 %collective-permute-start.6 = (bf16[256,2048]{1,0:T(8,128)(2,1)S(1)}, bf16[256,2048]{1,0:T(8,128)(2,1)S(1)}, u32[]{:S(2)}, u32[]{:S(2)}) collective-permute-start(bf16[256,2048]{1,0:T(8,128)(2,1)S(1)} %bitcast.22), channel_id=1, source_target_pairs={{0,1},{1,0},{2,3},{3,2},{4,5},{5,4},{6,7},{7,6},{8,9},{9,8},{10,11... | collective-permute-start | bytes 3145736 | tf_op jit(solution)/shard_map/ppermute | solution.py:526
  44.4 8.8 %collective-permute-done.7.refs_0_ = bf16[32,4096]{1,0:T(8,128)(2,1)S(1)} collective-permute-done((bf16[32,4096]{1,0:T(8,128)(2,1)S(1)}, bf16[32,4096]{1,0:T(8,128)(2,1)S(1)}, u32[]{:S(2)}, u32[]{:S(2)}) %collective-permute-start.7) | collective-permute-done | bytes 262176 | tf_op jit(solution)/shard_map/ppermute | solution.py:530
  53.2 9.9 %collective-permute-done.8.refs_0_ = bf16[32,4096]{1,0:T(8,128)(2,1)S(1)} collective-permute-done((bf16[32,4096]{1,0:T(8,128)(2,1)S(1)}, bf16[32,4096]{1,0:T(8,128)(2,1)S(1)}, u32[]{:S(2)}, u32[]{:S(2)}) %collective-permute-start.8) | collective-permute-done | bytes 262176 | tf_op jit(solution)/shard_map/ppermute | solution.py:530
  63.0 2.0 %collective-permute-done.9.refs_0_ = bf16[32,4096]{1,0:T(8,128)(2,1)S(1)} collective-permute-done((bf16[32,4096]{1,0:T(8,128)(2,1)S(1)}, bf16[32,4096]{1,0:T(8,128)(2,1)S(1)}, u32[]{:S(2)}, u32[]{:S(2)}) %collective-permute-start.9) | collective-permute-done | bytes 262176 | tf_op jit(solution)/shard_map/ppermute | solution.py:530
  67.8 1.8 %choose_carried.1 = (bf16[32,8192]{1,0:T(8,128)(2,1)S(1)}, bf16[32,8192]{1,0:T(8,128)(2,1)S(1)}, bf16[32,8192]{1,0:T(8,128)(2,1)S(1)}, bf16[32,8192]{1,0:T(8,128)(2,1)S(1)}) custom-call(s32[128]{0:T(128)S(1)} %copy-done.2, s32[128]{0:T(128)S(1)} %copy-done.3, s32[1,128]{1,0:T(1,128)S(1)} %bitcast.35, bf16[256,2048]{1,0:T(8,128)(2,1)S(1)} %bitcast.23, ...), custom_call_target="tpu_custom_call" | custom-call | flops 536870912 | bytes 6291456 | tf_op jit(solution)/shard_map/choose_carried/pallas_call | solution.py:301
  69.6 2.0 %encode_rows.4 = (bf16[32,2,16,128]{3,2,1,0:T(8,128)(2,1)S(1)}, bf16[32,2,16,128]{3,2,1,0:T(8,128)(2,1)S(1)}) custom-call(bf16[32,4096]{1,0:T(8,128)(2,1)S(1)} %pad_maximum_fusion.2.refs_0_, bf16[32,4096]{1,0:T(8,128)(2,1)S(1)} %collective-permute-done.4.refs_1_, bf16[32,8192]{1,0:T(8,128)(2,1)S(1)} %get-tuple-element.57.refs_2_, ...), custom_call_target="tpu_custom_call" | custom-call | flops 1610612736 | bytes 3670016 | tf_op jit(solution)/shard_map/encode_rows/pallas_call | solution.py:445
  72.0 1.4 %collective-permute-done.11.refs_1_ = bf16[32,4096]{1,0:T(8,128)(2,1)S(1)} collective-permute-done((bf16[32,4096]{1,0:T(8,128)(2,1)S(1)}, bf16[32,4096]{1,0:T(8,128)(2,1)S(1)}, u32[]{:S(2)}, u32[]{:S(2)}) %collective-permute-start.11) | collective-permute-done | bytes 262176 | tf_op jit(solution)/shard_map/ppermute | solution.py:526
  73.4 2.0 %encode_rows.5 = (bf16[32,2,16,128]{3,2,1,0:T(8,128)(2,1)S(1)}, bf16[32,2,16,128]{3,2,1,0:T(8,128)(2,1)S(1)}) custom-call(bf16[32,4096]{1,0:T(8,128)(2,1)S(1)} %collective-permute-done.7.refs_0_, bf16[32,4096]{1,0:T(8,128)(2,1)S(1)} %collective-permute-done.11.refs_1_, bf16[32,8192]{1,0:T(8,128)(2,1)S(1)} %get-tuple-element.63.refs_2_, ...), custom_call_target="tpu_custom_call" | custom-call | flops 1610612736 | bytes 3670016 | tf_op jit(solution)/shard_map/encode_rows/pallas_call | solution.py:445
  75.4 1.3 %collective-permute-start.15 = (bf16[32,2,16,128]{3,2,1,0:T(8,128)(2,1)S(1)}, bf16[32,2,16,128]{3,2,1,0:T(8,128)(2,1)S(1)}, u32[]{:S(2)}, u32[]{:S(2)}) collective-permute-start(bf16[32,2,16,128]{3,2,1,0:T(8,128)(2,1)S(1)} %get-tuple-element.72), channel_id=1, source_target_pairs={{0,1},{1,0},{2,3},{3,2},{4,5},{5,4},{6,7},{7,6},{8,9},{9,8},{10,11... | collective-permute-start | bytes 786440 | tf_op jit(solution)/shard_map/ppermute | solution.py:526
  76.7 2.4 %collective-permute-done.12.refs_1_ = bf16[32,4096]{1,0:T(8,128)(2,1)S(1)} collective-permute-done((bf16[32,4096]{1,0:T(8,128)(2,1)S(1)}, bf16[32,4096]{1,0:T(8,128)(2,1)S(1)}, u32[]{:S(2)}, u32[]{:S(2)}) %collective-permute-start.12) | collective-permute-done | bytes 262176 | tf_op jit(solution)/shard_map/ppermute | solution.py:526
  79.0 1.9 %encode_rows.6 = (bf16[32,2,16,128]{3,2,1,0:T(8,128)(2,1)S(1)}, bf16[32,2,16,128]{3,2,1,0:T(8,128)(2,1)S(1)}) custom-call(bf16[32,4096]{1,0:T(8,128)(2,1)S(1)} %collective-permute-done.8.refs_0_, bf16[32,4096]{1,0:T(8,128)(2,1)S(1)} %collective-permute-done.12.refs_1_, bf16[32,8192]{1,0:T(8,128)(2,1)S(1)} %get-tuple-element.66.refs_2_, ...), custom_call_target="tpu_custom_call" | custom-call | flops 1610612736 | bytes 3670016 | tf_op jit(solution)/shard_map/encode_rows/pallas_call | solution.py:445
  82.3 2.4 %collective-permute-done.13.refs_1_ = bf16[32,4096]{1,0:T(8,128)(2,1)S(1)} collective-permute-done((bf16[32,4096]{1,0:T(8,128)(2,1)S(1)}, bf16[32,4096]{1,0:T(8,128)(2,1)S(1)}, u32[]{:S(2)}, u32[]{:S(2)}) %collective-permute-start.13) | collective-permute-done | bytes 262176 | tf_op jit(solution)/shard_map/ppermute | solution.py:526
  84.7 1.9 %encode_rows.7 = (bf16[32,2,16,128]{3,2,1,0:T(8,128)(2,1)S(1)}, bf16[32,2,16,128]{3,2,1,0:T(8,128)(2,1)S(1)}) custom-call(bf16[32,4096]{1,0:T(8,128)(2,1)S(1)} %collective-permute-done.9.refs_0_, bf16[32,4096]{1,0:T(8,128)(2,1)S(1)} %collective-permute-done.13.refs_1_, bf16[32,8192]{1,0:T(8,128)(2,1)S(1)} %get-tuple-element.69.refs_2_, ...), custom_call_target="tpu_custom_call" | custom-call | flops 1610612736 | bytes 3670016 | tf_op jit(solution)/shard_map/encode_rows/pallas_call | solution.py:445
  88.6 2.1 %place_rows.1 = bf16[2,8,8,2,2,16,128]{6,5,4,3,2,1,0:T(8,128)(2,1)} custom-call(s32[128]{0:T(128)S(1)} %copy-done.2, bf16[2,8,2,2,16,128]{5,4,3,2,1,0:T(8,128)(2,1)S(1)} %bitcast.27, bf16[2,8,2,2,16,128]{5,4,3,2,1,0:T(8,128)(2,1)S(1)} %bitcast.29, bf16[2,8,2,2,16,128]{5,4,3,2,1,0:T(8,128)(2,1)S(1)} %bitcast.31, bf16[2,8,2,2,16,128]{5,4,3,2,1,0:T(8,128)(2,1)S(1)} %bitcast.33, ...), custom_call_target="tpu_custom_call" | custom-call | bytes 4194304 | tf_op jit(solution)/shard_map/place_rows/pallas_call | solution.py:484
  (53 shorter events, 16.8 us)
Async XLA Ops:
  0.0 3.2 %copy-start = (bf16[256,2,16,64]{0,3,2,1:T(8,128)(2,1)S(1)}, bf16[256,2,16,64]{0,3,2,1:T(8,128)(2,1)}, u32[]{:S(2)}) copy-start(bf16[256,2,16,64]{0,3,2,1:T(8,128)(2,1)} %param.10) | copy-start | bytes 3145732
  0.0 3.3 %copy-start.2 = (s32[128]{0:T(128)S(1)}, s32[128]{0:T(128)}, u32[]{:S(2)}) copy-start(s32[128]{0:T(128)} %offset_ref.5) | copy-start | bytes 1540
  0.0 3.3 %copy-start.5 = (s32[1,128]{1,0:T(1,128)S(1)}, s32[1,128]{1,0:T(1,128)}, u32[]{:S(2)}) copy-start(s32[1,128]{1,0:T(1,128)} %flag_ref.1) | copy-start | bytes 1540
  0.0 3.2 %collective-permute-start = (bf16[2048,256]{1,0:T(8,128)(2,1)}, bf16[2048,256]{1,0:T(8,128)(2,1)S(1)}, u32[]{:S(2)}, u32[]{:S(2)}) collective-permute-start(bf16[2048,256]{1,0:T(8,128)(2,1)} %bitcast.24), channel_id=1, source_target_pairs={{0,1},{1,0},{2,3},{3,2},{4,5},{5,4},{6,7},{7,6},{8,9},{9,8},{10,11... | collective-permute-start | bytes 3145736 | tf_op jit(solution)/shard_map/ppermute | solution.py:526
  2.5 2.5 %copy-start.1 = (bf16[256,2,16,64]{0,3,2,1:T(8,128)(2,1)S(1)}, bf16[256,2,16,64]{0,3,2,1:T(8,128)(2,1)}, u32[]{:S(2)}) copy-start(bf16[256,2,16,64]{0,3,2,1:T(8,128)(2,1)} %param.11) | copy-start | bytes 3145732
  2.5 10.3 %collective-permute-start.2 = (bf16[2320,128]{1,0:T(8,128)(2,1)S(1)}, bf16[2320,128]{1,0:T(8,128)(2,1)S(1)}, u32[]{:S(2)}, u32[]{:S(2)}) collective-permute-start(bf16[2320,128]{1,0:T(8,128)(2,1)S(1)} %pad_maximum_fusion.own), channel_id=1, source_target_pairs={{0,1},{1,0},{2,3},{3,2},{4,5},{5,4},{6,7},{7,6},{8,9},{9,8},{10,11... | collective-permute-start | bytes 1781768 | tf_op jit(solution)/shard_map/ppermute | solution.py:526
  4.7 18.9 %collective-permute-start.1 = (bf16[64,4096]{1,0:T(8,128)(2,1)S(1)}, bf16[64,4096]{1,0:T(8,128)(2,1)}, u32[]{:S(2)}, u32[]{:S(2)}) collective-permute-start(bf16[64,4096]{1,0:T(8,128)(2,1)S(1)} %get-tuple-element.41), channel_id=1, source_target_pairs={{0,4},{4,0},{8,12},{12,8},{16,20},{20,16},{24,28},{28,24},{1,5},{5... | collective-permute-start | bytes 1572872 | tf_op jit(solution)/shard_map/ppermute | solution.py:548
  7.1 28.9 %all-to-all-start = ((bf16[8,32,2048]{2,1,0:T(8,128)(2,1)}), bf16[8,32,2048]{2,1,0:T(8,128)(2,1)S(1)}, u32[]{:S(2)}, u32[]{:S(2)}) async-start(bf16[8,32,2048]{2,1,0:T(8,128)(2,1)} %bitcast.6), calls=%async_computation | async-start | bytes 2097152 | tf_op jit(solution)/shard_map/all_to_all | solution.py:537
  13.8 13.0 %collective-permute-start.3 = (bf16[1568,128]{1,0:T(8,128)(2,1)S(1)}, bf16[1568,128]{1,0:T(8,128)(2,1)S(1)}, u32[]{:S(2)}, u32[]{:S(2)}) collective-permute-start(bf16[1568,128]{1,0:T(8,128)(2,1)S(1)} %pad_maximum_fusion.1), channel_id=1, source_target_pairs={{0,2},{1,3},{2,0},{3,1},{4,6},{5,7},{6,4},{7,5},{8,10},{9,11},{10,... | collective-permute-start | bytes 1204232 | tf_op jit(solution)/shard_map/ppermute | solution.py:526
  25.5 5.9 %collective-permute-start.4 = (bf16[32,4096]{1,0:T(8,128)(2,1)S(1)}, bf16[32,4096]{1,0:T(8,128)(2,1)S(1)}, u32[]{:S(2)}, u32[]{:S(2)}) collective-permute-start(bf16[32,4096]{1,0:T(8,128)(2,1)S(1)} %pad_maximum_fusion.2.refs_0_), channel_id=1, source_target_pairs={{0,2},{1,3},{2,0},{3,1},{4,6},{5,7},{6,4},{7,5},{8,10},{9,11},{10,... | collective-permute-start | bytes 786440 | tf_op jit(solution)/shard_map/ppermute | solution.py:526
  28.9 38.9 %copy-start.4 = (s32[128]{0:T(128)S(1)}, s32[128]{0:T(128)}, u32[]{:S(2)}) copy-start(s32[128]{0:T(128)} %param.14) | copy-start | bytes 1540
  36.0 29.0 %collective-permute-start.5 = (bf16[256,2048]{1,0:T(8,128)(2,1)S(1)}, bf16[256,2048]{1,0:T(8,128)(2,1)S(1)}, u32[]{:S(2)}, u32[]{:S(2)}) collective-permute-start(bf16[256,2048]{1,0:T(8,128)(2,1)S(1)} %bitcast.21), channel_id=1, source_target_pairs={{0,2},{1,3},{2,0},{3,1},{4,6},{5,7},{6,4},{7,5},{8,10},{9,11},{10,... | collective-permute-start | bytes 3145736 | tf_op jit(solution)/shard_map/ppermute | solution.py:526
  38.3 14.9 %collective-permute-start.7 = (bf16[32,4096]{1,0:T(8,128)(2,1)S(1)}, bf16[32,4096]{1,0:T(8,128)(2,1)S(1)}, u32[]{:S(2)}, u32[]{:S(2)}) collective-permute-start(bf16[32,4096]{1,0:T(8,128)(2,1)S(1)} %pad_maximum_fusion.5), channel_id=1, source_target_pairs={{0,16},{4,20},{8,24},{12,28},{16,0},{20,4},{24,8},{28,12},{1,17},{... | collective-permute-start | bytes 786440 | tf_op jit(solution)/shard_map/ppermute | solution.py:530
  41.3 21.7 %collective-permute-start.8 = (bf16[32,4096]{1,0:T(8,128)(2,1)S(1)}, bf16[32,4096]{1,0:T(8,128)(2,1)S(1)}, u32[]{:S(2)}, u32[]{:S(2)}) collective-permute-start(bf16[32,4096]{1,0:T(8,128)(2,1)S(1)} %get-tuple-element.54), channel_id=1, source_target_pairs={{0,8},{4,12},{8,16},{12,20},{16,24},{20,28},{24,0},{28,4},{1,9},{5... | collective-permute-start | bytes 786440 | tf_op jit(solution)/shard_map/ppermute | solution.py:530
  41.6 23.4 %collective-permute-start.9 = (bf16[32,4096]{1,0:T(8,128)(2,1)S(1)}, bf16[32,4096]{1,0:T(8,128)(2,1)S(1)}, u32[]{:S(2)}, u32[]{:S(2)}) collective-permute-start(bf16[32,4096]{1,0:T(8,128)(2,1)S(1)} %get-tuple-element.55), channel_id=1, source_target_pairs={{0,24},{4,28},{8,0},{12,4},{16,8},{20,12},{24,16},{28,20},{1,25},{... | collective-permute-start | bytes 786440 | tf_op jit(solution)/shard_map/ppermute | solution.py:530
  42.8 24.4 %collective-permute-start.6 = (bf16[256,2048]{1,0:T(8,128)(2,1)S(1)}, bf16[256,2048]{1,0:T(8,128)(2,1)S(1)}, u32[]{:S(2)}, u32[]{:S(2)}) collective-permute-start(bf16[256,2048]{1,0:T(8,128)(2,1)S(1)} %bitcast.22), channel_id=1, source_target_pairs={{0,1},{1,0},{2,3},{3,2},{4,5},{5,4},{6,7},{7,6},{8,9},{9,8},{10,11... | collective-permute-start | bytes 3145736 | tf_op jit(solution)/shard_map/ppermute | solution.py:526
  65.0 2.8 %collective-permute-start.10 = (bf16[256,2048]{1,0:T(8,128)(2,1)S(1)}, bf16[256,2048]{1,0:T(8,128)(2,1)S(1)}, u32[]{:S(2)}, u32[]{:S(2)}) collective-permute-start(bf16[256,2048]{1,0:T(8,128)(2,1)S(1)} %collective-permute-done.5.refs_1_), channel_id=1, source_target_pairs={{0,1},{1,0},{2,3},{3,2},{4,5},{5,4},{6,7},{7,6},{8,9},{9,8},{10,11... | collective-permute-start | bytes 3145736 | tf_op jit(solution)/shard_map/ppermute | solution.py:526
  65.5 7.9 %collective-permute-start.11 = (bf16[32,4096]{1,0:T(8,128)(2,1)S(1)}, bf16[32,4096]{1,0:T(8,128)(2,1)S(1)}, u32[]{:S(2)}, u32[]{:S(2)}) collective-permute-start(bf16[32,4096]{1,0:T(8,128)(2,1)S(1)} %collective-permute-done.7.refs_0_), channel_id=1, source_target_pairs={{0,2},{1,3},{2,0},{3,1},{4,6},{5,7},{6,4},{7,5},{8,10},{9,11},{10,... | collective-permute-start | bytes 786440 | tf_op jit(solution)/shard_map/ppermute | solution.py:526
  65.7 13.3 %collective-permute-start.12 = (bf16[32,4096]{1,0:T(8,128)(2,1)S(1)}, bf16[32,4096]{1,0:T(8,128)(2,1)S(1)}, u32[]{:S(2)}, u32[]{:S(2)}) collective-permute-start(bf16[32,4096]{1,0:T(8,128)(2,1)S(1)} %collective-permute-done.8.refs_0_), channel_id=1, source_target_pairs={{0,2},{1,3},{2,0},{3,1},{4,6},{5,7},{6,4},{7,5},{8,10},{9,11},{10,... | collective-permute-start | bytes 786440 | tf_op jit(solution)/shard_map/ppermute | solution.py:526
  67.0 17.7 %collective-permute-start.13 = (bf16[32,4096]{1,0:T(8,128)(2,1)S(1)}, bf16[32,4096]{1,0:T(8,128)(2,1)S(1)}, u32[]{:S(2)}, u32[]{:S(2)}) collective-permute-start(bf16[32,4096]{1,0:T(8,128)(2,1)S(1)} %collective-permute-done.9.refs_0_), channel_id=1, source_target_pairs={{0,2},{1,3},{2,0},{3,1},{4,6},{5,7},{6,4},{7,5},{8,10},{9,11},{10,... | collective-permute-start | bytes 786440 | tf_op jit(solution)/shard_map/ppermute | solution.py:526
  71.6 15.9 %collective-permute-start.14 = (bf16[32,2,16,128]{3,2,1,0:T(8,128)(2,1)S(1)}, bf16[32,2,16,128]{3,2,1,0:T(8,128)(2,1)S(1)}, u32[]{:S(2)}, u32[]{:S(2)}) collective-permute-start(bf16[32,2,16,128]{3,2,1,0:T(8,128)(2,1)S(1)} %get-tuple-element.71), channel_id=1, source_target_pairs={{0,1},{1,0},{2,3},{3,2},{4,5},{5,4},{6,7},{7,6},{8,9},{9,8},{10,11... | collective-permute-start | bytes 786440 | tf_op jit(solution)/shard_map/ppermute | solution.py:526
  75.4 12.1 %collective-permute-start.15 = (bf16[32,2,16,128]{3,2,1,0:T(8,128)(2,1)S(1)}, bf16[32,2,16,128]{3,2,1,0:T(8,128)(2,1)S(1)}, u32[]{:S(2)}, u32[]{:S(2)}) collective-permute-start(bf16[32,2,16,128]{3,2,1,0:T(8,128)(2,1)S(1)} %get-tuple-element.72), channel_id=1, source_target_pairs={{0,1},{1,0},{2,3},{3,2},{4,5},{5,4},{6,7},{7,6},{8,9},{9,8},{10,11... | collective-permute-start | bytes 786440 | tf_op jit(solution)/shard_map/ppermute | solution.py:526
  81.0 6.5 %collective-permute-start.16 = (bf16[32,2,16,128]{3,2,1,0:T(8,128)(2,1)S(1)}, bf16[32,2,16,128]{3,2,1,0:T(8,128)(2,1)S(1)}, u32[]{:S(2)}, u32[]{:S(2)}) collective-permute-start(bf16[32,2,16,128]{3,2,1,0:T(8,128)(2,1)S(1)} %get-tuple-element.73), channel_id=1, source_target_pairs={{0,1},{1,0},{2,3},{3,2},{4,5},{5,4},{6,7},{7,6},{8,9},{9,8},{10,11... | collective-permute-start | bytes 786440 | tf_op jit(solution)/shard_map/ppermute | solution.py:526
  86.6 2.0 %collective-permute-start.17 = (bf16[32,2,16,128]{3,2,1,0:T(8,128)(2,1)S(1)}, bf16[32,2,16,128]{3,2,1,0:T(8,128)(2,1)S(1)}, u32[]{:S(2)}, u32[]{:S(2)}) collective-permute-start(bf16[32,2,16,128]{3,2,1,0:T(8,128)(2,1)S(1)} %get-tuple-element.74), channel_id=1, source_target_pairs={{0,1},{1,0},{2,3},{3,2},{4,5},{5,4},{6,7},{7,6},{8,9},{9,8},{10,11... | collective-permute-start | bytes 786440 | tf_op jit(solution)/shard_map/ppermute | solution.py:526
  (6 other events, 10.5 us)

commit v4 on v3

--- a/solution.py
+++ b/solution.py
@@ -135,6 +135,7 @@
 
 CORES = 2
 MIB = 1024 * 1024
+EARLY = (2,)
 
 
 def hop_order(hops):
@@ -567,12 +568,15 @@
         jnp.concatenate([own_w[:time_rows], other_w[0][:time_rows]], axis=0), 2
     )
     arranged = [[x] for x in arrange_weights(taps, own_w, other_w[0], far_w[0])]
-    far = flip(near[0], 2, arranged[0], first_far)
+    early = {at: flip(ready[at][0], 2) for at in EARLY if at < hops}
+    far = flip(near[0], 2, arranged[0], first_far, *early.values())
     near_other = flip(near[0], 1, first_far)
-    frame_near, frame_far = [ready[0]], [first_far]
+    frame_near, frame_far = [ready[0]], {0: first_far}
     for at, distance in enumerate(hop_order(hops)[1:], 1):
         frame_near.append(hop(ready[at][0], distance, near))
-    far_other = flip(far[0], 1, *frame_near[1:])
+        if at in early:
+            frame_far[at] = hop(early[at][0], distance, near)
+    far_other = flip(far[0], 1, *frame_near[1:], *[frame_far[at] for at in early])
     carried = choose(
         shifts,
         pair_rows,
@@ -585,7 +589,9 @@
         near_other[0],
         far_other[0],
     )
-    frame_far += [flip(x[0], 2) for x in frame_near[1:]]
+    for at in range(1, hops):
+        if at not in early:
+            frame_far[at] = flip(frame_near[at][0], 2)
     kept, got = [], []
     for index in range(hops):
         ours = [(frame_near[index][0], 0, 2 * slots)]

time: 91 us -> 90.2 us (level)
  starting transfers between devices: 22.9 us -> 24.3 us
  waiting for transfers between devices: 44.7 us -> 43.6 us
  other arithmetic: 3.08 us -> 2.12 us
    all_to_all x1, waiting for transfers between devices: 4.65 us -> 0.01 us  [routed_local(): lax.all_to_all(cache_packed, 'dp', split_axis=0, concat_axis=0, tiled=True)]
    ppermute x3 -> x4, waiting for transfers between devices: 20.6 us -> 23 us  [hop(): lax.ppermute(x, 'dp', [(i, (i + 2 * distance) % shifts) for i in range(sh...]
    ppermute x14, starting transfers between devices: 12.4 us -> 14.5 us  [flip(): return [lax.ppermute(x, 'mp', [(i, i ^ mask) for i in range(parts)])]]
    ppermute x14, waiting for transfers between devices: 11 us -> 12 us  [flip(): return [lax.ppermute(x, 'mp', [(i, i ^ mask) for i in range(parts)])]]
    concatenate x3 -> x4, other arithmetic: 1.04 us -> 0.08 us  [routed_local(): jnp.concatenate([x, crossed[at * slots:(at + 1) * slots]], axis=0)]
    ppermute x3 -> x4, starting transfers between devices: 4.53 us -> 3.81 us  [hop(): lax.ppermute(x, 'dp', [(i, (i + 2 * distance) % shifts) for i in range(sh...]
    unnamed x22 -> x26, local copies, waits for them, and re-layouts: 1.83 us -> 1.83 us
  transfers between devices with their start and end apart: 19 -> 20, of which waited for: 12 -> 11; matrix products, arithmetic and copies ran while one was open for 6% -> 5% of each run, Pallas kernels for 15% -> 15%
where the time goes in v4:
time: 90.2 us; the launch traced here: 89.9 us
  waiting for transfers between devices  43.6 us (48%)
  starting transfers between devices  24.3 us (27%)
  Pallas kernels  15.5 us (17%)
  local copies, waits for them, and re-layouts  4.29 us (5%)
  other arithmetic  2.12 us (2%)
    ppermute x4, waiting for transfers between devices, hop(): lax.ppermute(x, 'dp', [(i, (i + 2 * distance) % shifts) for i in range(sh...  23 us
    ppermute x14, starting transfers between devices, flip(): return [lax.ppermute(x, 'mp', [(i, i ^ mask) for i in range(parts)])]  14.5 us
    ppermute x14, waiting for transfers between devices, flip(): return [lax.ppermute(x, 'mp', [(i, i ^ mask) for i in range(parts)])]  12 us
    ppermute x1, waiting for transfers between devices, routed_local(): crossed = lax.ppermute(crossing, 'dp', [(i, i ^ 1) for i in range(shifts)])  8.55 us
    pallas_call x4, Pallas kernels, encode(): pl.pallas_call(functools.partial(encode_kernel, cuts, width), out_shape=[...  7.79 us
    all_to_all x1, starting transfers between devices, routed_local(): lax.all_to_all(cache_packed, 'dp', split_axis=0, concat_axis=0, tiled=True)  5.69 us
    ppermute x4, starting transfers between devices, hop(): lax.ppermute(x, 'dp', [(i, (i + 2 * distance) % shifts) for i in range(sh...  3.81 us
    pallas_call x2, Pallas kernels, pack(): pl.pallas_call(functools.partial(pack_kernel, shifts, pair_rows, mark_dea...  3.53 us
  transfers between devices with their start and end apart: 20, of which 11 were waited for; matrix products, arithmetic and copies ran while one was open for 5% of the time, Pallas kernels for 15%

profile of v4, /device:TPU:11, one launch (start us, length us, event | category | flops | bytes accessed | tf_op | source)
XLA Modules:
  0.0 89.9 jit_solution(12399401328021773814)
XLA Ops:
  3.3 1.5 %pack_dead.1 = (bf16[16,4096]{1,0:T(8,128)(2,1)S(1)}, bf16[16,4096]{1,0:T(8,128)(2,1)S(1)}, bf16[16,4096]{1,0:T(8,128)(2,1)S(1)}, bf16[16,4096]{1,0:T(8,128)(2,1)S(1)}, bf16[64,4096]{1,0:T(8,128)(2,1)S(1)}) custom-call(s32[128]{0:T(128)S(1)} %copy-done.2, s32[1,128]{1,0:T(1,128)S(1)} %copy-done.5, bf16[2048,256]{1,0:T(8,128)(2,1)S(1)} %bitcast.25, ...), custom_call_target="tpu_custom_call" | custom-call | flops 268435456 | bytes 2097152 | tf_op jit(solution)/shard_map/pack_dead/pallas_call | solution.py:237
  5.1 2.1 %pack_carried.1 = bf16[256,2048]{1,0:T(8,128)(2,1)} custom-call(s32[128]{0:T(128)S(1)} %copy-done.3, s32[1,128]{1,0:T(1,128)S(1)} %bitcast.36, bf16[2048,256]{1,0:T(8,128)(2,1)S(1)} %bitcast.26), custom_call_target="tpu_custom_call" | custom-call | flops 268435456 | bytes 1048576 | tf_op jit(solution)/shard_map/pack_carried/pallas_call | solution.py:237
  7.1 5.7 %all-to-all-start = ((bf16[8,32,2048]{2,1,0:T(8,128)(2,1)}), bf16[8,32,2048]{2,1,0:T(8,128)(2,1)S(1)}, u32[]{:S(2)}, u32[]{:S(2)}) async-start(bf16[8,32,2048]{2,1,0:T(8,128)(2,1)} %bitcast.6), calls=%async_computation | async-start | bytes 2097152 | tf_op jit(solution)/shard_map/all_to_all | solution.py:538
  13.8 1.3 %collective-permute-start.3 = (bf16[1568,128]{1,0:T(8,128)(2,1)S(1)}, bf16[1568,128]{1,0:T(8,128)(2,1)S(1)}, u32[]{:S(2)}, u32[]{:S(2)}) collective-permute-start(bf16[1568,128]{1,0:T(8,128)(2,1)S(1)} %pad_maximum_fusion.1), channel_id=1, source_target_pairs={{0,2},{1,3},{2,0},{3,1},{4,6},{5,7},{6,4},{7,5},{8,10},{9,11},{10,... | collective-permute-start | bytes 1204232 | tf_op jit(solution)/shard_map/ppermute | solution.py:527
  15.1 8.5 %collective-permute-done.1 = bf16[64,4096]{1,0:T(8,128)(2,1)} collective-permute-done((bf16[64,4096]{1,0:T(8,128)(2,1)S(1)}, bf16[64,4096]{1,0:T(8,128)(2,1)}, u32[]{:S(2)}, u32[]{:S(2)}) %collective-permute-start.1) | collective-permute-done | bytes 524320 | tf_op jit(solution)/shard_map/ppermute | solution.py:549
  23.7 1.8 %fusion = (bf16[16,4096]{1,0:T(8,128)(2,1)S(1)}, bf16[16,4096]{1,0:T(8,128)(2,1)}, bf16[16,4096]{1,0:T(8,128)(2,1)S(1)}, bf16[16,4096]{1,0:T(8,128)(2,1)S(1)}) fusion(bf16[64,4096]{1,0:T(8,128)(2,1)} %collective-permute-done.1), kind=kLoop, calls=%fused_computation.6 | loop fusion | bytes 1048576 | tf_op jit(solution)/shard_map/slice | solution.py:552
  25.5 1.3 %collective-permute-start.4 = (bf16[32,4096]{1,0:T(8,128)(2,1)S(1)}, bf16[32,4096]{1,0:T(8,128)(2,1)S(1)}, u32[]{:S(2)}, u32[]{:S(2)}) collective-permute-start(bf16[32,4096]{1,0:T(8,128)(2,1)S(1)} %pad_maximum_fusion.2.refs_0_), channel_id=1, source_target_pairs={{0,2},{1,3},{2,0},{3,1},{4,6},{5,7},{6,4},{7,5},{8,10},{9,11},{10,... | collective-permute-start | bytes 786440 | tf_op jit(solution)/shard_map/ppermute | solution.py:527
  29.2 2.1 %collective-permute-done.4.refs_1_ = bf16[32,4096]{1,0:T(8,128)(2,1)S(1)} collective-permute-done((bf16[32,4096]{1,0:T(8,128)(2,1)S(1)}, bf16[32,4096]{1,0:T(8,128)(2,1)S(1)}, u32[]{:S(2)}, u32[]{:S(2)}) %collective-permute-start.4) | collective-permute-done | bytes 262176 | tf_op jit(solution)/shard_map/ppermute | solution.py:527
  31.3 5.7 %collective-permute-done.5 = bf16[32,4096]{1,0:T(8,128)(2,1)} collective-permute-done((bf16[32,4096]{1,0:T(8,128)(2,1)S(1)}, bf16[32,4096]{1,0:T(8,128)(2,1)}, u32[]{:S(2)}, u32[]{:S(2)}) %collective-permute-start.5) | collective-permute-done | bytes 262176 | tf_op jit(solution)/shard_map/ppermute | solution.py:527
  38.3 2.3 %collective-permute-start.8 = (bf16[32,4096]{1,0:T(8,128)(2,1)S(1)}, bf16[32,4096]{1,0:T(8,128)(2,1)S(1)}, u32[]{:S(2)}, u32[]{:S(2)}) collective-permute-start(bf16[32,4096]{1,0:T(8,128)(2,1)S(1)} %pad_maximum_fusion.5), channel_id=1, source_target_pairs={{0,16},{4,20},{8,24},{12,28},{16,0},{20,4},{24,8},{28,12},{1,17},{... | collective-permute-start | bytes 786440 | tf_op jit(solution)/shard_map/ppermute | solution.py:531
  40.7 1.5 %collective-permute-start.10 = (bf16[32,4096]{1,0:T(8,128)(2,1)S(1)}, bf16[32,4096]{1,0:T(8,128)(2,1)S(1)}, u32[]{:S(2)}, u32[]{:S(2)}) collective-permute-start(bf16[32,4096]{1,0:T(8,128)(2,1)S(1)} %pad_maximum_fusion.4), channel_id=1, source_target_pairs={{0,24},{4,28},{8,0},{12,4},{16,8},{20,12},{24,16},{28,20},{1,25},{... | collective-permute-start | bytes 786440 | tf_op jit(solution)/shard_map/ppermute | solution.py:531
  42.2 10.0 %collective-permute-done.8.refs_0_ = bf16[32,4096]{1,0:T(8,128)(2,1)S(1)} collective-permute-done((bf16[32,4096]{1,0:T(8,128)(2,1)S(1)}, bf16[32,4096]{1,0:T(8,128)(2,1)S(1)}, u32[]{:S(2)}, u32[]{:S(2)}) %collective-permute-start.8) | collective-permute-done | bytes 262176 | tf_op jit(solution)/shard_map/ppermute | solution.py:531
  52.2 4.4 %collective-permute-start.7 = (bf16[256,2048]{1,0:T(8,128)(2,1)S(1)}, bf16[256,2048]{1,0:T(8,128)(2,1)S(1)}, u32[]{:S(2)}, u32[]{:S(2)}) collective-permute-start(bf16[256,2048]{1,0:T(8,128)(2,1)S(1)} %bitcast.22), channel_id=1, source_target_pairs={{0,1},{1,0},{2,3},{3,2},{4,5},{5,4},{6,7},{7,6},{8,9},{9,8},{10,11... | collective-permute-start | bytes 3145736 | tf_op jit(solution)/shard_map/ppermute | solution.py:527
  56.6 4.1 %collective-permute-done.9.refs_0_ = bf16[32,4096]{1,0:T(8,128)(2,1)S(1)} collective-permute-done((bf16[32,4096]{1,0:T(8,128)(2,1)}, bf16[32,4096]{1,0:T(8,128)(2,1)S(1)}, u32[]{:S(2)}, u32[]{:S(2)}) %collective-permute-start.9) | collective-permute-done | bytes 262176 | tf_op jit(solution)/shard_map/ppermute | solution.py:531
  60.7 8.9 %collective-permute-done.10.refs_0_ = bf16[32,4096]{1,0:T(8,128)(2,1)S(1)} collective-permute-done((bf16[32,4096]{1,0:T(8,128)(2,1)S(1)}, bf16[32,4096]{1,0:T(8,128)(2,1)S(1)}, u32[]{:S(2)}, u32[]{:S(2)}) %collective-permute-start.10) | collective-permute-done | bytes 262176 | tf_op jit(solution)/shard_map/ppermute | solution.py:531
  70.5 1.2 %collective-permute-start.14 = (bf16[32,4096]{1,0:T(8,128)(2,1)S(1)}, bf16[32,4096]{1,0:T(8,128)(2,1)S(1)}, u32[]{:S(2)}, u32[]{:S(2)}) collective-permute-start(bf16[32,4096]{1,0:T(8,128)(2,1)S(1)} %collective-permute-done.10.refs_0_), channel_id=1, source_target_pairs={{0,2},{1,3},{2,0},{3,1},{4,6},{5,7},{6,4},{7,5},{8,10},{9,11},{10,... | collective-permute-start | bytes 786440 | tf_op jit(solution)/shard_map/ppermute | solution.py:527
  72.6 1.8 %choose_carried.1 = (bf16[32,8192]{1,0:T(8,128)(2,1)S(1)}, bf16[32,8192]{1,0:T(8,128)(2,1)S(1)}, bf16[32,8192]{1,0:T(8,128)(2,1)S(1)}, bf16[32,8192]{1,0:T(8,128)(2,1)S(1)}) custom-call(s32[128]{0:T(128)S(1)} %copy-done.2, s32[128]{0:T(128)S(1)} %copy-done.3, s32[1,128]{1,0:T(1,128)S(1)} %bitcast.35, bf16[256,2048]{1,0:T(8,128)(2,1)S(1)} %bitcast.23, ...), custom_call_target="tpu_custom_call" | custom-call | flops 536870912 | bytes 6291456 | tf_op jit(solution)/shard_map/choose_carried/pallas_call | solution.py:302
  74.4 1.9 %encode_rows.4 = (bf16[32,2,16,128]{3,2,1,0:T(8,128)(2,1)S(1)}, bf16[32,2,16,128]{3,2,1,0:T(8,128)(2,1)S(1)}) custom-call(bf16[32,4096]{1,0:T(8,128)(2,1)S(1)} %pad_maximum_fusion.2.refs_0_, bf16[32,4096]{1,0:T(8,128)(2,1)S(1)} %collective-permute-done.4.refs_1_, bf16[32,8192]{1,0:T(8,128)(2,1)S(1)} %get-tuple-element.64.refs_2_, ...), custom_call_target="tpu_custom_call" | custom-call | flops 1610612736 | bytes 3670016 | tf_op jit(solution)/shard_map/encode_rows/pallas_call | solution.py:446
  76.8 1.3 %collective-permute-done.13.refs_1_ = bf16[32,4096]{1,0:T(8,128)(2,1)S(1)} collective-permute-done((bf16[32,4096]{1,0:T(8,128)(2,1)S(1)}, bf16[32,4096]{1,0:T(8,128)(2,1)S(1)}, u32[]{:S(2)}, u32[]{:S(2)}) %collective-permute-start.13) | collective-permute-done | bytes 262176 | tf_op jit(solution)/shard_map/ppermute | solution.py:527
  78.2 1.9 %encode_rows.5 = (bf16[32,2,16,128]{3,2,1,0:T(8,128)(2,1)S(1)}, bf16[32,2,16,128]{3,2,1,0:T(8,128)(2,1)S(1)}) custom-call(bf16[32,4096]{1,0:T(8,128)(2,1)S(1)} %collective-permute-done.8.refs_0_, bf16[32,4096]{1,0:T(8,128)(2,1)S(1)} %collective-permute-done.13.refs_1_, bf16[32,8192]{1,0:T(8,128)(2,1)S(1)} %get-tuple-element.70.refs_2_, ...), custom_call_target="tpu_custom_call" | custom-call | flops 1610612736 | bytes 3670016 | tf_op jit(solution)/shard_map/encode_rows/pallas_call | solution.py:446
  80.1 1.4 %collective-permute-start.16 = (bf16[32,2,16,128]{3,2,1,0:T(8,128)(2,1)S(1)}, bf16[32,2,16,128]{3,2,1,0:T(8,128)(2,1)S(1)}, u32[]{:S(2)}, u32[]{:S(2)}) collective-permute-start(bf16[32,2,16,128]{3,2,1,0:T(8,128)(2,1)S(1)} %get-tuple-element.80), channel_id=1, source_target_pairs={{0,1},{1,0},{2,3},{3,2},{4,5},{5,4},{6,7},{7,6},{8,9},{9,8},{10,11... | collective-permute-start | bytes 786440 | tf_op jit(solution)/shard_map/ppermute | solution.py:527
  81.5 1.9 %encode_rows.6 = (bf16[32,2,16,128]{3,2,1,0:T(8,128)(2,1)S(1)}, bf16[32,2,16,128]{3,2,1,0:T(8,128)(2,1)S(1)}) custom-call(bf16[32,4096]{1,0:T(8,128)(2,1)S(1)} %collective-permute-done.9.refs_0_, bf16[32,4096]{1,0:T(8,128)(2,1)S(1)} %collective-permute-done.11.refs_1_, bf16[32,8192]{1,0:T(8,128)(2,1)S(1)} %get-tuple-element.74.refs_2_, ...), custom_call_target="tpu_custom_call" | custom-call | flops 1610612736 | bytes 3670016 | tf_op jit(solution)/shard_map/encode_rows/pallas_call | solution.py:446
  83.8 1.9 %encode_rows.7 = (bf16[32,2,16,128]{3,2,1,0:T(8,128)(2,1)S(1)}, bf16[32,2,16,128]{3,2,1,0:T(8,128)(2,1)S(1)}) custom-call(bf16[32,4096]{1,0:T(8,128)(2,1)S(1)} %collective-permute-done.10.refs_0_, bf16[32,4096]{1,0:T(8,128)(2,1)S(1)} %collective-permute-done.14.refs_1_, bf16[32,8192]{1,0:T(8,128)(2,1)S(1)} %get-tuple-element.77.refs_2_, ...), custom_call_target="tpu_custom_call" | custom-call | flops 1610612736 | bytes 3670016 | tf_op jit(solution)/shard_map/encode_rows/pallas_call | solution.py:446
  87.8 2.1 %place_rows.1 = bf16[2,8,8,2,2,16,128]{6,5,4,3,2,1,0:T(8,128)(2,1)} custom-call(s32[128]{0:T(128)S(1)} %copy-done.2, bf16[2,8,2,2,16,128]{5,4,3,2,1,0:T(8,128)(2,1)S(1)} %bitcast.27, bf16[2,8,2,2,16,128]{5,4,3,2,1,0:T(8,128)(2,1)S(1)} %bitcast.29, bf16[2,8,2,2,16,128]{5,4,3,2,1,0:T(8,128)(2,1)S(1)} %bitcast.31, bf16[2,8,2,2,16,128]{5,4,3,2,1,0:T(8,128)(2,1)S(1)} %bitcast.33, ...), custom_call_target="tpu_custom_call" | custom-call | bytes 4194304 | tf_op jit(solution)/shard_map/place_rows/pallas_call | solution.py:485
  (60 shorter events, 12.8 us)
Async XLA Ops:
  0.0 3.3 %copy-start.5 = (s32[1,128]{1,0:T(1,128)S(1)}, s32[1,128]{1,0:T(1,128)}, u32[]{:S(2)}) copy-start(s32[1,128]{1,0:T(1,128)} %flag_ref.1) | copy-start | bytes 1540
  0.0 3.2 %collective-permute-start = (bf16[2048,256]{1,0:T(8,128)(2,1)}, bf16[2048,256]{1,0:T(8,128)(2,1)S(1)}, u32[]{:S(2)}, u32[]{:S(2)}) collective-permute-start(bf16[2048,256]{1,0:T(8,128)(2,1)} %bitcast.24), channel_id=1, source_target_pairs={{0,1},{1,0},{2,3},{3,2},{4,5},{5,4},{6,7},{7,6},{8,9},{9,8},{10,11... | collective-permute-start | bytes 3145736 | tf_op jit(solution)/shard_map/ppermute | solution.py:527
  2.5 10.3 %collective-permute-start.2 = (bf16[2320,128]{1,0:T(8,128)(2,1)S(1)}, bf16[2320,128]{1,0:T(8,128)(2,1)S(1)}, u32[]{:S(2)}, u32[]{:S(2)}) collective-permute-start(bf16[2320,128]{1,0:T(8,128)(2,1)S(1)} %pad_maximum_fusion.own), channel_id=1, source_target_pairs={{0,1},{1,0},{2,3},{3,2},{4,5},{5,4},{6,7},{7,6},{8,9},{9,8},{10,11... | collective-permute-start | bytes 1781768 | tf_op jit(solution)/shard_map/ppermute | solution.py:527
  4.7 18.9 %collective-permute-start.1 = (bf16[64,4096]{1,0:T(8,128)(2,1)S(1)}, bf16[64,4096]{1,0:T(8,128)(2,1)}, u32[]{:S(2)}, u32[]{:S(2)}) collective-permute-start(bf16[64,4096]{1,0:T(8,128)(2,1)S(1)} %get-tuple-element.45), channel_id=1, source_target_pairs={{0,4},{4,0},{8,12},{12,8},{16,20},{20,16},{24,28},{28,24},{1,5},{5... | collective-permute-start | bytes 1572872 | tf_op jit(solution)/shard_map/ppermute | solution.py:549
  7.1 29.9 %all-to-all-start = ((bf16[8,32,2048]{2,1,0:T(8,128)(2,1)}), bf16[8,32,2048]{2,1,0:T(8,128)(2,1)S(1)}, u32[]{:S(2)}, u32[]{:S(2)}) async-start(bf16[8,32,2048]{2,1,0:T(8,128)(2,1)} %bitcast.6), calls=%async_computation | async-start | bytes 2097152 | tf_op jit(solution)/shard_map/all_to_all | solution.py:538
  13.8 13.3 %collective-permute-start.3 = (bf16[1568,128]{1,0:T(8,128)(2,1)S(1)}, bf16[1568,128]{1,0:T(8,128)(2,1)S(1)}, u32[]{:S(2)}, u32[]{:S(2)}) collective-permute-start(bf16[1568,128]{1,0:T(8,128)(2,1)S(1)} %pad_maximum_fusion.1), channel_id=1, source_target_pairs={{0,2},{1,3},{2,0},{3,1},{4,6},{5,7},{6,4},{7,5},{8,10},{9,11},{10,... | collective-permute-start | bytes 1204232 | tf_op jit(solution)/shard_map/ppermute | solution.py:527
  25.5 12.8 %copy-start.11 = (bf16[16,4096]{1,0:T(8,128)(2,1)S(1)}, bf16[16,4096]{1,0:T(8,128)(2,1)}, u32[]{:S(2)}) copy-start(bf16[16,4096]{1,0:T(8,128)(2,1)} %get-tuple-element.84) | copy-start | bytes 393220
  25.5 5.9 %collective-permute-start.4 = (bf16[32,4096]{1,0:T(8,128)(2,1)S(1)}, bf16[32,4096]{1,0:T(8,128)(2,1)S(1)}, u32[]{:S(2)}, u32[]{:S(2)}) collective-permute-start(bf16[32,4096]{1,0:T(8,128)(2,1)S(1)} %pad_maximum_fusion.2.refs_0_), channel_id=1, source_target_pairs={{0,2},{1,3},{2,0},{3,1},{4,6},{5,7},{6,4},{7,5},{8,10},{9,11},{10,... | collective-permute-start | bytes 786440 | tf_op jit(solution)/shard_map/ppermute | solution.py:527
  26.8 4.5 %copy-start.12 = (bf16[32,4096]{1,0:T(8,128)(2,1)}, bf16[32,4096]{1,0:T(8,128)(2,1)S(1)}, u32[]{:S(2)}) copy-start(bf16[32,4096]{1,0:T(8,128)(2,1)S(1)} %pad_maximum_fusion.3) | copy-start | bytes 786436
  26.8 45.8 %copy-start.4 = (s32[128]{0:T(128)S(1)}, s32[128]{0:T(128)}, u32[]{:S(2)}) copy-start(s32[128]{0:T(128)} %param.14) | copy-start | bytes 1540
  26.8 10.2 %collective-permute-start.5 = (bf16[32,4096]{1,0:T(8,128)(2,1)S(1)}, bf16[32,4096]{1,0:T(8,128)(2,1)}, u32[]{:S(2)}, u32[]{:S(2)}) collective-permute-start(bf16[32,4096]{1,0:T(8,128)(2,1)S(1)} %pad_maximum_fusion.3), channel_id=1, source_target_pairs={{0,2},{1,3},{2,0},{3,1},{4,6},{5,7},{6,4},{7,5},{8,10},{9,11},{10,... | collective-permute-start | bytes 786440 | tf_op jit(solution)/shard_map/ppermute | solution.py:527
  37.0 32.6 %collective-permute-start.6 = (bf16[256,2048]{1,0:T(8,128)(2,1)S(1)}, bf16[256,2048]{1,0:T(8,128)(2,1)S(1)}, u32[]{:S(2)}, u32[]{:S(2)}) collective-permute-start(bf16[256,2048]{1,0:T(8,128)(2,1)S(1)} %bitcast.21), channel_id=1, source_target_pairs={{0,2},{1,3},{2,0},{3,1},{4,6},{5,7},{6,4},{7,5},{8,10},{9,11},{10,... | collective-permute-start | bytes 3145736 | tf_op jit(solution)/shard_map/ppermute | solution.py:527
  38.3 13.8 %collective-permute-start.8 = (bf16[32,4096]{1,0:T(8,128)(2,1)S(1)}, bf16[32,4096]{1,0:T(8,128)(2,1)S(1)}, u32[]{:S(2)}, u32[]{:S(2)}) collective-permute-start(bf16[32,4096]{1,0:T(8,128)(2,1)S(1)} %pad_maximum_fusion.5), channel_id=1, source_target_pairs={{0,16},{4,20},{8,24},{12,28},{16,0},{20,4},{24,8},{28,12},{1,17},{... | collective-permute-start | bytes 786440 | tf_op jit(solution)/shard_map/ppermute | solution.py:531
  40.7 20.0 %collective-permute-start.9 = (bf16[32,4096]{1,0:T(8,128)(2,1)}, bf16[32,4096]{1,0:T(8,128)(2,1)S(1)}, u32[]{:S(2)}, u32[]{:S(2)}) collective-permute-start(bf16[32,4096]{1,0:T(8,128)(2,1)} %copy-done.12), channel_id=1, source_target_pairs={{0,8},{4,12},{8,16},{12,20},{16,24},{20,28},{24,0},{28,4},{1,9},{5... | collective-permute-start | bytes 786440 | tf_op jit(solution)/shard_map/ppermute | solution.py:531
  40.7 28.9 %collective-permute-start.10 = (bf16[32,4096]{1,0:T(8,128)(2,1)S(1)}, bf16[32,4096]{1,0:T(8,128)(2,1)S(1)}, u32[]{:S(2)}, u32[]{:S(2)}) collective-permute-start(bf16[32,4096]{1,0:T(8,128)(2,1)S(1)} %pad_maximum_fusion.4), channel_id=1, source_target_pairs={{0,24},{4,28},{8,0},{12,4},{16,8},{20,12},{24,16},{28,20},{1,25},{... | collective-permute-start | bytes 786440 | tf_op jit(solution)/shard_map/ppermute | solution.py:531
  42.1 27.5 %collective-permute-start.11 = (bf16[32,4096]{1,0:T(8,128)(2,1)}, bf16[32,4096]{1,0:T(8,128)(2,1)S(1)}, u32[]{:S(2)}, u32[]{:S(2)}) collective-permute-start(bf16[32,4096]{1,0:T(8,128)(2,1)} %collective-permute-done.5), channel_id=1, source_target_pairs={{0,8},{4,12},{8,16},{12,20},{16,24},{20,28},{24,0},{28,4},{1,9},{5... | collective-permute-start | bytes 786440 | tf_op jit(solution)/shard_map/ppermute | solution.py:531
  52.2 19.6 %collective-permute-start.7 = (bf16[256,2048]{1,0:T(8,128)(2,1)S(1)}, bf16[256,2048]{1,0:T(8,128)(2,1)S(1)}, u32[]{:S(2)}, u32[]{:S(2)}) collective-permute-start(bf16[256,2048]{1,0:T(8,128)(2,1)S(1)} %bitcast.22), channel_id=1, source_target_pairs={{0,1},{1,0},{2,3},{3,2},{4,5},{5,4},{6,7},{7,6},{8,9},{9,8},{10,11... | collective-permute-start | bytes 3145736 | tf_op jit(solution)/shard_map/ppermute | solution.py:527
  69.6 3.0 %collective-permute-start.12 = (bf16[256,2048]{1,0:T(8,128)(2,1)S(1)}, bf16[256,2048]{1,0:T(8,128)(2,1)S(1)}, u32[]{:S(2)}, u32[]{:S(2)}) collective-permute-start(bf16[256,2048]{1,0:T(8,128)(2,1)S(1)} %collective-permute-done.6.refs_1_), channel_id=1, source_target_pairs={{0,1},{1,0},{2,3},{3,2},{4,5},{5,4},{6,7},{7,6},{8,9},{9,8},{10,11... | collective-permute-start | bytes 3145736 | tf_op jit(solution)/shard_map/ppermute | solution.py:527
  70.3 7.9 %collective-permute-start.13 = (bf16[32,4096]{1,0:T(8,128)(2,1)S(1)}, bf16[32,4096]{1,0:T(8,128)(2,1)S(1)}, u32[]{:S(2)}, u32[]{:S(2)}) collective-permute-start(bf16[32,4096]{1,0:T(8,128)(2,1)S(1)} %collective-permute-done.8.refs_0_), channel_id=1, source_target_pairs={{0,2},{1,3},{2,0},{3,1},{4,6},{5,7},{6,4},{7,5},{8,10},{9,11},{10,... | collective-permute-start | bytes 786440 | tf_op jit(solution)/shard_map/ppermute | solution.py:527
  70.5 13.3 %collective-permute-start.14 = (bf16[32,4096]{1,0:T(8,128)(2,1)S(1)}, bf16[32,4096]{1,0:T(8,128)(2,1)S(1)}, u32[]{:S(2)}, u32[]{:S(2)}) collective-permute-start(bf16[32,4096]{1,0:T(8,128)(2,1)S(1)} %collective-permute-done.10.refs_0_), channel_id=1, source_target_pairs={{0,2},{1,3},{2,0},{3,1},{4,6},{5,7},{6,4},{7,5},{8,10},{9,11},{10,... | collective-permute-start | bytes 786440 | tf_op jit(solution)/shard_map/ppermute | solution.py:527
  76.4 10.3 %collective-permute-start.15 = (bf16[32,2,16,128]{3,2,1,0:T(8,128)(2,1)S(1)}, bf16[32,2,16,128]{3,2,1,0:T(8,128)(2,1)S(1)}, u32[]{:S(2)}, u32[]{:S(2)}) collective-permute-start(bf16[32,2,16,128]{3,2,1,0:T(8,128)(2,1)S(1)} %get-tuple-element.79), channel_id=1, source_target_pairs={{0,1},{1,0},{2,3},{3,2},{4,5},{5,4},{6,7},{7,6},{8,9},{9,8},{10,11... | collective-permute-start | bytes 786440 | tf_op jit(solution)/shard_map/ppermute | solution.py:527
  80.1 6.5 %collective-permute-start.16 = (bf16[32,2,16,128]{3,2,1,0:T(8,128)(2,1)S(1)}, bf16[32,2,16,128]{3,2,1,0:T(8,128)(2,1)S(1)}, u32[]{:S(2)}, u32[]{:S(2)}) collective-permute-start(bf16[32,2,16,128]{3,2,1,0:T(8,128)(2,1)S(1)} %get-tuple-element.80), channel_id=1, source_target_pairs={{0,1},{1,0},{2,3},{3,2},{4,5},{5,4},{6,7},{7,6},{8,9},{9,8},{10,11... | collective-permute-start | bytes 786440 | tf_op jit(solution)/shard_map/ppermute | solution.py:527
  83.5 3.2 %collective-permute-start.17 = (bf16[32,2,16,128]{3,2,1,0:T(8,128)(2,1)S(1)}, bf16[32,2,16,128]{3,2,1,0:T(8,128)(2,1)S(1)}, u32[]{:S(2)}, u32[]{:S(2)}) collective-permute-start(bf16[32,2,16,128]{3,2,1,0:T(8,128)(2,1)S(1)} %get-tuple-element.81), channel_id=1, source_target_pairs={{0,1},{1,0},{2,3},{3,2},{4,5},{5,4},{6,7},{7,6},{8,9},{9,8},{10,11... | collective-permute-start | bytes 786440 | tf_op jit(solution)/shard_map/ppermute | solution.py:527
  85.7 2.1 %collective-permute-start.18 = (bf16[32,2,16,128]{3,2,1,0:T(8,128)(2,1)S(1)}, bf16[32,2,16,128]{3,2,1,0:T(8,128)(2,1)S(1)}, u32[]{:S(2)}, u32[]{:S(2)}) collective-permute-start(bf16[32,2,16,128]{3,2,1,0:T(8,128)(2,1)S(1)} %get-tuple-element.82), channel_id=1, source_target_pairs={{0,1},{1,0},{2,3},{3,2},{4,5},{5,4},{6,7},{7,6},{8,9},{9,8},{10,11... | collective-permute-start | bytes 786440 | tf_op jit(solution)/shard_map/ppermute | solution.py:527
  (9 other events, 19.5 us)

commit v5 on v4

--- a/solution.py
+++ b/solution.py
@@ -573,7 +573,7 @@
     near_other = flip(near[0], 1, first_far)
     frame_near, frame_far = [ready[0]], {0: first_far}
     for at, distance in enumerate(hop_order(hops)[1:], 1):
-        frame_near.append(hop(ready[at][0], distance, near))
+        frame_near.append(hop(ready[at][0], distance, near if at == 1 else first_far))
         if at in early:
             frame_far[at] = hop(early[at][0], distance, near)
     far_other = flip(far[0], 1, *frame_near[1:], *[frame_far[at] for at in early])

time: 90.2 us -> 90.2 us (level)
  no operation moved by 1% of the time
where the time goes in v5:
time: 90.2 us; the launch traced here: 89.9 us
  waiting for transfers between devices  43.6 us (48%)
  starting transfers between devices  24.3 us (27%)
  Pallas kernels  15.5 us (17%)
  local copies, waits for them, and re-layouts  4.29 us (5%)
  other arithmetic  2.12 us (2%)
    ppermute x4, waiting for transfers between devices, hop(): lax.ppermute(x, 'dp', [(i, (i + 2 * distance) % shifts) for i in range(sh...  23 us
    ppermute x14, starting transfers between devices, flip(): return [lax.ppermute(x, 'mp', [(i, i ^ mask) for i in range(parts)])]  14.5 us
    ppermute x14, waiting for transfers between devices, flip(): return [lax.ppermute(x, 'mp', [(i, i ^ mask) for i in range(parts)])]  12 us
    ppermute x1, waiting for transfers between devices, routed_local(): crossed = lax.ppermute(crossing, 'dp', [(i, i ^ 1) for i in range(shifts)])  8.55 us
    pallas_call x4, Pallas kernels, encode(): pl.pallas_call(functools.partial(encode_kernel, cuts, width), out_shape=[...  7.79 us
    all_to_all x1, starting transfers between devices, routed_local(): lax.all_to_all(cache_packed, 'dp', split_axis=0, concat_axis=0, tiled=True)  5.69 us
    ppermute x4, starting transfers between devices, hop(): lax.ppermute(x, 'dp', [(i, (i + 2 * distance) % shifts) for i in range(sh...  3.81 us
    pallas_call x2, Pallas kernels, pack(): pl.pallas_call(functools.partial(pack_kernel, shifts, pair_rows, mark_dea...  3.53 us
  transfers between devices with their start and end apart: 20, of which 11 were waited for; matrix products, arithmetic and copies ran while one was open for 5% of the time, Pallas kernels for 15%

profile of v5, /device:TPU:11, one launch (start us, length us, event | category | flops | bytes accessed | tf_op | source)
XLA Modules:
  0.0 89.9 jit_solution(14920436100586658522)
XLA Ops:
  3.3 1.5 %pack_dead.1 = (bf16[16,4096]{1,0:T(8,128)(2,1)S(1)}, bf16[16,4096]{1,0:T(8,128)(2,1)S(1)}, bf16[16,4096]{1,0:T(8,128)(2,1)S(1)}, bf16[16,4096]{1,0:T(8,128)(2,1)S(1)}, bf16[64,4096]{1,0:T(8,128)(2,1)S(1)}) custom-call(s32[128]{0:T(128)S(1)} %copy-done.2, s32[1,128]{1,0:T(1,128)S(1)} %copy-done.5, bf16[2048,256]{1,0:T(8,128)(2,1)S(1)} %bitcast.25, ...), custom_call_target="tpu_custom_call" | custom-call | flops 268435456 | bytes 2097152 | tf_op jit(solution)/shard_map/pack_dead/pallas_call | solution.py:237
  5.1 2.1 %pack_carried.1 = bf16[256,2048]{1,0:T(8,128)(2,1)} custom-call(s32[128]{0:T(128)S(1)} %copy-done.3, s32[1,128]{1,0:T(1,128)S(1)} %bitcast.36, bf16[2048,256]{1,0:T(8,128)(2,1)S(1)} %bitcast.26), custom_call_target="tpu_custom_call" | custom-call | flops 268435456 | bytes 1048576 | tf_op jit(solution)/shard_map/pack_carried/pallas_call | solution.py:237
  7.1 5.7 %all-to-all-start = ((bf16[8,32,2048]{2,1,0:T(8,128)(2,1)}), bf16[8,32,2048]{2,1,0:T(8,128)(2,1)S(1)}, u32[]{:S(2)}, u32[]{:S(2)}) async-start(bf16[8,32,2048]{2,1,0:T(8,128)(2,1)} %bitcast.6), calls=%async_computation | async-start | bytes 2097152 | tf_op jit(solution)/shard_map/all_to_all | solution.py:538
  13.8 1.3 %collective-permute-start.3 = (bf16[1568,128]{1,0:T(8,128)(2,1)S(1)}, bf16[1568,128]{1,0:T(8,128)(2,1)S(1)}, u32[]{:S(2)}, u32[]{:S(2)}) collective-permute-start(bf16[1568,128]{1,0:T(8,128)(2,1)S(1)} %pad_maximum_fusion.1), channel_id=1, source_target_pairs={{0,2},{1,3},{2,0},{3,1},{4,6},{5,7},{6,4},{7,5},{8,10},{9,11},{10,... | collective-permute-start | bytes 1204232 | tf_op jit(solution)/shard_map/ppermute | solution.py:527
  15.1 8.5 %collective-permute-done.1 = bf16[64,4096]{1,0:T(8,128)(2,1)} collective-permute-done((bf16[64,4096]{1,0:T(8,128)(2,1)S(1)}, bf16[64,4096]{1,0:T(8,128)(2,1)}, u32[]{:S(2)}, u32[]{:S(2)}) %collective-permute-start.1) | collective-permute-done | bytes 524320 | tf_op jit(solution)/shard_map/ppermute | solution.py:549
  23.7 1.8 %fusion = (bf16[16,4096]{1,0:T(8,128)(2,1)S(1)}, bf16[16,4096]{1,0:T(8,128)(2,1)S(1)}, bf16[16,4096]{1,0:T(8,128)(2,1)}, bf16[16,4096]{1,0:T(8,128)(2,1)S(1)}) fusion(bf16[64,4096]{1,0:T(8,128)(2,1)} %collective-permute-done.1), kind=kLoop, calls=%fused_computation.6 | loop fusion | bytes 1048576 | tf_op jit(solution)/shard_map/slice | solution.py:552
  25.5 1.3 %collective-permute-start.4 = (bf16[32,4096]{1,0:T(8,128)(2,1)S(1)}, bf16[32,4096]{1,0:T(8,128)(2,1)S(1)}, u32[]{:S(2)}, u32[]{:S(2)}) collective-permute-start(bf16[32,4096]{1,0:T(8,128)(2,1)S(1)} %pad_maximum_fusion.2.refs_0_), channel_id=1, source_target_pairs={{0,2},{1,3},{2,0},{3,1},{4,6},{5,7},{6,4},{7,5},{8,10},{9,11},{10,... | collective-permute-start | bytes 786440 | tf_op jit(solution)/shard_map/ppermute | solution.py:527
  29.2 2.1 %collective-permute-done.4.refs_1_ = bf16[32,4096]{1,0:T(8,128)(2,1)S(1)} collective-permute-done((bf16[32,4096]{1,0:T(8,128)(2,1)S(1)}, bf16[32,4096]{1,0:T(8,128)(2,1)S(1)}, u32[]{:S(2)}, u32[]{:S(2)}) %collective-permute-start.4) | collective-permute-done | bytes 262176 | tf_op jit(solution)/shard_map/ppermute | solution.py:527
  31.3 5.7 %collective-permute-done.5 = bf16[32,4096]{1,0:T(8,128)(2,1)} collective-permute-done((bf16[32,4096]{1,0:T(8,128)(2,1)S(1)}, bf16[32,4096]{1,0:T(8,128)(2,1)}, u32[]{:S(2)}, u32[]{:S(2)}) %collective-permute-start.5) | collective-permute-done | bytes 262176 | tf_op jit(solution)/shard_map/ppermute | solution.py:527
  38.3 2.3 %collective-permute-start.8 = (bf16[32,4096]{1,0:T(8,128)(2,1)S(1)}, bf16[32,4096]{1,0:T(8,128)(2,1)S(1)}, u32[]{:S(2)}, u32[]{:S(2)}) collective-permute-start(bf16[32,4096]{1,0:T(8,128)(2,1)S(1)} %pad_maximum_fusion.5), channel_id=1, source_target_pairs={{0,16},{4,20},{8,24},{12,28},{16,0},{20,4},{24,8},{28,12},{1,17},{... | collective-permute-start | bytes 786440 | tf_op jit(solution)/shard_map/ppermute | solution.py:531
  40.7 1.5 %collective-permute-start.10 = (bf16[32,4096]{1,0:T(8,128)(2,1)S(1)}, bf16[32,4096]{1,0:T(8,128)(2,1)S(1)}, u32[]{:S(2)}, u32[]{:S(2)}) collective-permute-start(bf16[32,4096]{1,0:T(8,128)(2,1)S(1)} %pad_maximum_fusion.3), channel_id=1, source_target_pairs={{0,24},{4,28},{8,0},{12,4},{16,8},{20,12},{24,16},{28,20},{1,25},{... | collective-permute-start | bytes 786440 | tf_op jit(solution)/shard_map/ppermute | solution.py:531
  42.2 10.0 %collective-permute-done.8.refs_0_ = bf16[32,4096]{1,0:T(8,128)(2,1)S(1)} collective-permute-done((bf16[32,4096]{1,0:T(8,128)(2,1)S(1)}, bf16[32,4096]{1,0:T(8,128)(2,1)S(1)}, u32[]{:S(2)}, u32[]{:S(2)}) %collective-permute-start.8) | collective-permute-done | bytes 262176 | tf_op jit(solution)/shard_map/ppermute | solution.py:531
  52.2 4.4 %collective-permute-start.7 = (bf16[256,2048]{1,0:T(8,128)(2,1)S(1)}, bf16[256,2048]{1,0:T(8,128)(2,1)S(1)}, u32[]{:S(2)}, u32[]{:S(2)}) collective-permute-start(bf16[256,2048]{1,0:T(8,128)(2,1)S(1)} %bitcast.22), channel_id=1, source_target_pairs={{0,1},{1,0},{2,3},{3,2},{4,5},{5,4},{6,7},{7,6},{8,9},{9,8},{10,11... | collective-permute-start | bytes 3145736 | tf_op jit(solution)/shard_map/ppermute | solution.py:527
  56.6 4.1 %collective-permute-done.9.refs_0_ = bf16[32,4096]{1,0:T(8,128)(2,1)S(1)} collective-permute-done((bf16[32,4096]{1,0:T(8,128)(2,1)}, bf16[32,4096]{1,0:T(8,128)(2,1)S(1)}, u32[]{:S(2)}, u32[]{:S(2)}) %collective-permute-start.9) | collective-permute-done | bytes 262176 | tf_op jit(solution)/shard_map/ppermute | solution.py:531
  60.7 8.9 %collective-permute-done.10.refs_0_ = bf16[32,4096]{1,0:T(8,128)(2,1)S(1)} collective-permute-done((bf16[32,4096]{1,0:T(8,128)(2,1)S(1)}, bf16[32,4096]{1,0:T(8,128)(2,1)S(1)}, u32[]{:S(2)}, u32[]{:S(2)}) %collective-permute-start.10) | collective-permute-done | bytes 262176 | tf_op jit(solution)/shard_map/ppermute | solution.py:531
  70.5 1.2 %collective-permute-start.14 = (bf16[32,4096]{1,0:T(8,128)(2,1)S(1)}, bf16[32,4096]{1,0:T(8,128)(2,1)S(1)}, u32[]{:S(2)}, u32[]{:S(2)}) collective-permute-start(bf16[32,4096]{1,0:T(8,128)(2,1)S(1)} %collective-permute-done.10.refs_0_), channel_id=1, source_target_pairs={{0,2},{1,3},{2,0},{3,1},{4,6},{5,7},{6,4},{7,5},{8,10},{9,11},{10,... | collective-permute-start | bytes 786440 | tf_op jit(solution)/shard_map/ppermute | solution.py:527
  72.6 1.8 %choose_carried.1 = (bf16[32,8192]{1,0:T(8,128)(2,1)S(1)}, bf16[32,8192]{1,0:T(8,128)(2,1)S(1)}, bf16[32,8192]{1,0:T(8,128)(2,1)S(1)}, bf16[32,8192]{1,0:T(8,128)(2,1)S(1)}) custom-call(s32[128]{0:T(128)S(1)} %copy-done.2, s32[128]{0:T(128)S(1)} %copy-done.3, s32[1,128]{1,0:T(1,128)S(1)} %bitcast.35, bf16[256,2048]{1,0:T(8,128)(2,1)S(1)} %bitcast.23, ...), custom_call_target="tpu_custom_call" | custom-call | flops 536870912 | bytes 6291456 | tf_op jit(solution)/shard_map/choose_carried/pallas_call | solution.py:302
  74.4 1.9 %encode_rows.4 = (bf16[32,2,16,128]{3,2,1,0:T(8,128)(2,1)S(1)}, bf16[32,2,16,128]{3,2,1,0:T(8,128)(2,1)S(1)}) custom-call(bf16[32,4096]{1,0:T(8,128)(2,1)S(1)} %pad_maximum_fusion.2.refs_0_, bf16[32,4096]{1,0:T(8,128)(2,1)S(1)} %collective-permute-done.4.refs_1_, bf16[32,8192]{1,0:T(8,128)(2,1)S(1)} %get-tuple-element.64.refs_2_, ...), custom_call_target="tpu_custom_call" | custom-call | flops 1610612736 | bytes 3670016 | tf_op jit(solution)/shard_map/encode_rows/pallas_call | solution.py:446
  76.8 1.3 %collective-permute-done.13.refs_1_ = bf16[32,4096]{1,0:T(8,128)(2,1)S(1)} collective-permute-done((bf16[32,4096]{1,0:T(8,128)(2,1)S(1)}, bf16[32,4096]{1,0:T(8,128)(2,1)S(1)}, u32[]{:S(2)}, u32[]{:S(2)}) %collective-permute-start.13) | collective-permute-done | bytes 262176 | tf_op jit(solution)/shard_map/ppermute | solution.py:527
  78.2 1.9 %encode_rows.5 = (bf16[32,2,16,128]{3,2,1,0:T(8,128)(2,1)S(1)}, bf16[32,2,16,128]{3,2,1,0:T(8,128)(2,1)S(1)}) custom-call(bf16[32,4096]{1,0:T(8,128)(2,1)S(1)} %collective-permute-done.8.refs_0_, bf16[32,4096]{1,0:T(8,128)(2,1)S(1)} %collective-permute-done.13.refs_1_, bf16[32,8192]{1,0:T(8,128)(2,1)S(1)} %get-tuple-element.70.refs_2_, ...), custom_call_target="tpu_custom_call" | custom-call | flops 1610612736 | bytes 3670016 | tf_op jit(solution)/shard_map/encode_rows/pallas_call | solution.py:446
  80.1 1.4 %collective-permute-start.16 = (bf16[32,2,16,128]{3,2,1,0:T(8,128)(2,1)S(1)}, bf16[32,2,16,128]{3,2,1,0:T(8,128)(2,1)S(1)}, u32[]{:S(2)}, u32[]{:S(2)}) collective-permute-start(bf16[32,2,16,128]{3,2,1,0:T(8,128)(2,1)S(1)} %get-tuple-element.80), channel_id=1, source_target_pairs={{0,1},{1,0},{2,3},{3,2},{4,5},{5,4},{6,7},{7,6},{8,9},{9,8},{10,11... | collective-permute-start | bytes 786440 | tf_op jit(solution)/shard_map/ppermute | solution.py:527
  81.5 1.9 %encode_rows.6 = (bf16[32,2,16,128]{3,2,1,0:T(8,128)(2,1)S(1)}, bf16[32,2,16,128]{3,2,1,0:T(8,128)(2,1)S(1)}) custom-call(bf16[32,4096]{1,0:T(8,128)(2,1)S(1)} %collective-permute-done.9.refs_0_, bf16[32,4096]{1,0:T(8,128)(2,1)S(1)} %collective-permute-done.11.refs_1_, bf16[32,8192]{1,0:T(8,128)(2,1)S(1)} %get-tuple-element.74.refs_2_, ...), custom_call_target="tpu_custom_call" | custom-call | flops 1610612736 | bytes 3670016 | tf_op jit(solution)/shard_map/encode_rows/pallas_call | solution.py:446
  83.8 1.9 %encode_rows.7 = (bf16[32,2,16,128]{3,2,1,0:T(8,128)(2,1)S(1)}, bf16[32,2,16,128]{3,2,1,0:T(8,128)(2,1)S(1)}) custom-call(bf16[32,4096]{1,0:T(8,128)(2,1)S(1)} %collective-permute-done.10.refs_0_, bf16[32,4096]{1,0:T(8,128)(2,1)S(1)} %collective-permute-done.14.refs_1_, bf16[32,8192]{1,0:T(8,128)(2,1)S(1)} %get-tuple-element.77.refs_2_, ...), custom_call_target="tpu_custom_call" | custom-call | flops 1610612736 | bytes 3670016 | tf_op jit(solution)/shard_map/encode_rows/pallas_call | solution.py:446
  87.8 2.1 %place_rows.1 = bf16[2,8,8,2,2,16,128]{6,5,4,3,2,1,0:T(8,128)(2,1)} custom-call(s32[128]{0:T(128)S(1)} %copy-done.2, bf16[2,8,2,2,16,128]{5,4,3,2,1,0:T(8,128)(2,1)S(1)} %bitcast.27, bf16[2,8,2,2,16,128]{5,4,3,2,1,0:T(8,128)(2,1)S(1)} %bitcast.29, bf16[2,8,2,2,16,128]{5,4,3,2,1,0:T(8,128)(2,1)S(1)} %bitcast.31, bf16[2,8,2,2,16,128]{5,4,3,2,1,0:T(8,128)(2,1)S(1)} %bitcast.33, ...), custom_call_target="tpu_custom_call" | custom-call | bytes 4194304 | tf_op jit(solution)/shard_map/place_rows/pallas_call | solution.py:485
  (60 shorter events, 12.8 us)
Async XLA Ops:
  0.0 3.3 %copy-start.5 = (s32[1,128]{1,0:T(1,128)S(1)}, s32[1,128]{1,0:T(1,128)}, u32[]{:S(2)}) copy-start(s32[1,128]{1,0:T(1,128)} %flag_ref.1) | copy-start | bytes 1540
  0.0 3.2 %collective-permute-start = (bf16[2048,256]{1,0:T(8,128)(2,1)}, bf16[2048,256]{1,0:T(8,128)(2,1)S(1)}, u32[]{:S(2)}, u32[]{:S(2)}) collective-permute-start(bf16[2048,256]{1,0:T(8,128)(2,1)} %bitcast.24), channel_id=1, source_target_pairs={{0,1},{1,0},{2,3},{3,2},{4,5},{5,4},{6,7},{7,6},{8,9},{9,8},{10,11... | collective-permute-start | bytes 3145736 | tf_op jit(solution)/shard_map/ppermute | solution.py:527
  2.5 10.3 %collective-permute-start.2 = (bf16[2320,128]{1,0:T(8,128)(2,1)S(1)}, bf16[2320,128]{1,0:T(8,128)(2,1)S(1)}, u32[]{:S(2)}, u32[]{:S(2)}) collective-permute-start(bf16[2320,128]{1,0:T(8,128)(2,1)S(1)} %pad_maximum_fusion.own), channel_id=1, source_target_pairs={{0,1},{1,0},{2,3},{3,2},{4,5},{5,4},{6,7},{7,6},{8,9},{9,8},{10,11... | collective-permute-start | bytes 1781768 | tf_op jit(solution)/shard_map/ppermute | solution.py:527
  4.7 18.9 %collective-permute-start.1 = (bf16[64,4096]{1,0:T(8,128)(2,1)S(1)}, bf16[64,4096]{1,0:T(8,128)(2,1)}, u32[]{:S(2)}, u32[]{:S(2)}) collective-permute-start(bf16[64,4096]{1,0:T(8,128)(2,1)S(1)} %get-tuple-element.45), channel_id=1, source_target_pairs={{0,4},{4,0},{8,12},{12,8},{16,20},{20,16},{24,28},{28,24},{1,5},{5... | collective-permute-start | bytes 1572872 | tf_op jit(solution)/shard_map/ppermute | solution.py:549
  7.1 29.9 %all-to-all-start = ((bf16[8,32,2048]{2,1,0:T(8,128)(2,1)}), bf16[8,32,2048]{2,1,0:T(8,128)(2,1)S(1)}, u32[]{:S(2)}, u32[]{:S(2)}) async-start(bf16[8,32,2048]{2,1,0:T(8,128)(2,1)} %bitcast.6), calls=%async_computation | async-start | bytes 2097152 | tf_op jit(solution)/shard_map/all_to_all | solution.py:538
  13.8 13.3 %collective-permute-start.3 = (bf16[1568,128]{1,0:T(8,128)(2,1)S(1)}, bf16[1568,128]{1,0:T(8,128)(2,1)S(1)}, u32[]{:S(2)}, u32[]{:S(2)}) collective-permute-start(bf16[1568,128]{1,0:T(8,128)(2,1)S(1)} %pad_maximum_fusion.1), channel_id=1, source_target_pairs={{0,2},{1,3},{2,0},{3,1},{4,6},{5,7},{6,4},{7,5},{8,10},{9,11},{10,... | collective-permute-start | bytes 1204232 | tf_op jit(solution)/shard_map/ppermute | solution.py:527
  25.5 12.8 %copy-start.11 = (bf16[16,4096]{1,0:T(8,128)(2,1)S(1)}, bf16[16,4096]{1,0:T(8,128)(2,1)}, u32[]{:S(2)}) copy-start(bf16[16,4096]{1,0:T(8,128)(2,1)} %get-tuple-element.85) | copy-start | bytes 393220
  25.5 5.9 %collective-permute-start.4 = (bf16[32,4096]{1,0:T(8,128)(2,1)S(1)}, bf16[32,4096]{1,0:T(8,128)(2,1)S(1)}, u32[]{:S(2)}, u32[]{:S(2)}) collective-permute-start(bf16[32,4096]{1,0:T(8,128)(2,1)S(1)} %pad_maximum_fusion.2.refs_0_), channel_id=1, source_target_pairs={{0,2},{1,3},{2,0},{3,1},{4,6},{5,7},{6,4},{7,5},{8,10},{9,11},{10,... | collective-permute-start | bytes 786440 | tf_op jit(solution)/shard_map/ppermute | solution.py:527
  26.8 4.5 %copy-start.12 = (bf16[32,4096]{1,0:T(8,128)(2,1)}, bf16[32,4096]{1,0:T(8,128)(2,1)S(1)}, u32[]{:S(2)}) copy-start(bf16[32,4096]{1,0:T(8,128)(2,1)S(1)} %pad_maximum_fusion.4) | copy-start | bytes 786436
  26.8 45.8 %copy-start.4 = (s32[128]{0:T(128)S(1)}, s32[128]{0:T(128)}, u32[]{:S(2)}) copy-start(s32[128]{0:T(128)} %param.14) | copy-start | bytes 1540
  26.8 10.2 %collective-permute-start.5 = (bf16[32,4096]{1,0:T(8,128)(2,1)S(1)}, bf16[32,4096]{1,0:T(8,128)(2,1)}, u32[]{:S(2)}, u32[]{:S(2)}) collective-permute-start(bf16[32,4096]{1,0:T(8,128)(2,1)S(1)} %pad_maximum_fusion.4), channel_id=1, source_target_pairs={{0,2},{1,3},{2,0},{3,1},{4,6},{5,7},{6,4},{7,5},{8,10},{9,11},{10,... | collective-permute-start | bytes 786440 | tf_op jit(solution)/shard_map/ppermute | solution.py:527
  37.0 32.6 %collective-permute-start.6 = (bf16[256,2048]{1,0:T(8,128)(2,1)S(1)}, bf16[256,2048]{1,0:T(8,128)(2,1)S(1)}, u32[]{:S(2)}, u32[]{:S(2)}) collective-permute-start(bf16[256,2048]{1,0:T(8,128)(2,1)S(1)} %bitcast.21), channel_id=1, source_target_pairs={{0,2},{1,3},{2,0},{3,1},{4,6},{5,7},{6,4},{7,5},{8,10},{9,11},{10,... | collective-permute-start | bytes 3145736 | tf_op jit(solution)/shard_map/ppermute | solution.py:527
  38.3 13.8 %collective-permute-start.8 = (bf16[32,4096]{1,0:T(8,128)(2,1)S(1)}, bf16[32,4096]{1,0:T(8,128)(2,1)S(1)}, u32[]{:S(2)}, u32[]{:S(2)}) collective-permute-start(bf16[32,4096]{1,0:T(8,128)(2,1)S(1)} %pad_maximum_fusion.5), channel_id=1, source_target_pairs={{0,16},{4,20},{8,24},{12,28},{16,0},{20,4},{24,8},{28,12},{1,17},{... | collective-permute-start | bytes 786440 | tf_op jit(solution)/shard_map/ppermute | solution.py:531
  40.7 20.0 %collective-permute-start.9 = (bf16[32,4096]{1,0:T(8,128)(2,1)}, bf16[32,4096]{1,0:T(8,128)(2,1)S(1)}, u32[]{:S(2)}, u32[]{:S(2)}) collective-permute-start(bf16[32,4096]{1,0:T(8,128)(2,1)} %copy-done.12), channel_id=1, source_target_pairs={{0,8},{4,12},{8,16},{12,20},{16,24},{20,28},{24,0},{28,4},{1,9},{5... | collective-permute-start | bytes 786440 | tf_op jit(solution)/shard_map/ppermute | solution.py:531
  40.7 28.9 %collective-permute-start.10 = (bf16[32,4096]{1,0:T(8,128)(2,1)S(1)}, bf16[32,4096]{1,0:T(8,128)(2,1)S(1)}, u32[]{:S(2)}, u32[]{:S(2)}) collective-permute-start(bf16[32,4096]{1,0:T(8,128)(2,1)S(1)} %pad_maximum_fusion.3), channel_id=1, source_target_pairs={{0,24},{4,28},{8,0},{12,4},{16,8},{20,12},{24,16},{28,20},{1,25},{... | collective-permute-start | bytes 786440 | tf_op jit(solution)/shard_map/ppermute | solution.py:531
  42.1 27.5 %collective-permute-start.11 = (bf16[32,4096]{1,0:T(8,128)(2,1)}, bf16[32,4096]{1,0:T(8,128)(2,1)S(1)}, u32[]{:S(2)}, u32[]{:S(2)}) collective-permute-start(bf16[32,4096]{1,0:T(8,128)(2,1)} %collective-permute-done.5), channel_id=1, source_target_pairs={{0,8},{4,12},{8,16},{12,20},{16,24},{20,28},{24,0},{28,4},{1,9},{5... | collective-permute-start | bytes 786440 | tf_op jit(solution)/shard_map/ppermute | solution.py:531
  52.2 19.6 %collective-permute-start.7 = (bf16[256,2048]{1,0:T(8,128)(2,1)S(1)}, bf16[256,2048]{1,0:T(8,128)(2,1)S(1)}, u32[]{:S(2)}, u32[]{:S(2)}) collective-permute-start(bf16[256,2048]{1,0:T(8,128)(2,1)S(1)} %bitcast.22), channel_id=1, source_target_pairs={{0,1},{1,0},{2,3},{3,2},{4,5},{5,4},{6,7},{7,6},{8,9},{9,8},{10,11... | collective-permute-start | bytes 3145736 | tf_op jit(solution)/shard_map/ppermute | solution.py:527
  69.6 3.0 %collective-permute-start.12 = (bf16[256,2048]{1,0:T(8,128)(2,1)S(1)}, bf16[256,2048]{1,0:T(8,128)(2,1)S(1)}, u32[]{:S(2)}, u32[]{:S(2)}) collective-permute-start(bf16[256,2048]{1,0:T(8,128)(2,1)S(1)} %collective-permute-done.6.refs_1_), channel_id=1, source_target_pairs={{0,1},{1,0},{2,3},{3,2},{4,5},{5,4},{6,7},{7,6},{8,9},{9,8},{10,11... | collective-permute-start | bytes 3145736 | tf_op jit(solution)/shard_map/ppermute | solution.py:527
  70.3 7.9 %collective-permute-start.13 = (bf16[32,4096]{1,0:T(8,128)(2,1)S(1)}, bf16[32,4096]{1,0:T(8,128)(2,1)S(1)}, u32[]{:S(2)}, u32[]{:S(2)}) collective-permute-start(bf16[32,4096]{1,0:T(8,128)(2,1)S(1)} %collective-permute-done.8.refs_0_), channel_id=1, source_target_pairs={{0,2},{1,3},{2,0},{3,1},{4,6},{5,7},{6,4},{7,5},{8,10},{9,11},{10,... | collective-permute-start | bytes 786440 | tf_op jit(solution)/shard_map/ppermute | solution.py:527
  70.5 13.3 %collective-permute-start.14 = (bf16[32,4096]{1,0:T(8,128)(2,1)S(1)}, bf16[32,4096]{1,0:T(8,128)(2,1)S(1)}, u32[]{:S(2)}, u32[]{:S(2)}) collective-permute-start(bf16[32,4096]{1,0:T(8,128)(2,1)S(1)} %collective-permute-done.10.refs_0_), channel_id=1, source_target_pairs={{0,2},{1,3},{2,0},{3,1},{4,6},{5,7},{6,4},{7,5},{8,10},{9,11},{10,... | collective-permute-start | bytes 786440 | tf_op jit(solution)/shard_map/ppermute | solution.py:527
  76.4 10.3 %collective-permute-start.15 = (bf16[32,2,16,128]{3,2,1,0:T(8,128)(2,1)S(1)}, bf16[32,2,16,128]{3,2,1,0:T(8,128)(2,1)S(1)}, u32[]{:S(2)}, u32[]{:S(2)}) collective-permute-start(bf16[32,2,16,128]{3,2,1,0:T(8,128)(2,1)S(1)} %get-tuple-element.79), channel_id=1, source_target_pairs={{0,1},{1,0},{2,3},{3,2},{4,5},{5,4},{6,7},{7,6},{8,9},{9,8},{10,11... | collective-permute-start | bytes 786440 | tf_op jit(solution)/shard_map/ppermute | solution.py:527
  80.1 6.5 %collective-permute-start.16 = (bf16[32,2,16,128]{3,2,1,0:T(8,128)(2,1)S(1)}, bf16[32,2,16,128]{3,2,1,0:T(8,128)(2,1)S(1)}, u32[]{:S(2)}, u32[]{:S(2)}) collective-permute-start(bf16[32,2,16,128]{3,2,1,0:T(8,128)(2,1)S(1)} %get-tuple-element.80), channel_id=1, source_target_pairs={{0,1},{1,0},{2,3},{3,2},{4,5},{5,4},{6,7},{7,6},{8,9},{9,8},{10,11... | collective-permute-start | bytes 786440 | tf_op jit(solution)/shard_map/ppermute | solution.py:527
  83.5 3.2 %collective-permute-start.17 = (bf16[32,2,16,128]{3,2,1,0:T(8,128)(2,1)S(1)}, bf16[32,2,16,128]{3,2,1,0:T(8,128)(2,1)S(1)}, u32[]{:S(2)}, u32[]{:S(2)}) collective-permute-start(bf16[32,2,16,128]{3,2,1,0:T(8,128)(2,1)S(1)} %get-tuple-element.81), channel_id=1, source_target_pairs={{0,1},{1,0},{2,3},{3,2},{4,5},{5,4},{6,7},{7,6},{8,9},{9,8},{10,11... | collective-permute-start | bytes 786440 | tf_op jit(solution)/shard_map/ppermute | solution.py:527
  85.7 2.1 %collective-permute-start.18 = (bf16[32,2,16,128]{3,2,1,0:T(8,128)(2,1)S(1)}, bf16[32,2,16,128]{3,2,1,0:T(8,128)(2,1)S(1)}, u32[]{:S(2)}, u32[]{:S(2)}) collective-permute-start(bf16[32,2,16,128]{3,2,1,0:T(8,128)(2,1)S(1)} %get-tuple-element.82), channel_id=1, source_target_pairs={{0,1},{1,0},{2,3},{3,2},{4,5},{5,4},{6,7},{7,6},{8,9},{9,8},{10,11... | collective-permute-start | bytes 786440 | tf_op jit(solution)/shard_map/ppermute | solution.py:527
  (9 other events, 19.5 us)
